TPU v7x, 32 devices: a whole 2x2x4 slice. The times are simulated.
32 devices in a mesh: rows: 2 (over x), res: 16 (over z, y, core).
Axes of the slice: x: 2, y: 2, z: 4, core: 2. Of those that a mesh axis runs over, the one named last changes fastest.
Arguments:
- source_alignment_rows: bfloat16 [128, 256, 256], P('rows', 'res'), may hold values from -120 to 120
- pairs: int32 [6, 128], P(None, 'rows'), may hold values from -1 to 127, as said below
- chain_first_residue: int32 [6], replicated, may hold values from 0 to 235, as said below
- gap_embedding: bfloat16 [256], replicated, may hold values from -4 to 4
- layer_norm_gain: bfloat16 [256], replicated, may hold values from 0.099609375 to 1.8984375
- layer_norm_bias: bfloat16 [256], replicated, may hold values from -3 to 3
- projection_weight: bfloat16 [256, 8, 128], replicated, may hold values from -0.375 to 0.375
- gate_bias_heads: bfloat16 [256], replicated, may hold values from -4 to 4
- pair_bias_logits: bfloat16 [8, 256, 256], P(None, 'res'), may hold values from -6 to 320
- output_weight: bfloat16 [256, 256], replicated, may hold values from -0.375 to 0.375
- output_bias: bfloat16 [256], replicated, may hold values from -3 to 3
Outputs:
- update: bfloat16 [128, 256, 256], P('rows', 'res')
Inputs may be any that keep to these rules, and one draw needn't show every extreme that they name: `pairs`: within one chain each source row is named at most once; chain 0 has no gaps. For each chain and each aligned block of 64 joint rows, at most 32 entries name rows of one aligned block of 64 source rows, and exactly 32 in some block. chain_first_residue[0] is 0, the starts rise, chain k holds residues from its start up to the next start (the last up to 256), and each chain has at least 21 residues; the last chain has exactly that many.
All inputs are finite; a program needn't handle non-finite values.
Results may differ from a plain program's by a relative error of at most 0.012.
Values may be sent and summed in bfloat16 or wider, within the bound.
No kernel may reach another device: no remote copies, remote signals or barrier semaphores. Data moves between devices by JAX's collectives and lax.ppermute only.
A program may use at most 64 MiB of HBM per device.

v0:
```python
import jax
import jax.numpy as jnp
from jax import lax
from jax.sharding import PartitionSpec as P

norm_eps = 1e-05


def layer_norm(values, gain, shift):
    widened = values.astype(jnp.float32)
    center = jnp.mean(widened, axis=-1, keepdims=True)
    spread = jnp.mean(jnp.square(widened - center), axis=-1, keepdims=True)
    scaled = (widened - center) * lax.rsqrt(spread + norm_eps)
    return (scaled * gain.astype(jnp.float32) + shift.astype(jnp.float32)).astype(jnp.bfloat16)


def slot_table(row_lists, owner_ids, block_rows, capacity):
    owner_of = jnp.floor_divide(row_lists, block_rows)
    within = row_lists - owner_of * block_rows
    matches = (row_lists[..., None] >= 0) & (owner_of[..., None] == owner_ids)
    rank_of = jnp.cumsum(matches.astype(jnp.int32), axis=2) - 1
    slot_hit = matches[..., None] & (rank_of[..., None] == jnp.arange(capacity, dtype=jnp.int32))
    slot_list = jnp.sum(slot_hit.astype(jnp.int32) * (within + 1)[..., None, None], axis=2) - 1
    return (slot_list, owner_of, jnp.sum(jnp.where(matches, rank_of, 0), axis=-1))


def attend_core(queries, key_rows, value_rows, gate_rows, bias_rows):
    scores = jnp.einsum("...qd,...kd->...qk", queries, key_rows, preferred_element_type=jnp.float32)
    scores = scores + bias_rows.astype(jnp.float32)
    highest = jnp.max(scores, axis=-1, keepdims=True)
    lifted = jnp.exp(scores - highest)
    weights = (lifted / jnp.sum(lifted, axis=-1, keepdims=True)).astype(jnp.bfloat16)
    summed = jnp.einsum(
        "...qk,...kd->...qd", weights, value_rows, preferred_element_type=jnp.float32
    )
    return (summed * gate_rows.astype(jnp.float32)).astype(jnp.bfloat16)


def local(
    source_alignment_rows,
    pairs,
    chain_first_residue,
    gap_embedding,
    layer_norm_gain,
    layer_norm_bias,
    projection_weight,
    gate_bias_heads,
    pair_bias_logits,
    output_weight,
    output_bias,
):
    local_rows, local_columns, channel_count = source_alignment_rows.shape
    chains = pairs.shape[0]
    owners = lax.axis_size("rows")
    capacity = local_rows // owners
    column_indices = lax.axis_index("res") * local_columns + jnp.arange(
        local_columns, dtype=jnp.int32
    )
    chain_index = jnp.sum(
        (column_indices[:, None] >= chain_first_residue[None, 1:]).astype(jnp.int32), axis=1
    )
    chain_hot = (chain_index[:, None] == jnp.arange(chains, dtype=jnp.int32)[None, :]).astype(
        jnp.int32
    )
    owner_ids = jnp.arange(owners, dtype=jnp.int32)
    requested, owner_of, rank_of = slot_table(pairs[:, None, :], owner_ids, local_rows, capacity)
    wanted = lax.all_to_all(
        jnp.transpose(requested[:, 0], (1, 0, 2)), "rows", split_axis=0, concat_axis=0, tiled=True
    )
    take_rows = jnp.transpose(
        jnp.sum(wanted[:, None, :, :] * chain_hot[None, :, :, None], axis=2), (0, 2, 1)
    )
    col_grid = jnp.arange(local_columns, dtype=jnp.int32)
    flattened_source = source_alignment_rows.reshape(local_rows * local_columns, channel_count)
    outgoing = flattened_source[jnp.maximum(take_rows, 0) * local_columns + col_grid]
    arrived = lax.all_to_all(outgoing, "rows", split_axis=0, concat_axis=0, tiled=True)
    hot_cols = chain_hot.T[:, None, :]
    source_owner = jnp.sum(owner_of[:, 0, :, None] * hot_cols, axis=0)
    source_rank = jnp.sum(rank_of[:, 0, :, None] * hot_cols, axis=0)
    source_list = jnp.sum(pairs[:, :, None] * hot_cols, axis=0)
    arrived_flat = arrived.reshape(owners * capacity * local_columns, channel_count)
    where_from = (jnp.maximum(source_owner, 0) * capacity + source_rank) * local_columns + col_grid[
        None, :
    ]
    joint_rows = jnp.where(
        (source_list >= 0)[..., None], arrived_flat[where_from], gap_embedding[None, None, :]
    )
    normed = layer_norm(joint_rows, layer_norm_gain, layer_norm_bias)
    head_total = projection_weight.shape[1]
    head_dim = projection_weight.shape[2] // 4
    query_scale = head_dim ** (-0.5)
    gate_shift = gate_bias_heads.astype(jnp.float32).reshape(head_total, head_dim)
    out_weight = output_weight.reshape(head_total, head_dim, channel_count)
    full_rows = lax.all_to_all(normed, "res", split_axis=0, concat_axis=1, tiled=True)
    projected = jnp.einsum(
        "rcm,mhe->rhce", full_rows, projection_weight, preferred_element_type=jnp.float32
    )
    queries = (projected[..., :head_dim] * query_scale).astype(jnp.bfloat16)
    key_rows = projected[..., head_dim : 2 * head_dim].astype(jnp.bfloat16)
    value_rows = projected[..., 2 * head_dim : 3 * head_dim].astype(jnp.bfloat16)
    gate_rows = jax.nn.sigmoid(
        projected[..., 3 * head_dim :] + gate_shift[None, :, None, :]
    ).astype(jnp.bfloat16)
    attended = attend_core(
        queries,
        key_rows,
        value_rows,
        gate_rows,
        lax.all_gather(pair_bias_logits, "res", axis=1, tiled=True)[None],
    )
    update = jnp.einsum("rhqd,hdm->rqm", attended, out_weight, preferred_element_type=jnp.float32)
    update = (update + output_bias.astype(jnp.float32)).astype(jnp.bfloat16)
    result = lax.all_to_all(update, "res", split_axis=1, concat_axis=0, tiled=True)
    return result


def solution(mesh):
    return jax.shard_map(
        local,
        mesh=mesh,
        in_specs=(
            P("rows", "res", None),
            P(None, "rows"),
            P(),
            P(),
            P(),
            P(),
            P(),
            P(),
            P(None, "res", None),
            P(),
            P(),
        ),
        out_specs=P("rows", "res", None),
        check_vma=False,
    )
```

profile of v0, /device:TPU:0, one launch (start us, length us, event | category | flops | bytes accessed | tf_op | source)
XLA Modules:
  0.0 107.4 jit_solution(10141146545495716724)
XLA Ops:
  6.5 0.0 copy-start
  6.5 0.8 add_select_fusion
  7.3 0.7 broadcast_compare_fusion.1
  8.0 0.2 fusion.38
  8.2 0.2 reduce_window_sum.11
  8.4 0.3 select_reduce_fusion
  8.7 0.1 copy.28
  8.8 0.3 select_reduce_fusion.1
  9.1 0.7 reshape.252
  9.8 4.2 %all-to-all-start = ((s32[2,1,192]{2,1,0:T(1,128)}), s32[2,1,192]{2,1,0:T(1,128)S(1)}, u32[]{:S(2)}, u32[]{:S(2)}) async-start(s32[2,1,192]{2,1,0:T(1,128)} %reshape.252), calls=%async_computation | async-start | bytes 4096 | tf_op jit(solution)/shard_map/all_to_all | solution.py:67
  14.0 0.7 all-gather.2.cloned.1.call-update
  14.7 0.7 slice.17
  15.5 0.1 convert_reduce_fusion.1
  15.6 0.8 multiply_reduce_fusion.3
  16.4 1.4 %all-to-all-done = s32[2,1,192]{2,1,0:T(1,128)S(1)} async-done(((s32[2,1,192]{2,1,0:T(1,128)}), s32[2,1,192]{2,1,0:T(1,128)S(1)}, u32[]{:S(2)}, u32[]{:S(2)}) %all-to-all-start) | async-done | bytes 1568 | tf_op jit(solution)/shard_map/all_to_all | solution.py:67
  17.8 0.5 broadcast.299
  18.3 0.7 reduce.2
  19.0 0.1 reshape.253
  19.0 0.1 multiply_reduce_fusion
  19.1 0.1 copy.30
  19.2 0.1 reshape.231
  19.3 0.0 copy-start.2
  19.3 5.0 %gather_fusion = bf16[1024,256]{1,0:T(8,128)(2,1)} fusion(bf16[1024,256]{1,0:T(8,128)(2,1)S(1)} %bitcast.50, s32[1024]{0:T(1024)S(1)} %broadcast_clamp_fusion.1), kind=kCustom, calls=%fused_computation | custom fusion | bytes 1052672 | tf_op jit(solution)/shard_map/gather | solution.py:75
  24.3 3.5 %all-to-all-start.1 = ((bf16[2,32,16,256]{3,2,1,0:T(8,128)(2,1)}), bf16[2,32,16,256]{3,2,1,0:T(8,128)(2,1)S(1)}, u32[]{:S(2)}, u32[]{:S(2)}) async-start(bf16[2,32,16,256]{3,2,1,0:T(8,128)(2,1)} %bitcast.4), calls=%async_computation.1 | async-start | bytes 1048576 | tf_op jit(solution)/shard_map/all_to_all | solution.py:76
  27.8 0.0 copy-start.1
  27.8 0.1 copy.31
  27.9 0.1 reshape.239
  28.0 0.1 copy.27
  28.2 6.9 %all-to-all-done.1 = bf16[2,32,16,256]{3,2,1,0:T(8,128)(2,1)S(1)} async-done(((bf16[2,32,16,256]{3,2,1,0:T(8,128)(2,1)}), bf16[2,32,16,256]{3,2,1,0:T(8,128)(2,1)S(1)}, u32[]{:S(2)}, u32[]{:S(2)}) %all-to-all-start.1) | async-done | bytes 524320 | tf_op jit(solution)/shard_map/all_to_all | solution.py:76
  35.1 3.9 %gather_fusion.1 = bf16[1024,256]{1,0:T(8,128)(2,1)S(1)} fusion(bf16[1024,256]{1,0:T(8,128)(2,1)S(1)} %bitcast.51, s32[1024]{0:T(1024)S(1)} %broadcast_clamp_fusion), kind=kCustom, calls=%fused_computation.1 | custom fusion | bytes 1052672 | tf_op jit(solution)/shard_map/gather | solution.py:86
  39.1 0.4 convert_reduce_fusion
  39.4 0.5 fusion.12
  40.0 1.3 %fusion.15 = bf16[64,16,256]{2,1,0:T(8,128)(2,1)} fusion(f32[256]{0:T(256)S(1)} %convert_element_type.75, f32[256]{0:T(256)S(1)} %convert_element_type.74, f32[64,16]{1,0:T(8,128)S(1)} %add_rsqrt_fusion, f32[64,16]{1,0:T(8,128)S(1)} %broadcast_multiply_fusion, pred[64,16]{1,0:T(8,128)(4,1)S(1)} %copy.27, bf16[256]{0:T(256)(128)(2,1)S(1)} %copy-done.2, ...), kind=kLoop, calls=%fused_computation.22 | loop fusion | flops 1835008 | bytes 1060352 | tf_op jit(solution)/shard_map/convert_element_type | solution.py:14
  41.2 6.2 %all-to-all-start.2 = ((bf16[64,16,256]{2,1,0:T(8,128)(2,1)}), bf16[64,16,256]{2,1,0:T(8,128)(2,1)S(1)}, u32[]{:S(2)}, u32[]{:S(2)}) async-start(bf16[64,16,256]{2,1,0:T(8,128)(2,1)} %fusion.15), calls=%async_computation.2 | async-start | bytes 1048576 | tf_op jit(solution)/shard_map/all_to_all | solution.py:94
  47.4 0.0 copy-done.1
  47.4 0.3 copy.33
  47.8 0.0 copy-done.3
  47.8 0.1 reshape.228
  47.9 15.0 %all-to-all-done.2 = bf16[64,16,256]{2,1,0:T(8,128)(2,1)S(1)} async-done(((bf16[64,16,256]{2,1,0:T(8,128)(2,1)}), bf16[64,16,256]{2,1,0:T(8,128)(2,1)S(1)}, u32[]{:S(2)}, u32[]{:S(2)}) %all-to-all-start.2) | async-done | bytes 524320 | tf_op jit(solution)/shard_map/all_to_all | solution.py:94
  62.9 3.5 %fusion.53 = (bf16[4,8,256,128]{2,3,1,0:T(8,128)(2,1)}, f32[4,8,256,128]{2,3,1,0:T(8,128)}) fusion(bf16[4,256,256,1]{2,1,3,0:T(8,128)(2,1)S(1)} %bitcast.54, bf16[256,8,128]{0,2,1:T(8,128)(2,1)S(1)} %copy.33), kind=kOutput, calls=%fused_computation.81 | convolution fusion | flops 537919488 | bytes 7340032 | tf_op jit(solution)/shard_map/rcm,mhe->rhce/dot_general | solution.py:95
  66.4 1.5 %copy.34 = f32[8,256,256]{1,2,0:T(8,128)S(1)} copy(bf16[8,256,256]{2,1,0:T(8,128)(2,1)} %all-gather.2.cloned.1.call-done) | data formatting | bytes 3145728 | tf_op jit(solution)/shard_map/convert_element_type | solution.py:29
  67.9 0.0 copy-start.4
  67.9 7.3 %fusion.54 = (f32[4,8,256]{2,1,0:T(8,128)S(1)}, f32[4,8,256,256]{2,3,1,0:T(8,128)}) fusion(f32[8,256,256]{1,2,0:T(8,128)S(1)} %copy.34, bf16[4,8,256,128]{2,3,1,0:T(8,128)(2,1)} %get-tuple-element.12, f32[4,8,256,128]{2,3,1,0:T(8,128)} %get-tuple-element.13), kind=kOutput, calls=%fused_computation.82 | convolution fusion | flops 141033728 | bytes 12091392 | tf_op jit(solution)/shard_map/sub | solution.py:31
  75.2 0.0 copy-done.4
  75.2 5.0 %fusion.9 = bf16[4,256,256]{2,1,0:T(8,128)(2,1)S(1)} fusion(bf16[8,32,256,1]{2,1,0,3:T(8,128)(2,1)S(1)} %bitcast.57, f32[4,8,256,256]{2,3,1,0:T(8,128)} %get-tuple-element.15, f32[4,8,256]{2,1,0:T(8,128)S(1)} %get-tuple-element.14, f32[4,8,256,128]{2,3,1,0:T(8,128)} %get-tuple-element.13, bf16[4,8,256,128]{2,3,1,0:T(8,128)(2,1)} %get-tuple-element.12, ...), kind=kOutput, calls=%fused_computation.16 | convolution fusion | flops 275251200 | bytes 10651648 | tf_op jit(solution)/shard_map/rhqd,hdm->rqm/dot_general | solution.py:111
  80.2 0.4 copy.36
  80.6 19.1 %all_to_all.46 = bf16[4,256,256]{2,0,1:T(4,128)(2,1)S(1)} all-to-all(bf16[4,256,256]{2,0,1:T(4,128)(2,1)S(1)} %copy.36), channel_id=1, replica_groups=mesh['rows'=2,'res'=16] {'res'}, dimensions={1} | all-to-all | bytes 1048576 | tf_op jit(solution)/shard_map/all_to_all | solution.py:113
  99.7 0.9 copy.37
  (28 shorter events, 0.2 us)
Async XLA Ops:
  6.5 12.8 %copy-start = (bf16[64,16,256]{2,1,0:T(8,128)(2,1)S(1)}, bf16[64,16,256]{2,1,0:T(8,128)(2,1)}, u32[]{:S(2)}) copy-start(bf16[64,16,256]{2,1,0:T(8,128)(2,1)} %param.11) | copy-start | bytes 1572868
  6.5 21.6 %copy-start.5 = (bf16[256]{0:T(256)(128)(2,1)S(1)}, bf16[256]{0:T(256)(128)(2,1)}, u32[]{:S(2)}) copy-start(bf16[256]{0:T(256)(128)(2,1)} %param.15) | copy-start | bytes 1540
  6.5 21.6 %copy-start.6 = (bf16[256]{0:T(256)(128)(2,1)S(1)}, bf16[256]{0:T(256)(128)(2,1)}, u32[]{:S(2)}) copy-start(bf16[256]{0:T(256)(128)(2,1)} %param.16) | copy-start | bytes 1540
  9.8 8.0 %all-to-all-start = ((s32[2,1,192]{2,1,0:T(1,128)}), s32[2,1,192]{2,1,0:T(1,128)S(1)}, u32[]{:S(2)}, u32[]{:S(2)}) async-start(s32[2,1,192]{2,1,0:T(1,128)} %reshape.252), calls=%async_computation | async-start | bytes 4096 | tf_op jit(solution)/shard_map/all_to_all | solution.py:67
  14.0 52.4 %all-gather.2.cloned.1.call-start = ((), (), s32[]{:S(2)}) async-start(), calls=%async_computation.4 | async-start | bytes 1114112 | tf_op jit(solution)/shard_map/all_gather | solution.py:109
  19.3 19.7 %copy-start.2 = (bf16[256]{0:T(256)(128)(2,1)S(1)}, bf16[256]{0:T(256)(128)(2,1)}, u32[]{:S(2)}) copy-start(bf16[256]{0:T(256)(128)(2,1)} %param.14) | copy-start | bytes 1540
  24.3 10.8 %all-to-all-start.1 = ((bf16[2,32,16,256]{3,2,1,0:T(8,128)(2,1)}), bf16[2,32,16,256]{3,2,1,0:T(8,128)(2,1)S(1)}, u32[]{:S(2)}, u32[]{:S(2)}) async-start(bf16[2,32,16,256]{3,2,1,0:T(8,128)(2,1)} %bitcast.4), calls=%async_computation.1 | async-start | bytes 1048576 | tf_op jit(solution)/shard_map/all_to_all | solution.py:76
  27.8 19.6 %copy-start.1 = (bf16[256,8,128]{2,1,0:T(8,128)(2,1)S(1)}, bf16[256,8,128]{2,1,0:T(8,128)(2,1)}, u32[]{:S(2)}) copy-start(bf16[256,8,128]{2,1,0:T(8,128)(2,1)} %param.17) | copy-start | bytes 1572868
  35.1 12.7 %copy-start.3 = (bf16[256]{0:T(256)(128)(2,1)S(1)}, bf16[256]{0:T(256)(128)(2,1)}, u32[]{:S(2)}) copy-start(bf16[256]{0:T(256)(128)(2,1)} %param.18) | copy-start | bytes 1540
  35.1 12.8 %copy-start.7 = (bf16[256]{0:T(256)(128)(2,1)S(1)}, bf16[256]{0:T(256)(128)(2,1)}, u32[]{:S(2)}) copy-start(bf16[256]{0:T(256)(128)(2,1)} %param.21) | copy-start | bytes 1540
  41.2 21.6 %all-to-all-start.2 = ((bf16[64,16,256]{2,1,0:T(8,128)(2,1)}), bf16[64,16,256]{2,1,0:T(8,128)(2,1)S(1)}, u32[]{:S(2)}, u32[]{:S(2)}) async-start(bf16[64,16,256]{2,1,0:T(8,128)(2,1)} %fusion.15), calls=%async_computation.2 | async-start | bytes 1048576 | tf_op jit(solution)/shard_map/all_to_all | solution.py:94
  67.9 7.3 %copy-start.4 = (bf16[256,256]{1,0:T(8,128)(2,1)S(1)}, bf16[256,256]{1,0:T(8,128)(2,1)}, u32[]{:S(2)}) copy-start(bf16[256,256]{1,0:T(8,128)(2,1)} %param.20) | copy-start | bytes 393220
Sparse Core Ops, SparseCore 0:
  17.0 41.9 all-gather.1
where the time goes:
time: 108 us; the launch traced here: 107 us
  waiting for transfers between devices  24.1 us (22%)
  blocking collectives  19.1 us (18%)
  matrix products  15.7 us (15%)
  local copies, waits for them, and re-layouts  14.7 us (14%)
  starting transfers between devices  13.9 us (13%)
  between operations  13.7 us (13%)
  other arithmetic  6.28 us (6%)
    all_to_all x1, blocking collectives, local(): lax.all_to_all(update, 'res', split_axis=1, concat_axis=0, tiled=True)  19.1 us
    all_to_all x1, waiting for transfers between devices, local(): lax.all_to_all(normed, 'res', split_axis=0, concat_axis=1, tiled=True)  15 us
    sub x1, matrix products, attend_core(): lifted = jnp.exp(scores - highest)  7.3 us
    all_to_all x1, waiting for transfers between devices, local(): lax.all_to_all(outgoing, 'rows', split_axis=0, concat_axis=0, tiled=True)  6.94 us
    all_to_all x1, starting transfers between devices, local(): lax.all_to_all(normed, 'res', split_axis=0, concat_axis=1, tiled=True)  6.19 us
    gather x1, local copies, waits for them, and re-layouts, local(): flattened_source[jnp.maximum(take_rows, 0) * local_columns + col_grid]  4.98 us
    dot_general x1, matrix products, local(): jnp.einsum('rhqd,hdm->rqm', attended, out_weight, preferred_element_type=...  4.98 us
    all_to_all x1, starting transfers between devices, local(): lax.all_to_all(jnp.transpose(requested[:, 0], (1, 0, 2)), 'rows', split_a...  4.21 us
  transfers between devices with their start and end apart: 4, of which 3 were waited for; matrix products, arithmetic and copies ran while one was open for 17% of the time, Pallas kernels for 0%

commit v1 on v0

v1 whole, which is shorter than its diff:
```python
import functools
import math

import jax
import jax.numpy as jnp
from jax import lax
from jax.experimental import pallas as pl
from jax.experimental.pallas import tpu as pltpu
from jax.sharding import PartitionSpec as P

norm_eps = 1e-05
log2e = math.log2(math.e)
parts = 1


def pick_kernel(owners, first_row, pairs_ref, first_ref, gap_ref, *refs):
    blocks, (out_ref, held, sems) = refs[:owners], refs[-3:]
    local_rows, local_columns, channels = blocks[0].shape
    part_rows = out_ref.shape[0]
    pieces = sems.shape[0]
    piece_rows = part_rows // pieces
    chains = first_ref.shape[0]
    shift = local_rows.bit_length() - 1
    assert local_rows == 1 << shift
    me = lax.axis_index("rows")
    start = lax.axis_index("res") * local_columns
    low, high = jnp.int32(0), jnp.int32(0)
    for k in range(1, chains):
        low += (first_ref[k] <= start).astype(jnp.int32)
        high += (first_ref[k] <= start + local_columns - 1).astype(jnp.int32)
    edge = first_ref[high] - start
    in_high = lax.broadcasted_iota(jnp.int32, (local_columns, channels), 0) >= edge
    gap = gap_ref[...].astype(jnp.float32).reshape(1, channels)
    gap = jnp.broadcast_to(gap, (local_columns, channels))
    names = [lax.rem(me - k + owners, owners) for k in range(owners)]

    def cells(row):
        owner = row >> shift
        within = row & (local_rows - 1)
        found = blocks[0][within].astype(jnp.float32)
        for k in range(1, owners):
            found = jnp.where(owner == names[k], blocks[k][within].astype(jnp.float32), found)
        return jnp.where(row >= 0, found, gap)

    def one_row(s, carry):
        row = first_row + s
        picked = jnp.where(in_high, cells(pairs_ref[high, row]), cells(pairs_ref[low, row]))
        held[s] = picked.astype(jnp.bfloat16)
        return carry

    copies = []
    for k in range(pieces):
        rows = pl.ds(k * piece_rows, piece_rows)
        lax.fori_loop(k * piece_rows, (k + 1) * piece_rows, one_row, 0, unroll=piece_rows)
        copies.append(pltpu.make_async_copy(held.at[rows], out_ref.at[rows], sems.at[k]))
        copies[-1].start()
    for copy in copies:
        copy.wait()


def pick(part, parts, pairs, chain_first_residue, gap, blocks, earlier):
    owners = len(blocks)
    local_rows, local_columns, channels = blocks[0].shape
    part_rows = local_rows // parts
    pieces = part_rows // 16
    smem = pl.BlockSpec(memory_space=pltpu.SMEM)
    vmem = pl.BlockSpec(memory_space=pltpu.VMEM)
    anywhere = pl.BlockSpec(memory_space=pl.ANY)
    block_bytes = local_rows * local_columns * channels * 2
    shape = (part_rows, local_columns, channels)
    return pl.pallas_call(
        functools.partial(pick_kernel, owners, part * part_rows),
        out_shape=jax.ShapeDtypeStruct(shape, jnp.bfloat16),
        in_specs=[smem, smem, vmem] + [vmem] * owners + [anywhere] * len(earlier),
        out_specs=anywhere,
        scratch_shapes=[pltpu.VMEM(shape, jnp.bfloat16), pltpu.SemaphoreType.DMA((pieces,))],
        compiler_params=pltpu.CompilerParams(vmem_limit_bytes=(owners + 4) * block_bytes),
        name="pick_joint",
    )(pairs, chain_first_residue, gap, *blocks, *earlier)


def bias_kernel(order, near_ref, far_ref, *refs):
    rows, gate_ref, (out_ref, vectors_ref, held) = refs[:3], refs[3], refs[-3:]
    me = lax.axis_index("res")
    half, heads, block, _ = near_ref.shape
    for place, flip in enumerate(order):
        source = near_ref if place < half else far_ref
        first = pl.multiple_of((me ^ flip) * block, block)
        held[:, pl.ds(first, block), :] = source[place % half].astype(jnp.float32)

    def one_head(h, carry):
        out_ref[h] = held[h].T * log2e
        return carry

    lax.fori_loop(0, heads, one_head, 0)
    width = gate_ref.shape[0]
    for place, ref in enumerate(rows):
        vectors_ref[place : place + 1] = ref[...].astype(jnp.float32).reshape(1, width)
    gate = gate_ref[...].astype(jnp.float32).reshape(1, width)
    vectors_ref[8:] = jnp.broadcast_to(gate, (width, width)).T


def gather_bias(shard):
    members = lax.axis_size("res")

    def swap(piece, flip):
        return lax.ppermute(piece, "res", [(i, i ^ flip) for i in range(members)])

    far, next_far = members // 2, members // 4
    shard = shard[None]
    pieces = [shard]
    order = [0]
    for flip in (far, next_far, far + next_far):
        pieces.append(swap(shard, flip))
        order.append(flip)
    flip = members // 8
    while flip > 1:
        pieces += [swap(piece, flip) for piece in pieces]
        order += [place ^ flip for place in order]
        flip //= 2
    near = jnp.concatenate(pieces, axis=0)
    return near, swap(near, 1), order + [place ^ 1 for place in order]


def order_bias(near, other, order, vectors, earlier):
    half, heads, block, keys = near.shape
    width = vectors[-1].shape[0]
    vmem = pl.BlockSpec(memory_space=pltpu.VMEM)
    anywhere = pl.BlockSpec(memory_space=pl.ANY)
    return pl.pallas_call(
        functools.partial(bias_kernel, order),
        out_shape=[
            jax.ShapeDtypeStruct((heads, keys, 2 * half * block), jnp.float32),
            jax.ShapeDtypeStruct((8 + width, width), jnp.float32),
        ],
        in_specs=[vmem] * (2 + len(vectors)) + [anywhere] * len(earlier),
        out_specs=[vmem] * 2,
        scratch_shapes=[pltpu.VMEM((heads, 2 * half * block, keys), jnp.float32)],
        compiler_params=pltpu.CompilerParams(vmem_limit_bytes=14 << 20),
        name="order_bias",
    )(near, other, *vectors, *earlier)


def weights_kernel(heads, weight_ref, weights_ref):
    width = weight_ref.shape[1] // 4
    depth = width // heads
    turned = weight_ref[...].T
    kinds = []
    for kind in range(4):
        rows = [turned[(h * 4 + kind) * depth : (h * 4 + kind + 1) * depth] for h in range(heads)]
        kinds.append(jnp.concatenate(rows, axis=0))
    for place, kind in enumerate((kinds[0], kinds[2], kinds[3], kinds[1].T)):
        weights_ref[place * width : (place + 1) * width] = kind


def turn_weights(projection_weight):
    channels, heads, four = projection_weight.shape
    width = heads * four // 4
    vmem = pl.BlockSpec(memory_space=pltpu.VMEM)
    return pl.pallas_call(
        functools.partial(weights_kernel, heads),
        out_shape=jax.ShapeDtypeStruct((4 * width, channels), jnp.bfloat16),
        in_specs=[vmem],
        out_specs=vmem,
        compiler_params=pltpu.CompilerParams(vmem_limit_bytes=8 << 20),
        name="turn_weights",
    )(projection_weight.reshape(channels, heads * four))


def attend_kernel(cells_ref, weights_ref, out_weight_ref, vectors_ref, bias_ref, out_ref):
    senders, rows, block, channels = cells_ref.shape
    residues = senders * block
    heads = bias_ref.shape[0]
    width = weights_ref.shape[0] // 4
    depth = width // heads
    ones = jnp.ones((16, residues), jnp.bfloat16)

    def begin(r):
        wide = cells_ref[:, r].reshape(residues, channels).astype(jnp.float32)
        center = jnp.mean(wide, axis=-1, keepdims=True)
        wide = wide - center
        spread = jnp.mean(jnp.square(wide), axis=-1, keepdims=True)
        normed = wide * lax.rsqrt(spread + norm_eps) * vectors_ref[0:1] + vectors_ref[1:2]
        normed = normed.astype(jnp.bfloat16)
        keys = jnp.dot(
            normed, weights_ref[3 * width :], preferred_element_type=jnp.float32
        )
        rest = lax.dot_general(
            weights_ref[: 3 * width], normed, (((1,), (1,)), ((), ())),
            preferred_element_type=jnp.float32,
        )
        queries = (rest[:width] * (depth**-0.5 * log2e)).astype(jnp.bfloat16)
        values = rest[width : 2 * width].astype(jnp.bfloat16)
        gates = 0.5 + 0.5 * jnp.tanh(0.5 * (rest[2 * width :] + vectors_ref[8:]))
        return keys.astype(jnp.bfloat16), queries, values, gates

    def score(row, h):
        keys, queries = row[:2]
        low, high = h * depth, (h + 1) * depth
        scores = jnp.dot(keys[:, low:high], queries[low:high], preferred_element_type=jnp.float32)
        return scores + bias_ref[h]

    def weigh(row, h, scores):
        values, gates = row[2:]
        low, high = h * depth, (h + 1) * depth
        highest = jnp.max(scores, axis=0, keepdims=True)
        lifted = jnp.exp2(scores - highest).astype(jnp.bfloat16)
        left = jnp.concatenate([values[low:high], ones], axis=0)
        summed = jnp.dot(left, lifted, preferred_element_type=jnp.float32)
        inverse = 1.0 / summed[depth : depth + 1]
        return (summed[:depth] * (gates[low:high] * inverse)).astype(jnp.bfloat16)

    def finish(r, heads_out):
        attended = jnp.concatenate(heads_out, axis=0).T
        update = jnp.dot(attended, out_weight_ref[...], preferred_element_type=jnp.float32)
        update = (update + vectors_ref[2:3]).astype(jnp.bfloat16)
        out_ref[:, r] = update.reshape(senders, block, channels)

    steps = [(r, h) for r in range(rows) for h in range(heads)]
    begun = {0: begin(0)}
    scores = score(begun[0], 0)
    done = {r: [] for r in range(rows)}
    for (r, h), later in zip(steps, steps[1:] + [None]):
        if h == heads // 2 and r + 1 < rows:
            begun[r + 1] = begin(r + 1)
        later_scores = score(begun[later[0]], later[1]) if later else None
        if h == 0 and r:
            finish(r - 1, done[r - 1])
        done[r].append(weigh(begun[r], h, scores))
        scores = later_scores
    finish(rows - 1, done[rows - 1])


def attend(cells, weights, out_weight, vectors, bias):
    vmem = pl.BlockSpec(memory_space=pltpu.VMEM)
    return pl.pallas_call(
        attend_kernel,
        out_shape=jax.ShapeDtypeStruct(cells.shape, jnp.bfloat16),
        in_specs=[vmem] * 5,
        out_specs=vmem,
        compiler_params=pltpu.CompilerParams(vmem_limit_bytes=24 << 20),
        name="attend_rows",
    )(cells, weights, out_weight, vectors, bias)


def local(
    source_alignment_rows,
    pairs,
    chain_first_residue,
    gap_embedding,
    layer_norm_gain,
    layer_norm_bias,
    projection_weight,
    gate_bias_heads,
    pair_bias_logits,
    output_weight,
    output_bias,
):
    local_rows, local_columns, channels = source_alignment_rows.shape
    owners = lax.axis_size("rows")
    members = lax.axis_size("res")
    near, other, order = gather_bias(pair_bias_logits)
    blocks = [source_alignment_rows]
    for hop in range(1, owners):
        blocks.append(
            lax.ppermute(
                source_alignment_rows, "rows", [(i, (i + hop) % owners) for i in range(owners)]
            )
        )
    weights = turn_weights(projection_weight)
    arrived = []
    for part in range(parts):
        picked = pick(part, parts, pairs, chain_first_residue, gap_embedding, blocks, (weights,))
        arrived.append(lax.all_to_all(picked, "res", split_axis=0, concat_axis=0, tiled=True))
    bias, vectors = order_bias(
        near,
        other,
        order,
        (layer_norm_gain, layer_norm_bias, output_bias, gate_bias_heads),
        (weights, output_weight),
    )
    results = []
    for cells in arrived:
        part_rows = cells.shape[0]
        update = attend(
            cells.reshape(members, part_rows // members, local_columns, channels),
            weights,
            output_weight,
            vectors,
            bias,
        )
        update = update.reshape(part_rows, local_columns, channels)
        results.append(lax.all_to_all(update, "res", split_axis=0, concat_axis=0, tiled=True))
    return jnp.concatenate(results, axis=0)


def solution(mesh):
    return jax.shard_map(
        local,
        mesh=mesh,
        in_specs=(
            P("rows", "res", None),
            P(None, "rows"),
            P(),
            P(),
            P(),
            P(),
            P(),
            P(),
            P(None, "res", None),
            P(),
            P(),
        ),
        out_specs=P("rows", "res", None),
        check_vma=False,
    )
```

time: 108 us -> 62.4 us (0.58)
  matrix products: 15.7 us -> 0 us
  waiting for transfers between devices: 24.1 us -> 9.7 us
  between operations: 13.7 us -> 0.19 us
  local copies, waits for them, and re-layouts: 14.7 us -> 6.04 us
  Pallas kernels: 0 us -> 8.52 us
  other arithmetic: 6.28 us -> 0 us
  starting transfers between devices: 13.9 us -> 19.2 us
    all_to_all x3 -> x1, waiting for transfers between devices: 23.4 us -> 8.66 us  [local(): lax.all_to_all(picked, 'res', split_axis=0, concat_axis=0, tiled=True)]
    ppermute x0 -> x9, starting transfers between devices: none -> 13 us  [the longest x8 9.99 us: swap(): return lax.ppermute(piece, 'res', [(i, i ^ flip) for i in range(members)])]
    gather x2 -> x0, local copies, waits for them, and re-layouts: 8.92 us -> none  [the longest x1 4.98 us: local(): flattened_source[jnp.maximum(take_rows, 0) * local_columns + col_grid]]
    pallas_call x0 -> x4, Pallas kernels: none -> 8.52 us  [the longest x1 5.21 us: attend(): pl.pallas_call(attend_kernel, out_shape=jax.ShapeDtypeStruct(cells.shape,...]
    dot_general x2 -> x0, matrix products: 8.44 us -> none  [the longest x1 4.98 us: local(): jnp.einsum('rhqd,hdm->rqm', attended, out_weight, preferred_element_type=...]
    all_to_all x3 -> x1, starting transfers between devices: 13.9 us -> 6.2 us  [local(): lax.all_to_all(picked, 'res', split_axis=0, concat_axis=0, tiled=True)]
    sub x1 -> x0, matrix products: 7.3 us -> none  [attend_core(): lifted = jnp.exp(scores - highest)]
    unnamed x19 -> x31, local copies, waits for them, and re-layouts: 1.1 us -> 6.03 us
  transfers between devices with their start and end apart: 4 -> 10, of which waited for: 3 -> 4; matrix products, arithmetic and copies ran while one was open for 17% -> 3% of each run, Pallas kernels for 0% -> 5%
where the time goes in v1:
time: 62.4 us; the launch traced here: 62 us
  starting transfers between devices  19.2 us (31%)
  blocking collectives  18.4 us (29%)
  waiting for transfers between devices  9.7 us (16%)
  Pallas kernels  8.52 us (14%)
  local copies, waits for them, and re-layouts  6.04 us (10%)
    all_to_all x1, blocking collectives, local(): lax.all_to_all(update, 'res', split_axis=0, concat_axis=0, tiled=True)  18.4 us
    ppermute x8, starting transfers between devices, swap(): return lax.ppermute(piece, 'res', [(i, i ^ flip) for i in range(members)])  9.99 us
    all_to_all x1, waiting for transfers between devices, local(): lax.all_to_all(picked, 'res', split_axis=0, concat_axis=0, tiled=True)  8.66 us
    all_to_all x1, starting transfers between devices, local(): lax.all_to_all(picked, 'res', split_axis=0, concat_axis=0, tiled=True)  6.2 us
    unnamed x31, local copies, waits for them, and re-layouts  6.03 us
    pallas_call x1, Pallas kernels, attend(): pl.pallas_call(attend_kernel, out_shape=jax.ShapeDtypeStruct(cells.shape,...  5.21 us
    ppermute x1, starting transfers between devices, local(): lax.ppermute(source_alignment_rows, 'rows', [(i, (i + hop) % owners) for...  3.01 us
    pallas_call x1, Pallas kernels, pick(): pl.pallas_call(functools.partial(pick_kernel, owners, part * part_rows),...  1.77 us
  transfers between devices with their start and end apart: 10, of which 4 were waited for; matrix products, arithmetic and copies ran while one was open for 3% of the time, Pallas kernels for 5%

profile of v1, /device:TPU:0, one launch (start us, length us, event | category | flops | bytes accessed | tf_op | source)
XLA Modules:
  0.0 62.0 jit_solution(14923125495509768355)
XLA Ops:
  0.0 0.0 copy-start.2
  0.0 0.0 copy-start.4
  0.0 0.0 copy-start.9
  0.0 0.0 copy-start.10
  0.0 3.0 %collective-permute-start = (bf16[64,16,256]{2,1,0:T(8,128)(2,1)}, bf16[64,16,256]{2,1,0:T(8,128)(2,1)S(1)}, u32[]{:S(2)}, u32[]{:S(2)}) collective-permute-start(bf16[64,16,256]{2,1,0:T(8,128)(2,1)} %refs_0_.2), channel_id=1, source_target_pairs={{0,16},{16,0},{1,17},{17,1},{2,18},{18,2},{3,19},{19,3},{4,20},{20... | collective-permute-start | bytes 1572872 | tf_op jit(solution)/shard_map/ppermute | solution.py:266
  3.0 2.6 %collective-permute-start.1 = (bf16[1,8,16,256]{3,2,1,0:T(8,128)(2,1)}, bf16[1,8,16,256]{3,2,1,0:T(8,128)(2,1)S(1)}, u32[]{:S(2)}, u32[]{:S(2)}) collective-permute-start(bf16[1,8,16,256]{3,2,1,0:T(8,128)(2,1)} %bitcast.12), channel_id=1, source_target_pairs={{0,8},{1,9},{2,10},{3,11},{4,12},{5,13},{6,14},{7,15},{8,0},{9,1},... | collective-permute-start | bytes 196616 | tf_op jit(solution)/shard_map/ppermute | solution.py:107
  5.6 1.6 %collective-permute-start.2 = (bf16[1,8,16,256]{3,2,1,0:T(8,128)(2,1)}, bf16[1,8,16,256]{3,2,1,0:T(8,128)(2,1)S(1)}, u32[]{:S(2)}, u32[]{:S(2)}) collective-permute-start(bf16[1,8,16,256]{3,2,1,0:T(8,128)(2,1)} %bitcast.13), channel_id=1, source_target_pairs={{0,4},{1,5},{2,6},{3,7},{4,0},{5,1},{6,2},{7,3},{8,12},{9,13},{10,... | collective-permute-start | bytes 196616 | tf_op jit(solution)/shard_map/ppermute | solution.py:107
  7.2 0.2 collective-permute-start.3
  7.4 1.5 %collective-permute-start.4 = (bf16[1,8,16,256]{3,2,1,0:T(8,128)(2,1)}, bf16[1,8,16,256]{3,2,1,0:T(8,128)(2,1)S(1)}, u32[]{:S(2)}, u32[]{:S(2)}) collective-permute-start(bf16[1,8,16,256]{3,2,1,0:T(8,128)(2,1)} %bitcast.15), channel_id=1, source_target_pairs={{0,2},{1,3},{2,0},{3,1},{4,6},{5,7},{6,4},{7,5},{8,10},{9,11},{10,... | collective-permute-start | bytes 196616 | tf_op jit(solution)/shard_map/ppermute | solution.py:107
  8.9 0.9 %constant_dynamic-update-slice_fusion.7 = bf16[8,8,16,256]{3,2,1,0:T(8,128)(2,1)S(1)} fusion(bf16[8,16,256]{2,1,0:T(8,128)(2,1)} %param.19), kind=kLoop, calls=%fused_computation.8 | loop fusion | bytes 131072
  9.8 1.1 %copy.14 = bf16[32,8,8,128]{3,1,2,0:T(8,128)(2,1)S(1)} copy(bf16[32,8,8,128]{3,2,1,0:T(8,128)(2,1)} %bitcast.11) | data formatting | bytes 1048576
  10.9 0.2 turn_weights.1.refs_2_.refs_4_.weights_ref
  11.2 0.0 copy-start.3
  11.2 0.0 copy-start.5
  11.2 0.0 copy-start.6
  11.2 0.0 collective-permute-done.1
  11.2 0.6 collective-permute-start.5
  11.8 0.0 collective-permute-done.2
  11.8 1.5 %collective-permute-start.6 = (bf16[1,8,16,256]{3,2,1,0:T(8,128)(2,1)S(1)}, bf16[1,8,16,256]{3,2,1,0:T(8,128)(2,1)S(1)}, u32[]{:S(2)}, u32[]{:S(2)}) collective-permute-start(bf16[1,8,16,256]{3,2,1,0:T(8,128)(2,1)S(1)} %collective-permute-done.2), channel_id=1, source_target_pairs={{0,2},{1,3},{2,0},{3,1},{4,6},{5,7},{6,4},{7,5},{8,10},{9,11},{10,... | collective-permute-start | bytes 196616 | tf_op jit(solution)/shard_map/ppermute | solution.py:107
  13.3 0.1 collective-permute-done.3
  13.5 1.5 %collective-permute-start.7 = (bf16[1,8,16,256]{3,2,1,0:T(8,128)(2,1)S(1)}, bf16[1,8,16,256]{3,2,1,0:T(8,128)(2,1)S(1)}, u32[]{:S(2)}, u32[]{:S(2)}) collective-permute-start(bf16[1,8,16,256]{3,2,1,0:T(8,128)(2,1)S(1)} %collective-permute-done.3), channel_id=1, source_target_pairs={{0,2},{1,3},{2,0},{3,1},{4,6},{5,7},{6,4},{7,5},{8,10},{9,11},{10,... | collective-permute-start | bytes 196616 | tf_op jit(solution)/shard_map/ppermute | solution.py:107
  15.0 0.2 collective-permute-done.refs_1_
  15.2 0.0 copy-done.2
  15.2 0.0 copy-done.4
  15.2 0.0 copy-done.9
  15.2 0.0 copy-done.10
  15.2 1.8 %pick_joint.1 = bf16[64,16,256]{2,1,0:T(8,128)(2,1)} custom-call(s32[6,64]{1,0:T(8,128)S(1)} %copy-done.4, s32[6]{0:T(128)S(1)} %copy-done.9, bf16[256]{0:T(256)(128)(2,1)S(1)} %copy-done.10, bf16[64,16,256]{2,1,0:T(8,128)(2,1)S(1)} %copy-done.2, bf16[64,16,256]{2,1,0:T(8,128)(2,1)S(1)} %collective-permute-done.refs_1_, ...), custom_call_target="tpu_custom_call" | custom-call | tf_op jit(solution)/shard_map/pick_joint/pallas_call | solution.py:71
  17.0 6.2 %all-to-all-start = ((bf16[64,16,256]{2,1,0:T(8,128)(2,1)}), bf16[64,16,256]{2,1,0:T(8,128)(2,1)S(1)}, u32[]{:S(2)}, u32[]{:S(2)}) async-start(bf16[64,16,256]{2,1,0:T(8,128)(2,1)} %pick_joint.1), calls=%async_computation | async-start | bytes 1048576 | tf_op jit(solution)/shard_map/all_to_all | solution.py:274
  23.2 0.0 collective-permute-done.4
  23.2 0.0 collective-permute-done.5
  23.2 0.0 collective-permute-done.6
  23.3 0.0 collective-permute-done.7
  23.3 0.5 collective-permute-start.8
  23.7 0.0 copy-start
  23.7 0.8 %copy-done = bf16[8,8,16,256]{3,2,1,0:T(8,128)(2,1)} copy-done((bf16[8,8,16,256]{3,2,1,0:T(8,128)(2,1)}, bf16[8,8,16,256]{3,2,1,0:T(8,128)(2,1)S(1)}, u32[]{:S(2)}) %copy-start) | copy-done | bytes 524312
  24.6 0.7 %collective-permute-done.8.far_ref = bf16[8,8,16,256]{3,2,1,0:T(8,128)(2,1)S(1)} collective-permute-done((bf16[8,8,16,256]{3,2,1,0:T(8,128)(2,1)S(1)}, bf16[8,8,16,256]{3,2,1,0:T(8,128)(2,1)S(1)}, u32[]{:S(2)}, u32[]{:S(2)}) %collective-permute-start.8) | collective-permute-done | bytes 524320 | tf_op jit(solution)/shard_map/ppermute | solution.py:107
  25.3 0.0 copy-done.3
  25.3 0.0 copy-done.5
  25.3 0.0 copy-done.6
  25.3 0.0 copy-start.1
  25.3 1.0 %copy-done.1 = bf16[8,8,16,256]{3,2,1,0:T(8,128)(2,1)S(1)} copy-done((bf16[8,8,16,256]{3,2,1,0:T(8,128)(2,1)S(1)}, bf16[8,8,16,256]{3,2,1,0:T(8,128)(2,1)}, u32[]{:S(2)}) %copy-start.1) | copy-done | bytes 524312
  26.3 0.7 %copy-done.7 = bf16[256]{0:T(256)(128)(2,1)S(1)} copy-done((bf16[256]{0:T(256)(128)(2,1)S(1)}, bf16[256]{0:T(256)(128)(2,1)}, u32[]{:S(2)}) %copy-start.7) | copy-done | bytes 536
  27.0 0.7 %copy-done.8 = bf16[256]{0:T(256)(128)(2,1)S(1)} copy-done((bf16[256]{0:T(256)(128)(2,1)S(1)}, bf16[256]{0:T(256)(128)(2,1)}, u32[]{:S(2)}) %copy-start.8) | copy-done | bytes 536
  27.6 1.3 %order_bias.1 = (f32[8,256,256]{2,1,0:T(8,128)S(1)}, f32[264,256]{1,0:T(8,128)S(1)}) custom-call(bf16[8,8,16,256]{3,2,1,0:T(8,128)(2,1)S(1)} %copy-done.1, bf16[8,8,16,256]{3,2,1,0:T(8,128)(2,1)S(1)} %collective-permute-done.8.far_ref, bf16[256]{0:T(256)(128)(2,1)S(1)} %copy-done.5, bf16[256]{0:T(256)(128)(2,1)S(1)} %copy-done.6, ...), custom_call_target="tpu_custom_call" | custom-call | tf_op jit(solution)/shard_map/order_bias/pallas_call | solution.py:130
  29.0 8.7 %all-to-all-done = bf16[64,16,256]{2,1,0:T(8,128)(2,1)S(1)} async-done(((bf16[64,16,256]{2,1,0:T(8,128)(2,1)}), bf16[64,16,256]{2,1,0:T(8,128)(2,1)S(1)}, u32[]{:S(2)}, u32[]{:S(2)}) %all-to-all-start) | async-done | bytes 524320 | tf_op jit(solution)/shard_map/all_to_all | solution.py:274
  37.6 5.2 %attend_rows.1 = bf16[16,4,16,256]{3,2,1,0:T(8,128)(2,1)S(1)} custom-call(bf16[16,4,16,256]{3,2,1,0:T(8,128)(2,1)S(1)} %bitcast.9, bf16[1024,256]{1,0:T(8,128)(2,1)S(1)} %turn_weights.1.refs_2_.refs_4_.weights_ref, bf16[256,256]{1,0:T(8,128)(2,1)S(1)} %copy-done.3, f32[264,256]{1,0:T(8,128)S(1)} %get-tuple-element.7.vectors_ref, ...), custom_call_target="tpu_custom_call" | custom-call | tf_op jit(solution)/shard_map/attend_rows/pallas_call | solution.py:236
  42.8 18.4 %all_to_all.10 = bf16[64,16,256]{2,1,0:T(8,128)(2,1)S(1)} all-to-all(bf16[64,16,256]{2,1,0:T(8,128)(2,1)S(1)} %bitcast.10), channel_id=1, replica_groups=mesh['rows'=2,'res'=16] {'res'}, dimensions={0} | all-to-all | bytes 1048576 | tf_op jit(solution)/shard_map/all_to_all | solution.py:293
  61.2 0.8 %copy.23 = bf16[64,16,256]{2,1,0:T(8,128)(2,1)} copy(bf16[64,16,256]{2,1,0:T(8,128)(2,1)S(1)} %all_to_all.10) | data formatting | bytes 1048576
  (9 shorter events, 0.0 us)
Async XLA Ops:
  0.0 15.2 %copy-start.2 = (bf16[64,16,256]{2,1,0:T(8,128)(2,1)S(1)}, bf16[64,16,256]{2,1,0:T(8,128)(2,1)}, u32[]{:S(2)}) copy-start(bf16[64,16,256]{2,1,0:T(8,128)(2,1)} %refs_0_.2) | copy-start | bytes 1572868
  0.0 15.2 %copy-start.4 = (s32[6,64]{1,0:T(8,128)S(1)}, s32[6,64]{1,0:T(8,128)}, u32[]{:S(2)}) copy-start(s32[6,64]{1,0:T(8,128)} %pairs_ref.1) | copy-start | bytes 4612
  0.0 15.2 %copy-start.9 = (s32[6]{0:T(128)S(1)}, s32[6]{0:T(128)}, u32[]{:S(2)}) copy-start(s32[6]{0:T(128)} %first_ref.1) | copy-start | bytes 76
  0.0 15.2 %copy-start.10 = (bf16[256]{0:T(256)(128)(2,1)S(1)}, bf16[256]{0:T(256)(128)(2,1)}, u32[]{:S(2)}) copy-start(bf16[256]{0:T(256)(128)(2,1)} %gap_ref.1) | copy-start | bytes 1540
  0.0 15.1 %collective-permute-start = (bf16[64,16,256]{2,1,0:T(8,128)(2,1)}, bf16[64,16,256]{2,1,0:T(8,128)(2,1)S(1)}, u32[]{:S(2)}, u32[]{:S(2)}) collective-permute-start(bf16[64,16,256]{2,1,0:T(8,128)(2,1)} %refs_0_.2), channel_id=1, source_target_pairs={{0,16},{16,0},{1,17},{17,1},{2,18},{18,2},{3,19},{19,3},{4,20},{20... | collective-permute-start | bytes 1572872 | tf_op jit(solution)/shard_map/ppermute | solution.py:266
  3.0 8.2 %collective-permute-start.1 = (bf16[1,8,16,256]{3,2,1,0:T(8,128)(2,1)}, bf16[1,8,16,256]{3,2,1,0:T(8,128)(2,1)S(1)}, u32[]{:S(2)}, u32[]{:S(2)}) collective-permute-start(bf16[1,8,16,256]{3,2,1,0:T(8,128)(2,1)} %bitcast.12), channel_id=1, source_target_pairs={{0,8},{1,9},{2,10},{3,11},{4,12},{5,13},{6,14},{7,15},{8,0},{9,1},... | collective-permute-start | bytes 196616 | tf_op jit(solution)/shard_map/ppermute | solution.py:107
  5.6 6.2 %collective-permute-start.2 = (bf16[1,8,16,256]{3,2,1,0:T(8,128)(2,1)}, bf16[1,8,16,256]{3,2,1,0:T(8,128)(2,1)S(1)}, u32[]{:S(2)}, u32[]{:S(2)}) collective-permute-start(bf16[1,8,16,256]{3,2,1,0:T(8,128)(2,1)} %bitcast.13), channel_id=1, source_target_pairs={{0,4},{1,5},{2,6},{3,7},{4,0},{5,1},{6,2},{7,3},{8,12},{9,13},{10,... | collective-permute-start | bytes 196616 | tf_op jit(solution)/shard_map/ppermute | solution.py:107
  7.2 6.3 %collective-permute-start.3 = (bf16[1,8,16,256]{3,2,1,0:T(8,128)(2,1)}, bf16[1,8,16,256]{3,2,1,0:T(8,128)(2,1)S(1)}, u32[]{:S(2)}, u32[]{:S(2)}) collective-permute-start(bf16[1,8,16,256]{3,2,1,0:T(8,128)(2,1)} %bitcast.14), channel_id=1, source_target_pairs={{0,12},{1,13},{2,14},{3,15},{4,8},{5,9},{6,10},{7,11},{8,4},{9,5},... | collective-permute-start | bytes 196616 | tf_op jit(solution)/shard_map/ppermute | solution.py:107
  7.4 15.8 %collective-permute-start.4 = (bf16[1,8,16,256]{3,2,1,0:T(8,128)(2,1)}, bf16[1,8,16,256]{3,2,1,0:T(8,128)(2,1)S(1)}, u32[]{:S(2)}, u32[]{:S(2)}) collective-permute-start(bf16[1,8,16,256]{3,2,1,0:T(8,128)(2,1)} %bitcast.15), channel_id=1, source_target_pairs={{0,2},{1,3},{2,0},{3,1},{4,6},{5,7},{6,4},{7,5},{8,10},{9,11},{10,... | collective-permute-start | bytes 196616 | tf_op jit(solution)/shard_map/ppermute | solution.py:107
  11.2 14.1 %copy-start.3 = (bf16[256,256]{1,0:T(8,128)(2,1)S(1)}, bf16[256,256]{1,0:T(8,128)(2,1)}, u32[]{:S(2)}) copy-start(bf16[256,256]{1,0:T(8,128)(2,1)} %out_weight_ref.1) | copy-start | bytes 393220
  11.2 14.1 %copy-start.5 = (bf16[256]{0:T(256)(128)(2,1)S(1)}, bf16[256]{0:T(256)(128)(2,1)}, u32[]{:S(2)}) copy-start(bf16[256]{0:T(256)(128)(2,1)} %refs_0_.3) | copy-start | bytes 1540
  11.2 14.1 %copy-start.6 = (bf16[256]{0:T(256)(128)(2,1)S(1)}, bf16[256]{0:T(256)(128)(2,1)}, u32[]{:S(2)}) copy-start(bf16[256]{0:T(256)(128)(2,1)} %refs_1_.1) | copy-start | bytes 1540
  11.2 12.0 %collective-permute-start.5 = (bf16[1,8,16,256]{3,2,1,0:T(8,128)(2,1)S(1)}, bf16[1,8,16,256]{3,2,1,0:T(8,128)(2,1)S(1)}, u32[]{:S(2)}, u32[]{:S(2)}) collective-permute-start(bf16[1,8,16,256]{3,2,1,0:T(8,128)(2,1)S(1)} %collective-permute-done.1), channel_id=1, source_target_pairs={{0,2},{1,3},{2,0},{3,1},{4,6},{5,7},{6,4},{7,5},{8,10},{9,11},{10,... | collective-permute-start | bytes 196616 | tf_op jit(solution)/shard_map/ppermute | solution.py:107
  11.8 11.4 %collective-permute-start.6 = (bf16[1,8,16,256]{3,2,1,0:T(8,128)(2,1)S(1)}, bf16[1,8,16,256]{3,2,1,0:T(8,128)(2,1)S(1)}, u32[]{:S(2)}, u32[]{:S(2)}) collective-permute-start(bf16[1,8,16,256]{3,2,1,0:T(8,128)(2,1)S(1)} %collective-permute-done.2), channel_id=1, source_target_pairs={{0,2},{1,3},{2,0},{3,1},{4,6},{5,7},{6,4},{7,5},{8,10},{9,11},{10,... | collective-permute-start | bytes 196616 | tf_op jit(solution)/shard_map/ppermute | solution.py:107
  13.5 9.8 %collective-permute-start.7 = (bf16[1,8,16,256]{3,2,1,0:T(8,128)(2,1)S(1)}, bf16[1,8,16,256]{3,2,1,0:T(8,128)(2,1)S(1)}, u32[]{:S(2)}, u32[]{:S(2)}) collective-permute-start(bf16[1,8,16,256]{3,2,1,0:T(8,128)(2,1)S(1)} %collective-permute-done.3), channel_id=1, source_target_pairs={{0,2},{1,3},{2,0},{3,1},{4,6},{5,7},{6,4},{7,5},{8,10},{9,11},{10,... | collective-permute-start | bytes 196616 | tf_op jit(solution)/shard_map/ppermute | solution.py:107
  17.0 20.7 %all-to-all-start = ((bf16[64,16,256]{2,1,0:T(8,128)(2,1)}), bf16[64,16,256]{2,1,0:T(8,128)(2,1)S(1)}, u32[]{:S(2)}, u32[]{:S(2)}) async-start(bf16[64,16,256]{2,1,0:T(8,128)(2,1)} %pick_joint.1), calls=%async_computation | async-start | bytes 1048576 | tf_op jit(solution)/shard_map/all_to_all | solution.py:274
  23.3 2.0 %collective-permute-start.8 = (bf16[8,8,16,256]{3,2,1,0:T(8,128)(2,1)S(1)}, bf16[8,8,16,256]{3,2,1,0:T(8,128)(2,1)S(1)}, u32[]{:S(2)}, u32[]{:S(2)}) collective-permute-start(bf16[8,8,16,256]{3,2,1,0:T(8,128)(2,1)S(1)} %constant_dynamic-update-slice_fusion.near_ref), channel_id=1, source_target_pairs={{0,1},{1,0},{2,3},{3,2},{4,5},{5,4},{6,7},{7,6},{8,9},{9,8},{10,11... | collective-permute-start | bytes 1572872 | tf_op jit(solution)/shard_map/ppermute | solution.py:107
  23.7 0.8 %copy-start = (bf16[8,8,16,256]{3,2,1,0:T(8,128)(2,1)}, bf16[8,8,16,256]{3,2,1,0:T(8,128)(2,1)S(1)}, u32[]{:S(2)}) copy-start(bf16[8,8,16,256]{3,2,1,0:T(8,128)(2,1)S(1)} %constant_dynamic-update-slice_fusion.near_ref) | copy-start | bytes 1572868
  25.3 1.0 %copy-start.1 = (bf16[8,8,16,256]{3,2,1,0:T(8,128)(2,1)S(1)}, bf16[8,8,16,256]{3,2,1,0:T(8,128)(2,1)}, u32[]{:S(2)}) copy-start(bf16[8,8,16,256]{3,2,1,0:T(8,128)(2,1)} %copy-done) | copy-start | bytes 1572868
  26.3 0.7 %copy-start.7 = (bf16[256]{0:T(256)(128)(2,1)S(1)}, bf16[256]{0:T(256)(128)(2,1)}, u32[]{:S(2)}) copy-start(bf16[256]{0:T(256)(128)(2,1)} %refs_2_.1) | copy-start | bytes 1540
  27.0 0.7 %copy-start.8 = (bf16[256]{0:T(256)(128)(2,1)S(1)}, bf16[256]{0:T(256)(128)(2,1)}, u32[]{:S(2)}) copy-start(bf16[256]{0:T(256)(128)(2,1)} %refs_3_.1) | copy-start | bytes 1540

commit v2 on v1

--- a/solution.py
+++ b/solution.py
@@ -167,13 +167,18 @@
     )(projection_weight.reshape(channels, heads * four))
 
 
-def attend_kernel(cells_ref, weights_ref, out_weight_ref, vectors_ref, bias_ref, out_ref):
+def attend_kernel(
+    cells_ref, weights_ref, out_weight_ref, vectors_ref, bias_ref, out_ref, scores_ref
+):
     senders, rows, block, channels = cells_ref.shape
     residues = senders * block
     heads = bias_ref.shape[0]
     width = weights_ref.shape[0] // 4
     depth = width // heads
     ones = jnp.ones((16, residues), jnp.bfloat16)
+    group = min(128, width)
+    head_of = lax.broadcasted_iota(jnp.int32, (1, group), 1) // depth
+    masks = [(head_of == h).astype(jnp.bfloat16) for h in range(group // depth)]
 
     def begin(r):
         wide = cells_ref[:, r].reshape(residues, channels).astype(jnp.float32)
@@ -191,18 +196,21 @@
         )
         queries = (rest[:width] * (depth**-0.5 * log2e)).astype(jnp.bfloat16)
         values = rest[width : 2 * width].astype(jnp.bfloat16)
+        keys = keys.astype(jnp.bfloat16)
+        for k in range(width // group):
+            lanes = slice(k * group, (k + 1) * group)
+            stack = jnp.concatenate([keys[:, lanes] * mask for mask in masks], axis=0)
+            bias = bias_ref[k * len(masks) : (k + 1) * len(masks)]
+            scores = jnp.dot(stack, queries[lanes], preferred_element_type=jnp.float32)
+            scores_ref[r % 2, k] = scores + bias.reshape(scores.shape)
         gates = 0.5 + 0.5 * jnp.tanh(0.5 * (rest[2 * width :] + vectors_ref[8:]))
-        return keys.astype(jnp.bfloat16), queries, values, gates
-
-    def score(row, h):
-        keys, queries = row[:2]
+        return values, gates
+
+    def weigh(r, h):
+        values, gates = begun[r]
         low, high = h * depth, (h + 1) * depth
-        scores = jnp.dot(keys[:, low:high], queries[low:high], preferred_element_type=jnp.float32)
-        return scores + bias_ref[h]
-
-    def weigh(row, h, scores):
-        values, gates = row[2:]
-        low, high = h * depth, (h + 1) * depth
+        first = low % group // depth * residues
+        scores = scores_ref[r % 2, low // group, first : first + residues]
         highest = jnp.max(scores, axis=0, keepdims=True)
         lifted = jnp.exp2(scores - highest).astype(jnp.bfloat16)
         left = jnp.concatenate([values[low:high], ones], axis=0)
@@ -216,28 +224,30 @@
         update = (update + vectors_ref[2:3]).astype(jnp.bfloat16)
         out_ref[:, r] = update.reshape(senders, block, channels)
 
-    steps = [(r, h) for r in range(rows) for h in range(heads)]
     begun = {0: begin(0)}
-    scores = score(begun[0], 0)
     done = {r: [] for r in range(rows)}
-    for (r, h), later in zip(steps, steps[1:] + [None]):
-        if h == heads // 2 and r + 1 < rows:
-            begun[r + 1] = begin(r + 1)
-        later_scores = score(begun[later[0]], later[1]) if later else None
-        if h == 0 and r:
-            finish(r - 1, done[r - 1])
-        done[r].append(weigh(begun[r], h, scores))
-        scores = later_scores
+    for r in range(rows):
+        for h in range(heads):
+            if h == heads // 2 and r + 1 < rows:
+                begun[r + 1] = begin(r + 1)
+            done[r].append(weigh(r, h))
+            if h == 0 and r:
+                finish(r - 1, done[r - 1])
     finish(rows - 1, done[rows - 1])
 
 
 def attend(cells, weights, out_weight, vectors, bias):
+    heads, residues, _ = bias.shape
+    width = weights.shape[0] // 4
+    group = min(128, width)
     vmem = pl.BlockSpec(memory_space=pltpu.VMEM)
+    score_shape = (2, width // group, heads * group // width * residues, residues)
     return pl.pallas_call(
         attend_kernel,
         out_shape=jax.ShapeDtypeStruct(cells.shape, jnp.bfloat16),
         in_specs=[vmem] * 5,
         out_specs=vmem,
+        scratch_shapes=[pltpu.VMEM(score_shape, jnp.float32)],
         compiler_params=pltpu.CompilerParams(vmem_limit_bytes=24 << 20),
         name="attend_rows",
     )(cells, weights, out_weight, vectors, bias)

time: 62.4 us -> 61.6 us (0.987)
  Pallas kernels: 8.52 us -> 7.67 us
    pallas_call x1, Pallas kernels: 5.21 us -> 4.36 us  [attend(): pl.pallas_call(attend_kernel, out_shape=jax.ShapeDtypeStruct(cells.shape,...]
where the time goes in v2:
time: 61.6 us; the launch traced here: 61.2 us
  starting transfers between devices  19.2 us (31%)
  blocking collectives  18.4 us (30%)
  waiting for transfers between devices  9.7 us (16%)
  Pallas kernels  7.67 us (12%)
  local copies, waits for them, and re-layouts  6.04 us (10%)
    all_to_all x1, blocking collectives, local(): lax.all_to_all(update, 'res', split_axis=0, concat_axis=0, tiled=True)  18.4 us
    ppermute x8, starting transfers between devices, swap(): return lax.ppermute(piece, 'res', [(i, i ^ flip) for i in range(members)])  9.99 us
    all_to_all x1, waiting for transfers between devices, local(): lax.all_to_all(picked, 'res', split_axis=0, concat_axis=0, tiled=True)  8.66 us
    all_to_all x1, starting transfers between devices, local(): lax.all_to_all(picked, 'res', split_axis=0, concat_axis=0, tiled=True)  6.2 us
    unnamed x31, local copies, waits for them, and re-layouts  6.03 us
    pallas_call x1, Pallas kernels, attend(): pl.pallas_call(attend_kernel, out_shape=jax.ShapeDtypeStruct(cells.shape,...  4.36 us
    ppermute x1, starting transfers between devices, local(): lax.ppermute(source_alignment_rows, 'rows', [(i, (i + hop) % owners) for...  3.01 us
    pallas_call x1, Pallas kernels, pick(): pl.pallas_call(functools.partial(pick_kernel, owners, part * part_rows),...  1.77 us
  transfers between devices with their start and end apart: 10, of which 4 were waited for; matrix products, arithmetic and copies ran while one was open for 3% of the time, Pallas kernels for 5%

profile of v2, /device:TPU:0, one launch (start us, length us, event | category | flops | bytes accessed | tf_op | source)
XLA Modules:
  0.0 61.2 jit_solution(4347210624363410867)
XLA Ops:
  0.0 0.0 copy-start.2
  0.0 0.0 copy-start.4
  0.0 0.0 copy-start.9
  0.0 0.0 copy-start.10
  0.0 3.0 %collective-permute-start = (bf16[64,16,256]{2,1,0:T(8,128)(2,1)}, bf16[64,16,256]{2,1,0:T(8,128)(2,1)S(1)}, u32[]{:S(2)}, u32[]{:S(2)}) collective-permute-start(bf16[64,16,256]{2,1,0:T(8,128)(2,1)} %refs_0_.2), channel_id=1, source_target_pairs={{0,16},{16,0},{1,17},{17,1},{2,18},{18,2},{3,19},{19,3},{4,20},{20... | collective-permute-start | bytes 1572872 | tf_op jit(solution)/shard_map/ppermute | solution.py:276
  3.0 2.6 %collective-permute-start.1 = (bf16[1,8,16,256]{3,2,1,0:T(8,128)(2,1)}, bf16[1,8,16,256]{3,2,1,0:T(8,128)(2,1)S(1)}, u32[]{:S(2)}, u32[]{:S(2)}) collective-permute-start(bf16[1,8,16,256]{3,2,1,0:T(8,128)(2,1)} %bitcast.12), channel_id=1, source_target_pairs={{0,8},{1,9},{2,10},{3,11},{4,12},{5,13},{6,14},{7,15},{8,0},{9,1},... | collective-permute-start | bytes 196616 | tf_op jit(solution)/shard_map/ppermute | solution.py:107
  5.6 1.6 %collective-permute-start.2 = (bf16[1,8,16,256]{3,2,1,0:T(8,128)(2,1)}, bf16[1,8,16,256]{3,2,1,0:T(8,128)(2,1)S(1)}, u32[]{:S(2)}, u32[]{:S(2)}) collective-permute-start(bf16[1,8,16,256]{3,2,1,0:T(8,128)(2,1)} %bitcast.13), channel_id=1, source_target_pairs={{0,4},{1,5},{2,6},{3,7},{4,0},{5,1},{6,2},{7,3},{8,12},{9,13},{10,... | collective-permute-start | bytes 196616 | tf_op jit(solution)/shard_map/ppermute | solution.py:107
  7.2 0.2 collective-permute-start.3
  7.4 1.5 %collective-permute-start.4 = (bf16[1,8,16,256]{3,2,1,0:T(8,128)(2,1)}, bf16[1,8,16,256]{3,2,1,0:T(8,128)(2,1)S(1)}, u32[]{:S(2)}, u32[]{:S(2)}) collective-permute-start(bf16[1,8,16,256]{3,2,1,0:T(8,128)(2,1)} %bitcast.15), channel_id=1, source_target_pairs={{0,2},{1,3},{2,0},{3,1},{4,6},{5,7},{6,4},{7,5},{8,10},{9,11},{10,... | collective-permute-start | bytes 196616 | tf_op jit(solution)/shard_map/ppermute | solution.py:107
  8.9 0.9 %constant_dynamic-update-slice_fusion.7 = bf16[8,8,16,256]{3,2,1,0:T(8,128)(2,1)S(1)} fusion(bf16[8,16,256]{2,1,0:T(8,128)(2,1)} %param.19), kind=kLoop, calls=%fused_computation.8 | loop fusion | bytes 131072
  9.8 1.1 %copy.14 = bf16[32,8,8,128]{3,1,2,0:T(8,128)(2,1)S(1)} copy(bf16[32,8,8,128]{3,2,1,0:T(8,128)(2,1)} %bitcast.11) | data formatting | bytes 1048576
  10.9 0.2 turn_weights.1.refs_2_.refs_4_.weights_ref
  11.2 0.0 copy-start.3
  11.2 0.0 copy-start.5
  11.2 0.0 copy-start.6
  11.2 0.0 collective-permute-done.1
  11.2 0.6 collective-permute-start.5
  11.8 0.0 collective-permute-done.2
  11.8 1.5 %collective-permute-start.6 = (bf16[1,8,16,256]{3,2,1,0:T(8,128)(2,1)S(1)}, bf16[1,8,16,256]{3,2,1,0:T(8,128)(2,1)S(1)}, u32[]{:S(2)}, u32[]{:S(2)}) collective-permute-start(bf16[1,8,16,256]{3,2,1,0:T(8,128)(2,1)S(1)} %collective-permute-done.2), channel_id=1, source_target_pairs={{0,2},{1,3},{2,0},{3,1},{4,6},{5,7},{6,4},{7,5},{8,10},{9,11},{10,... | collective-permute-start | bytes 196616 | tf_op jit(solution)/shard_map/ppermute | solution.py:107
  13.3 0.1 collective-permute-done.3
  13.5 1.5 %collective-permute-start.7 = (bf16[1,8,16,256]{3,2,1,0:T(8,128)(2,1)S(1)}, bf16[1,8,16,256]{3,2,1,0:T(8,128)(2,1)S(1)}, u32[]{:S(2)}, u32[]{:S(2)}) collective-permute-start(bf16[1,8,16,256]{3,2,1,0:T(8,128)(2,1)S(1)} %collective-permute-done.3), channel_id=1, source_target_pairs={{0,2},{1,3},{2,0},{3,1},{4,6},{5,7},{6,4},{7,5},{8,10},{9,11},{10,... | collective-permute-start | bytes 196616 | tf_op jit(solution)/shard_map/ppermute | solution.py:107
  15.0 0.2 collective-permute-done.refs_1_
  15.2 0.0 copy-done.2
  15.2 0.0 copy-done.4
  15.2 0.0 copy-done.9
  15.2 0.0 copy-done.10
  15.2 1.8 %pick_joint.1 = bf16[64,16,256]{2,1,0:T(8,128)(2,1)} custom-call(s32[6,64]{1,0:T(8,128)S(1)} %copy-done.4, s32[6]{0:T(128)S(1)} %copy-done.9, bf16[256]{0:T(256)(128)(2,1)S(1)} %copy-done.10, bf16[64,16,256]{2,1,0:T(8,128)(2,1)S(1)} %copy-done.2, bf16[64,16,256]{2,1,0:T(8,128)(2,1)S(1)} %collective-permute-done.refs_1_, ...), custom_call_target="tpu_custom_call" | custom-call | tf_op jit(solution)/shard_map/pick_joint/pallas_call | solution.py:71
  17.0 6.2 %all-to-all-start = ((bf16[64,16,256]{2,1,0:T(8,128)(2,1)}), bf16[64,16,256]{2,1,0:T(8,128)(2,1)S(1)}, u32[]{:S(2)}, u32[]{:S(2)}) async-start(bf16[64,16,256]{2,1,0:T(8,128)(2,1)} %pick_joint.1), calls=%async_computation | async-start | bytes 1048576 | tf_op jit(solution)/shard_map/all_to_all | solution.py:284
  23.2 0.0 collective-permute-done.4
  23.2 0.0 collective-permute-done.5
  23.2 0.0 collective-permute-done.6
  23.3 0.0 collective-permute-done.7
  23.3 0.5 collective-permute-start.8
  23.7 0.0 copy-start
  23.7 0.8 %copy-done = bf16[8,8,16,256]{3,2,1,0:T(8,128)(2,1)} copy-done((bf16[8,8,16,256]{3,2,1,0:T(8,128)(2,1)}, bf16[8,8,16,256]{3,2,1,0:T(8,128)(2,1)S(1)}, u32[]{:S(2)}) %copy-start) | copy-done | bytes 524312
  24.6 0.7 %collective-permute-done.8.far_ref = bf16[8,8,16,256]{3,2,1,0:T(8,128)(2,1)S(1)} collective-permute-done((bf16[8,8,16,256]{3,2,1,0:T(8,128)(2,1)S(1)}, bf16[8,8,16,256]{3,2,1,0:T(8,128)(2,1)S(1)}, u32[]{:S(2)}, u32[]{:S(2)}) %collective-permute-start.8) | collective-permute-done | bytes 524320 | tf_op jit(solution)/shard_map/ppermute | solution.py:107
  25.3 0.0 copy-done.3
  25.3 0.0 copy-done.5
  25.3 0.0 copy-done.6
  25.3 0.0 copy-start.1
  25.3 1.0 %copy-done.1 = bf16[8,8,16,256]{3,2,1,0:T(8,128)(2,1)S(1)} copy-done((bf16[8,8,16,256]{3,2,1,0:T(8,128)(2,1)S(1)}, bf16[8,8,16,256]{3,2,1,0:T(8,128)(2,1)}, u32[]{:S(2)}) %copy-start.1) | copy-done | bytes 524312
  26.3 0.7 %copy-done.7 = bf16[256]{0:T(256)(128)(2,1)S(1)} copy-done((bf16[256]{0:T(256)(128)(2,1)S(1)}, bf16[256]{0:T(256)(128)(2,1)}, u32[]{:S(2)}) %copy-start.7) | copy-done | bytes 536
  27.0 0.7 %copy-done.8 = bf16[256]{0:T(256)(128)(2,1)S(1)} copy-done((bf16[256]{0:T(256)(128)(2,1)S(1)}, bf16[256]{0:T(256)(128)(2,1)}, u32[]{:S(2)}) %copy-start.8) | copy-done | bytes 536
  27.6 1.3 %order_bias.1 = (f32[8,256,256]{2,1,0:T(8,128)S(1)}, f32[264,256]{1,0:T(8,128)S(1)}) custom-call(bf16[8,8,16,256]{3,2,1,0:T(8,128)(2,1)S(1)} %copy-done.1, bf16[8,8,16,256]{3,2,1,0:T(8,128)(2,1)S(1)} %collective-permute-done.8.far_ref, bf16[256]{0:T(256)(128)(2,1)S(1)} %copy-done.5, bf16[256]{0:T(256)(128)(2,1)S(1)} %copy-done.6, ...), custom_call_target="tpu_custom_call" | custom-call | tf_op jit(solution)/shard_map/order_bias/pallas_call | solution.py:130
  29.0 8.7 %all-to-all-done = bf16[64,16,256]{2,1,0:T(8,128)(2,1)S(1)} async-done(((bf16[64,16,256]{2,1,0:T(8,128)(2,1)}), bf16[64,16,256]{2,1,0:T(8,128)(2,1)S(1)}, u32[]{:S(2)}, u32[]{:S(2)}) %all-to-all-start) | async-done | bytes 524320 | tf_op jit(solution)/shard_map/all_to_all | solution.py:284
  37.6 4.4 %attend_rows.1 = bf16[16,4,16,256]{3,2,1,0:T(8,128)(2,1)S(1)} custom-call(bf16[16,4,16,256]{3,2,1,0:T(8,128)(2,1)S(1)} %bitcast.9, bf16[1024,256]{1,0:T(8,128)(2,1)S(1)} %turn_weights.1.refs_2_.refs_4_.weights_ref, bf16[256,256]{1,0:T(8,128)(2,1)S(1)} %copy-done.3, f32[264,256]{1,0:T(8,128)S(1)} %get-tuple-element.7.vectors_ref, ...), custom_call_target="tpu_custom_call" | custom-call | tf_op jit(solution)/shard_map/attend_rows/pallas_call | solution.py:245
  42.0 18.4 %all_to_all.10 = bf16[64,16,256]{2,1,0:T(8,128)(2,1)S(1)} all-to-all(bf16[64,16,256]{2,1,0:T(8,128)(2,1)S(1)} %bitcast.10), channel_id=1, replica_groups=mesh['rows'=2,'res'=16] {'res'}, dimensions={0} | all-to-all | bytes 1048576 | tf_op jit(solution)/shard_map/all_to_all | solution.py:303
  60.4 0.8 %copy.23 = bf16[64,16,256]{2,1,0:T(8,128)(2,1)} copy(bf16[64,16,256]{2,1,0:T(8,128)(2,1)S(1)} %all_to_all.10) | data formatting | bytes 1048576
  (9 shorter events, 0.0 us)
Async XLA Ops:
  0.0 15.2 %copy-start.2 = (bf16[64,16,256]{2,1,0:T(8,128)(2,1)S(1)}, bf16[64,16,256]{2,1,0:T(8,128)(2,1)}, u32[]{:S(2)}) copy-start(bf16[64,16,256]{2,1,0:T(8,128)(2,1)} %refs_0_.2) | copy-start | bytes 1572868
  0.0 15.2 %copy-start.4 = (s32[6,64]{1,0:T(8,128)S(1)}, s32[6,64]{1,0:T(8,128)}, u32[]{:S(2)}) copy-start(s32[6,64]{1,0:T(8,128)} %pairs_ref.1) | copy-start | bytes 4612
  0.0 15.2 %copy-start.9 = (s32[6]{0:T(128)S(1)}, s32[6]{0:T(128)}, u32[]{:S(2)}) copy-start(s32[6]{0:T(128)} %first_ref.1) | copy-start | bytes 76
  0.0 15.2 %copy-start.10 = (bf16[256]{0:T(256)(128)(2,1)S(1)}, bf16[256]{0:T(256)(128)(2,1)}, u32[]{:S(2)}) copy-start(bf16[256]{0:T(256)(128)(2,1)} %gap_ref.1) | copy-start | bytes 1540
  0.0 15.1 %collective-permute-start = (bf16[64,16,256]{2,1,0:T(8,128)(2,1)}, bf16[64,16,256]{2,1,0:T(8,128)(2,1)S(1)}, u32[]{:S(2)}, u32[]{:S(2)}) collective-permute-start(bf16[64,16,256]{2,1,0:T(8,128)(2,1)} %refs_0_.2), channel_id=1, source_target_pairs={{0,16},{16,0},{1,17},{17,1},{2,18},{18,2},{3,19},{19,3},{4,20},{20... | collective-permute-start | bytes 1572872 | tf_op jit(solution)/shard_map/ppermute | solution.py:276
  3.0 8.2 %collective-permute-start.1 = (bf16[1,8,16,256]{3,2,1,0:T(8,128)(2,1)}, bf16[1,8,16,256]{3,2,1,0:T(8,128)(2,1)S(1)}, u32[]{:S(2)}, u32[]{:S(2)}) collective-permute-start(bf16[1,8,16,256]{3,2,1,0:T(8,128)(2,1)} %bitcast.12), channel_id=1, source_target_pairs={{0,8},{1,9},{2,10},{3,11},{4,12},{5,13},{6,14},{7,15},{8,0},{9,1},... | collective-permute-start | bytes 196616 | tf_op jit(solution)/shard_map/ppermute | solution.py:107
  5.6 6.2 %collective-permute-start.2 = (bf16[1,8,16,256]{3,2,1,0:T(8,128)(2,1)}, bf16[1,8,16,256]{3,2,1,0:T(8,128)(2,1)S(1)}, u32[]{:S(2)}, u32[]{:S(2)}) collective-permute-start(bf16[1,8,16,256]{3,2,1,0:T(8,128)(2,1)} %bitcast.13), channel_id=1, source_target_pairs={{0,4},{1,5},{2,6},{3,7},{4,0},{5,1},{6,2},{7,3},{8,12},{9,13},{10,... | collective-permute-start | bytes 196616 | tf_op jit(solution)/shard_map/ppermute | solution.py:107
  7.2 6.3 %collective-permute-start.3 = (bf16[1,8,16,256]{3,2,1,0:T(8,128)(2,1)}, bf16[1,8,16,256]{3,2,1,0:T(8,128)(2,1)S(1)}, u32[]{:S(2)}, u32[]{:S(2)}) collective-permute-start(bf16[1,8,16,256]{3,2,1,0:T(8,128)(2,1)} %bitcast.14), channel_id=1, source_target_pairs={{0,12},{1,13},{2,14},{3,15},{4,8},{5,9},{6,10},{7,11},{8,4},{9,5},... | collective-permute-start | bytes 196616 | tf_op jit(solution)/shard_map/ppermute | solution.py:107
  7.4 15.8 %collective-permute-start.4 = (bf16[1,8,16,256]{3,2,1,0:T(8,128)(2,1)}, bf16[1,8,16,256]{3,2,1,0:T(8,128)(2,1)S(1)}, u32[]{:S(2)}, u32[]{:S(2)}) collective-permute-start(bf16[1,8,16,256]{3,2,1,0:T(8,128)(2,1)} %bitcast.15), channel_id=1, source_target_pairs={{0,2},{1,3},{2,0},{3,1},{4,6},{5,7},{6,4},{7,5},{8,10},{9,11},{10,... | collective-permute-start | bytes 196616 | tf_op jit(solution)/shard_map/ppermute | solution.py:107
  11.2 14.1 %copy-start.3 = (bf16[256,256]{1,0:T(8,128)(2,1)S(1)}, bf16[256,256]{1,0:T(8,128)(2,1)}, u32[]{:S(2)}) copy-start(bf16[256,256]{1,0:T(8,128)(2,1)} %out_weight_ref.1) | copy-start | bytes 393220
  11.2 14.1 %copy-start.5 = (bf16[256]{0:T(256)(128)(2,1)S(1)}, bf16[256]{0:T(256)(128)(2,1)}, u32[]{:S(2)}) copy-start(bf16[256]{0:T(256)(128)(2,1)} %refs_0_.3) | copy-start | bytes 1540
  11.2 14.1 %copy-start.6 = (bf16[256]{0:T(256)(128)(2,1)S(1)}, bf16[256]{0:T(256)(128)(2,1)}, u32[]{:S(2)}) copy-start(bf16[256]{0:T(256)(128)(2,1)} %refs_1_.1) | copy-start | bytes 1540
  11.2 12.0 %collective-permute-start.5 = (bf16[1,8,16,256]{3,2,1,0:T(8,128)(2,1)S(1)}, bf16[1,8,16,256]{3,2,1,0:T(8,128)(2,1)S(1)}, u32[]{:S(2)}, u32[]{:S(2)}) collective-permute-start(bf16[1,8,16,256]{3,2,1,0:T(8,128)(2,1)S(1)} %collective-permute-done.1), channel_id=1, source_target_pairs={{0,2},{1,3},{2,0},{3,1},{4,6},{5,7},{6,4},{7,5},{8,10},{9,11},{10,... | collective-permute-start | bytes 196616 | tf_op jit(solution)/shard_map/ppermute | solution.py:107
  11.8 11.4 %collective-permute-start.6 = (bf16[1,8,16,256]{3,2,1,0:T(8,128)(2,1)S(1)}, bf16[1,8,16,256]{3,2,1,0:T(8,128)(2,1)S(1)}, u32[]{:S(2)}, u32[]{:S(2)}) collective-permute-start(bf16[1,8,16,256]{3,2,1,0:T(8,128)(2,1)S(1)} %collective-permute-done.2), channel_id=1, source_target_pairs={{0,2},{1,3},{2,0},{3,1},{4,6},{5,7},{6,4},{7,5},{8,10},{9,11},{10,... | collective-permute-start | bytes 196616 | tf_op jit(solution)/shard_map/ppermute | solution.py:107
  13.5 9.8 %collective-permute-start.7 = (bf16[1,8,16,256]{3,2,1,0:T(8,128)(2,1)S(1)}, bf16[1,8,16,256]{3,2,1,0:T(8,128)(2,1)S(1)}, u32[]{:S(2)}, u32[]{:S(2)}) collective-permute-start(bf16[1,8,16,256]{3,2,1,0:T(8,128)(2,1)S(1)} %collective-permute-done.3), channel_id=1, source_target_pairs={{0,2},{1,3},{2,0},{3,1},{4,6},{5,7},{6,4},{7,5},{8,10},{9,11},{10,... | collective-permute-start | bytes 196616 | tf_op jit(solution)/shard_map/ppermute | solution.py:107
  17.0 20.7 %all-to-all-start = ((bf16[64,16,256]{2,1,0:T(8,128)(2,1)}), bf16[64,16,256]{2,1,0:T(8,128)(2,1)S(1)}, u32[]{:S(2)}, u32[]{:S(2)}) async-start(bf16[64,16,256]{2,1,0:T(8,128)(2,1)} %pick_joint.1), calls=%async_computation | async-start | bytes 1048576 | tf_op jit(solution)/shard_map/all_to_all | solution.py:284
  23.3 2.0 %collective-permute-start.8 = (bf16[8,8,16,256]{3,2,1,0:T(8,128)(2,1)S(1)}, bf16[8,8,16,256]{3,2,1,0:T(8,128)(2,1)S(1)}, u32[]{:S(2)}, u32[]{:S(2)}) collective-permute-start(bf16[8,8,16,256]{3,2,1,0:T(8,128)(2,1)S(1)} %constant_dynamic-update-slice_fusion.near_ref), channel_id=1, source_target_pairs={{0,1},{1,0},{2,3},{3,2},{4,5},{5,4},{6,7},{7,6},{8,9},{9,8},{10,11... | collective-permute-start | bytes 1572872 | tf_op jit(solution)/shard_map/ppermute | solution.py:107
  23.7 0.8 %copy-start = (bf16[8,8,16,256]{3,2,1,0:T(8,128)(2,1)}, bf16[8,8,16,256]{3,2,1,0:T(8,128)(2,1)S(1)}, u32[]{:S(2)}) copy-start(bf16[8,8,16,256]{3,2,1,0:T(8,128)(2,1)S(1)} %constant_dynamic-update-slice_fusion.near_ref) | copy-start | bytes 1572868
  25.3 1.0 %copy-start.1 = (bf16[8,8,16,256]{3,2,1,0:T(8,128)(2,1)S(1)}, bf16[8,8,16,256]{3,2,1,0:T(8,128)(2,1)}, u32[]{:S(2)}) copy-start(bf16[8,8,16,256]{3,2,1,0:T(8,128)(2,1)} %copy-done) | copy-start | bytes 1572868
  26.3 0.7 %copy-start.7 = (bf16[256]{0:T(256)(128)(2,1)S(1)}, bf16[256]{0:T(256)(128)(2,1)}, u32[]{:S(2)}) copy-start(bf16[256]{0:T(256)(128)(2,1)} %refs_2_.1) | copy-start | bytes 1540
  27.0 0.7 %copy-start.8 = (bf16[256]{0:T(256)(128)(2,1)S(1)}, bf16[256]{0:T(256)(128)(2,1)}, u32[]{:S(2)}) copy-start(bf16[256]{0:T(256)(128)(2,1)} %refs_3_.1) | copy-start | bytes 1540

commit v3 on v2

--- a/solution.py
+++ b/solution.py
@@ -10,7 +10,7 @@
 
 norm_eps = 1e-05
 log2e = math.log2(math.e)
-parts = 1
+cores = 2
 
 
 def pick_kernel(owners, first_row, pairs_ref, first_ref, gap_ref, *refs):
@@ -167,10 +167,10 @@
     )(projection_weight.reshape(channels, heads * four))
 
 
-def attend_kernel(
-    cells_ref, weights_ref, out_weight_ref, vectors_ref, bias_ref, out_ref, scores_ref
-):
+def attend_kernel(cells_ref, weights_ref, out_weight_ref, vectors_ref, bias_ref, *refs):
+    out_refs, (staged_ref, scores_ref) = refs[:-2], refs[-2:]
     senders, rows, block, channels = cells_ref.shape
+    me = lax.axis_index("res")
     residues = senders * block
     heads = bias_ref.shape[0]
     width = weights_ref.shape[0] // 4
@@ -200,9 +200,9 @@
         for k in range(width // group):
             lanes = slice(k * group, (k + 1) * group)
             stack = jnp.concatenate([keys[:, lanes] * mask for mask in masks], axis=0)
-            bias = bias_ref[k * len(masks) : (k + 1) * len(masks)]
-            scores = jnp.dot(stack, queries[lanes], preferred_element_type=jnp.float32)
-            scores_ref[r % 2, k] = scores + bias.reshape(scores.shape)
+            scores_ref[r % 2, k] = jnp.dot(
+                stack, queries[lanes], preferred_element_type=jnp.float32
+            )
         gates = 0.5 + 0.5 * jnp.tanh(0.5 * (rest[2 * width :] + vectors_ref[8:]))
         return values, gates
 
@@ -210,7 +210,7 @@
         values, gates = begun[r]
         low, high = h * depth, (h + 1) * depth
         first = low % group // depth * residues
-        scores = scores_ref[r % 2, low // group, first : first + residues]
+        scores = scores_ref[r % 2, low // group, first : first + residues] + bias_ref[h]
         highest = jnp.max(scores, axis=0, keepdims=True)
         lifted = jnp.exp2(scores - highest).astype(jnp.bfloat16)
         left = jnp.concatenate([values[low:high], ones], axis=0)
@@ -222,7 +222,9 @@
         attended = jnp.concatenate(heads_out, axis=0).T
         update = jnp.dot(attended, out_weight_ref[...], preferred_element_type=jnp.float32)
         update = (update + vectors_ref[2:3]).astype(jnp.bfloat16)
-        out_ref[:, r] = update.reshape(senders, block, channels)
+        staged_ref[...] = update.reshape(senders, block, channels)
+        for flip in range(senders):
+            out_refs[flip // cores][flip % cores, r] = staged_ref[me ^ flip]
 
     begun = {0: begin(0)}
     done = {r: [] for r in range(rows)}
@@ -238,19 +240,65 @@
 
 def attend(cells, weights, out_weight, vectors, bias):
     heads, residues, _ = bias.shape
+    senders, rows, block, channels = cells.shape
     width = weights.shape[0] // 4
     group = min(128, width)
     vmem = pl.BlockSpec(memory_space=pltpu.VMEM)
     score_shape = (2, width // group, heads * group // width * residues, residues)
+    piece = jax.ShapeDtypeStruct((cores, rows, block, channels), jnp.bfloat16)
     return pl.pallas_call(
         attend_kernel,
-        out_shape=jax.ShapeDtypeStruct(cells.shape, jnp.bfloat16),
+        out_shape=[piece] * (senders // cores),
         in_specs=[vmem] * 5,
-        out_specs=vmem,
-        scratch_shapes=[pltpu.VMEM(score_shape, jnp.float32)],
+        out_specs=[vmem] * (senders // cores),
+        scratch_shapes=[
+            pltpu.VMEM((senders, block, channels), jnp.bfloat16),
+            pltpu.VMEM(score_shape, jnp.float32),
+        ],
         compiler_params=pltpu.CompilerParams(vmem_limit_bytes=24 << 20),
         name="attend_rows",
     )(cells, weights, out_weight, vectors, bias)
+
+
+def swap(array, flip):
+    members = lax.axis_size("res")
+    return lax.ppermute(array, "res", [(i, i ^ flip) for i in range(members)])
+
+
+def spread(pieces):
+    half = len(pieces) // 2
+    order = [1, *range(half, len(pieces)), *range(2, half), 0]
+    arrived = [swap(pieces[chip], chip * cores) if chip else pieces[0] for chip in order]
+    return order, arrived, swap(jnp.stack([piece[1] for piece in arrived]), 1)
+
+
+def place_kernel(order, *refs):
+    piece_refs, (other_ref, out_ref, sems) = refs[:-3], refs[-3:]
+    me = lax.axis_index("res")
+    rows = other_ref.shape[1]
+    copies = []
+    for k, chip in enumerate(order):
+        for core, source in enumerate((piece_refs[k].at[0], other_ref.at[k])):
+            first = (me ^ (chip * cores + core)) * rows
+            target = out_ref.at[pl.ds(first, rows)]
+            copies.append(pltpu.make_async_copy(source, target, sems.at[len(copies)]))
+    for copy in copies:
+        copy.start()
+    for copy in copies:
+        copy.wait()
+
+
+def place(order, pieces, other, shape):
+    vmem = pl.BlockSpec(memory_space=pltpu.VMEM)
+    return pl.pallas_call(
+        functools.partial(place_kernel, order),
+        out_shape=jax.ShapeDtypeStruct(shape, jnp.bfloat16),
+        in_specs=[vmem] * (len(pieces) + 1),
+        out_specs=pl.BlockSpec(memory_space=pl.ANY),
+        scratch_shapes=[pltpu.SemaphoreType.DMA((cores * len(pieces),))],
+        compiler_params=pltpu.CompilerParams(vmem_limit_bytes=8 << 20),
+        name="place_rows",
+    )(*pieces, other)
 
 
 def local(
@@ -278,10 +326,8 @@
             )
         )
     weights = turn_weights(projection_weight)
-    arrived = []
-    for part in range(parts):
-        picked = pick(part, parts, pairs, chain_first_residue, gap_embedding, blocks, (weights,))
-        arrived.append(lax.all_to_all(picked, "res", split_axis=0, concat_axis=0, tiled=True))
+    joint = pick(0, 1, pairs, chain_first_residue, gap_embedding, blocks, (weights,))
+    cells = lax.all_to_all(joint, "res", split_axis=0, concat_axis=0, tiled=True)
     bias, vectors = order_bias(
         near,
         other,
@@ -289,19 +335,9 @@
         (layer_norm_gain, layer_norm_bias, output_bias, gate_bias_heads),
         (weights, output_weight),
     )
-    results = []
-    for cells in arrived:
-        part_rows = cells.shape[0]
-        update = attend(
-            cells.reshape(members, part_rows // members, local_columns, channels),
-            weights,
-            output_weight,
-            vectors,
-            bias,
-        )
-        update = update.reshape(part_rows, local_columns, channels)
-        results.append(lax.all_to_all(update, "res", split_axis=0, concat_axis=0, tiled=True))
-    return jnp.concatenate(results, axis=0)
+    cells = cells.reshape(members, local_rows // members, local_columns, channels)
+    arrived = spread(attend(cells, weights, output_weight, vectors, bias))
+    return place(*arrived, (local_rows, local_columns, channels))
 
 
 def solution(mesh):

time: 61.6 us -> 61.4 us (level)
  blocking collectives: 18.4 us -> 0 us
  starting transfers between devices: 19.2 us -> 29 us
  waiting for transfers between devices: 9.7 us -> 17.8 us
  Pallas kernels: 7.67 us -> 8.6 us
  local copies, waits for them, and re-layouts: 6.04 us -> 5.27 us
    all_to_all x1 -> x0, blocking collectives: 18.4 us -> none  [local(): lax.all_to_all(update, 'res', split_axis=0, concat_axis=0, tiled=True)]
    ppermute x0 -> x8, starting transfers between devices: none -> 9.85 us  [swap(): return lax.ppermute(array, 'res', [(i, i ^ flip) for i in range(members)])]
    ppermute x0 -> x8, waiting for transfers between devices: none -> 8.14 us  [swap(): return lax.ppermute(array, 'res', [(i, i ^ flip) for i in range(members)])]
    pallas_call x1 -> x2, Pallas kernels: 4.36 us -> 5.28 us  [the longest x1 4.37 us: attend(): pl.pallas_call(attend_kernel, out_shape=[piece] * (senders // cores), in_...]
    unnamed x31 -> x37, local copies, waits for them, and re-layouts: 6.03 us -> 5.26 us
  transfers between devices with their start and end apart: 10 -> 18, of which waited for: 4 -> 8; matrix products, arithmetic and copies ran while one was open for 3% -> 3% of each run, Pallas kernels for 5% -> 5%
where the time goes in v3:
time: 61.4 us; the launch traced here: 61 us
  starting transfers between devices  29 us (47%)
  waiting for transfers between devices  17.8 us (29%)
  Pallas kernels  8.6 us (14%)
  local copies, waits for them, and re-layouts  5.27 us (9%)
    ppermute x8, starting transfers between devices, swap(): return lax.ppermute(piece, 'res', [(i, i ^ flip) for i in range(members)])  9.99 us
    ppermute x8, starting transfers between devices, swap(): return lax.ppermute(array, 'res', [(i, i ^ flip) for i in range(members)])  9.85 us
    all_to_all x1, waiting for transfers between devices, local(): lax.all_to_all(joint, 'res', split_axis=0, concat_axis=0, tiled=True)  8.66 us
    ppermute x8, waiting for transfers between devices, swap(): return lax.ppermute(array, 'res', [(i, i ^ flip) for i in range(members)])  8.14 us
    all_to_all x1, starting transfers between devices, local(): lax.all_to_all(joint, 'res', split_axis=0, concat_axis=0, tiled=True)  6.2 us
    unnamed x37, local copies, waits for them, and re-layouts  5.26 us
    pallas_call x1, Pallas kernels, attend(): pl.pallas_call(attend_kernel, out_shape=[piece] * (senders // cores), in_...  4.37 us
    ppermute x1, starting transfers between devices, local(): lax.ppermute(source_alignment_rows, 'rows', [(i, (i + hop) % owners) for...  3.01 us
  transfers between devices with their start and end apart: 18, of which 8 were waited for; matrix products, arithmetic and copies ran while one was open for 3% of the time, Pallas kernels for 5%

profile of v3, /device:TPU:0, one launch (start us, length us, event | category | flops | bytes accessed | tf_op | source)
XLA Modules:
  0.0 61.0 jit_solution(88663442176806452)
XLA Ops:
  0.0 3.0 %collective-permute-start = (bf16[64,16,256]{2,1,0:T(8,128)(2,1)}, bf16[64,16,256]{2,1,0:T(8,128)(2,1)S(1)}, u32[]{:S(2)}, u32[]{:S(2)}) collective-permute-start(bf16[64,16,256]{2,1,0:T(8,128)(2,1)} %refs_0_.2), channel_id=1, source_target_pairs={{0,16},{16,0},{1,17},{17,1},{2,18},{18,2},{3,19},{19,3},{4,20},{20... | collective-permute-start | bytes 1572872 | tf_op jit(solution)/shard_map/ppermute | solution.py:324
  3.0 2.6 %collective-permute-start.1 = (bf16[1,8,16,256]{3,2,1,0:T(8,128)(2,1)}, bf16[1,8,16,256]{3,2,1,0:T(8,128)(2,1)S(1)}, u32[]{:S(2)}, u32[]{:S(2)}) collective-permute-start(bf16[1,8,16,256]{3,2,1,0:T(8,128)(2,1)} %bitcast.10), channel_id=1, source_target_pairs={{0,8},{1,9},{2,10},{3,11},{4,12},{5,13},{6,14},{7,15},{8,0},{9,1},... | collective-permute-start | bytes 196616 | tf_op jit(solution)/shard_map/ppermute | solution.py:107
  5.6 1.6 %collective-permute-start.2 = (bf16[1,8,16,256]{3,2,1,0:T(8,128)(2,1)}, bf16[1,8,16,256]{3,2,1,0:T(8,128)(2,1)S(1)}, u32[]{:S(2)}, u32[]{:S(2)}) collective-permute-start(bf16[1,8,16,256]{3,2,1,0:T(8,128)(2,1)} %bitcast.11), channel_id=1, source_target_pairs={{0,4},{1,5},{2,6},{3,7},{4,0},{5,1},{6,2},{7,3},{8,12},{9,13},{10,... | collective-permute-start | bytes 196616 | tf_op jit(solution)/shard_map/ppermute | solution.py:107
  7.2 0.2 collective-permute-start.3
  7.4 1.5 %collective-permute-start.4 = (bf16[1,8,16,256]{3,2,1,0:T(8,128)(2,1)}, bf16[1,8,16,256]{3,2,1,0:T(8,128)(2,1)S(1)}, u32[]{:S(2)}, u32[]{:S(2)}) collective-permute-start(bf16[1,8,16,256]{3,2,1,0:T(8,128)(2,1)} %bitcast.13), channel_id=1, source_target_pairs={{0,2},{1,3},{2,0},{3,1},{4,6},{5,7},{6,4},{7,5},{8,10},{9,11},{10,... | collective-permute-start | bytes 196616 | tf_op jit(solution)/shard_map/ppermute | solution.py:107
  8.9 0.9 %constant_dynamic-update-slice_fusion.7 = bf16[8,8,16,256]{3,2,1,0:T(8,128)(2,1)S(1)} fusion(bf16[8,16,256]{2,1,0:T(8,128)(2,1)} %param.19), kind=kLoop, calls=%fused_computation.8 | loop fusion | bytes 131072
  9.8 1.1 %copy.14 = bf16[32,8,8,128]{3,1,2,0:T(8,128)(2,1)S(1)} copy(bf16[32,8,8,128]{3,2,1,0:T(8,128)(2,1)} %bitcast.9) | data formatting | bytes 1048576
  10.9 0.2 turn_weights.1.refs_2_.refs_4_.weights_ref
  11.2 0.0 copy-start.2
  11.2 0.0 copy-start.5
  11.2 0.0 copy-start.6
  11.2 0.0 collective-permute-done.1
  11.2 0.6 collective-permute-start.5
  11.8 0.0 collective-permute-done.2
  11.8 1.5 %collective-permute-start.6 = (bf16[1,8,16,256]{3,2,1,0:T(8,128)(2,1)S(1)}, bf16[1,8,16,256]{3,2,1,0:T(8,128)(2,1)S(1)}, u32[]{:S(2)}, u32[]{:S(2)}) collective-permute-start(bf16[1,8,16,256]{3,2,1,0:T(8,128)(2,1)S(1)} %collective-permute-done.2), channel_id=1, source_target_pairs={{0,2},{1,3},{2,0},{3,1},{4,6},{5,7},{6,4},{7,5},{8,10},{9,11},{10,... | collective-permute-start | bytes 196616 | tf_op jit(solution)/shard_map/ppermute | solution.py:107
  13.3 0.1 collective-permute-done.3
  13.5 1.5 %collective-permute-start.7 = (bf16[1,8,16,256]{3,2,1,0:T(8,128)(2,1)S(1)}, bf16[1,8,16,256]{3,2,1,0:T(8,128)(2,1)S(1)}, u32[]{:S(2)}, u32[]{:S(2)}) collective-permute-start(bf16[1,8,16,256]{3,2,1,0:T(8,128)(2,1)S(1)} %collective-permute-done.3), channel_id=1, source_target_pairs={{0,2},{1,3},{2,0},{3,1},{4,6},{5,7},{6,4},{7,5},{8,10},{9,11},{10,... | collective-permute-start | bytes 196616 | tf_op jit(solution)/shard_map/ppermute | solution.py:107
  15.0 0.2 collective-permute-done.refs_1_
  15.2 1.8 %pick_joint.1 = bf16[64,16,256]{2,1,0:T(8,128)(2,1)} custom-call(s32[6,64]{1,0:T(8,128)S(1)} %copy-done.4, s32[6]{0:T(128)S(1)} %copy-done.9, bf16[256]{0:T(256)(128)(2,1)S(1)} %copy-done.10, bf16[64,16,256]{2,1,0:T(8,128)(2,1)S(1)} %copy-done.3, bf16[64,16,256]{2,1,0:T(8,128)(2,1)S(1)} %collective-permute-done.refs_1_, ...), custom_call_target="tpu_custom_call" | custom-call | tf_op jit(solution)/shard_map/pick_joint/pallas_call | solution.py:71
  17.0 6.2 %all-to-all-start = ((bf16[64,16,256]{2,1,0:T(8,128)(2,1)}), bf16[64,16,256]{2,1,0:T(8,128)(2,1)S(1)}, u32[]{:S(2)}, u32[]{:S(2)}) async-start(bf16[64,16,256]{2,1,0:T(8,128)(2,1)} %pick_joint.1), calls=%async_computation | async-start | bytes 1048576 | tf_op jit(solution)/shard_map/all_to_all | solution.py:330
  23.2 0.0 collective-permute-done.4
  23.2 0.0 collective-permute-done.5
  23.2 0.0 collective-permute-done.6
  23.3 0.0 collective-permute-done.7
  23.3 0.5 collective-permute-start.8
  23.7 0.8 %copy-done = bf16[8,8,16,256]{3,2,1,0:T(8,128)(2,1)} copy-done((bf16[8,8,16,256]{3,2,1,0:T(8,128)(2,1)}, bf16[8,8,16,256]{3,2,1,0:T(8,128)(2,1)S(1)}, u32[]{:S(2)}) %copy-start) | copy-done | bytes 524312
  24.6 0.7 %collective-permute-done.8.far_ref = bf16[8,8,16,256]{3,2,1,0:T(8,128)(2,1)S(1)} collective-permute-done((bf16[8,8,16,256]{3,2,1,0:T(8,128)(2,1)S(1)}, bf16[8,8,16,256]{3,2,1,0:T(8,128)(2,1)S(1)}, u32[]{:S(2)}, u32[]{:S(2)}) %collective-permute-start.8) | collective-permute-done | bytes 524320 | tf_op jit(solution)/shard_map/ppermute | solution.py:107
  25.3 1.0 %copy-done.1 = bf16[8,8,16,256]{3,2,1,0:T(8,128)(2,1)S(1)} copy-done((bf16[8,8,16,256]{3,2,1,0:T(8,128)(2,1)S(1)}, bf16[8,8,16,256]{3,2,1,0:T(8,128)(2,1)}, u32[]{:S(2)}) %copy-start.1) | copy-done | bytes 524312
  26.3 0.7 %copy-done.7 = bf16[256]{0:T(256)(128)(2,1)S(1)} copy-done((bf16[256]{0:T(256)(128)(2,1)S(1)}, bf16[256]{0:T(256)(128)(2,1)}, u32[]{:S(2)}) %copy-start.7) | copy-done | bytes 536
  27.0 0.7 %copy-done.8 = bf16[256]{0:T(256)(128)(2,1)S(1)} copy-done((bf16[256]{0:T(256)(128)(2,1)S(1)}, bf16[256]{0:T(256)(128)(2,1)}, u32[]{:S(2)}) %copy-start.8) | copy-done | bytes 536
  27.6 1.3 %order_bias.1 = (f32[8,256,256]{2,1,0:T(8,128)S(1)}, f32[264,256]{1,0:T(8,128)S(1)}) custom-call(bf16[8,8,16,256]{3,2,1,0:T(8,128)(2,1)S(1)} %copy-done.1, bf16[8,8,16,256]{3,2,1,0:T(8,128)(2,1)S(1)} %collective-permute-done.8.far_ref, bf16[256]{0:T(256)(128)(2,1)S(1)} %copy-done.5, bf16[256]{0:T(256)(128)(2,1)S(1)} %copy-done.6, ...), custom_call_target="tpu_custom_call" | custom-call | tf_op jit(solution)/shard_map/order_bias/pallas_call | solution.py:130
  29.0 8.7 %all-to-all-done = bf16[64,16,256]{2,1,0:T(8,128)(2,1)S(1)} async-done(((bf16[64,16,256]{2,1,0:T(8,128)(2,1)}), bf16[64,16,256]{2,1,0:T(8,128)(2,1)S(1)}, u32[]{:S(2)}, u32[]{:S(2)}) %all-to-all-start) | async-done | bytes 524320 | tf_op jit(solution)/shard_map/all_to_all | solution.py:330
  37.6 4.4 %attend_rows.1 = (bf16[2,4,16,256]{3,2,1,0:T(8,128)(2,1)S(1)}, bf16[2,4,16,256]{3,2,1,0:T(8,128)(2,1)S(1)}, bf16[2,4,16,256]{3,2,1,0:T(8,128)(2,1)S(1)}, bf16[2,...) custom-call(bf16[16,4,16,256]{3,2,1,0:T(8,128)(2,1)S(1)} %bitcast.7,, ...), custom_call_target="tpu_custom_call" | custom-call | tf_op jit(solution)/shard_map/attend_rows/pallas_call | solution.py:249
  42.0 0.5 collective-permute-start.9
  42.5 1.9 %collective-permute-start.10 = (bf16[2,4,16,256]{3,2,1,0:T(8,128)(2,1)S(1)}, bf16[2,4,16,256]{3,2,1,0:T(8,128)(2,1)S(1)}, u32[]{:S(2)}, u32[]{:S(2)}) collective-permute-start(bf16[2,4,16,256]{3,2,1,0:T(8,128)(2,1)S(1)} %get-tuple-element.18), channel_id=1, source_target_pairs={{0,8},{1,9},{2,10},{3,11},{4,12},{5,13},{6,14},{7,15},{8,0},{9,1},... | collective-permute-start | bytes 196616 | tf_op jit(solution)/shard_map/ppermute | solution.py:265
  44.4 2.1 %collective-permute-start.11 = (bf16[2,4,16,256]{3,2,1,0:T(8,128)(2,1)S(1)}, bf16[2,4,16,256]{3,2,1,0:T(8,128)(2,1)S(1)}, u32[]{:S(2)}, u32[]{:S(2)}) collective-permute-start(bf16[2,4,16,256]{3,2,1,0:T(8,128)(2,1)S(1)} %get-tuple-element.19), channel_id=1, source_target_pairs={{0,10},{1,11},{2,8},{3,9},{4,14},{5,15},{6,12},{7,13},{8,2},{9,3},... | collective-permute-start | bytes 196616 | tf_op jit(solution)/shard_map/ppermute | solution.py:265
  46.5 1.4 %collective-permute-start.12 = (bf16[2,4,16,256]{3,2,1,0:T(8,128)(2,1)S(1)}, bf16[2,4,16,256]{3,2,1,0:T(8,128)(2,1)S(1)}, u32[]{:S(2)}, u32[]{:S(2)}) collective-permute-start(bf16[2,4,16,256]{3,2,1,0:T(8,128)(2,1)S(1)} %get-tuple-element.20), channel_id=1, source_target_pairs={{0,12},{1,13},{2,14},{3,15},{4,8},{5,9},{6,10},{7,11},{8,4},{9,5},... | collective-permute-start | bytes 196616 | tf_op jit(solution)/shard_map/ppermute | solution.py:265
  47.8 2.3 %collective-permute-start.13 = (bf16[2,4,16,256]{3,2,1,0:T(8,128)(2,1)S(1)}, bf16[2,4,16,256]{3,2,1,0:T(8,128)(2,1)S(1)}, u32[]{:S(2)}, u32[]{:S(2)}) collective-permute-start(bf16[2,4,16,256]{3,2,1,0:T(8,128)(2,1)S(1)} %get-tuple-element.21), channel_id=1, source_target_pairs={{0,14},{1,15},{2,12},{3,13},{4,10},{5,11},{6,8},{7,9},{8,6},{9,7},... | collective-permute-start | bytes 196616 | tf_op jit(solution)/shard_map/ppermute | solution.py:265
  50.1 0.0 collective-permute-done.9.refs_0_
  50.1 0.2 collective-permute-start.14
  50.3 1.4 %collective-permute-done.10.refs_1_ = bf16[2,4,16,256]{3,2,1,0:T(8,128)(2,1)S(1)} collective-permute-done((bf16[2,4,16,256]{3,2,1,0:T(8,128)(2,1)S(1)}, bf16[2,4,16,256]{3,2,1,0:T(8,128)(2,1)S(1)}, u32[]{:S(2)}, u32[]{:S(2)}) %collective-permute-start.10) | collective-permute-done | bytes 65568 | tf_op jit(solution)/shard_map/ppermute | solution.py:265
  51.7 1.5 %collective-permute-start.15 = (bf16[2,4,16,256]{3,2,1,0:T(8,128)(2,1)S(1)}, bf16[2,4,16,256]{3,2,1,0:T(8,128)(2,1)S(1)}, u32[]{:S(2)}, u32[]{:S(2)}) collective-permute-start(bf16[2,4,16,256]{3,2,1,0:T(8,128)(2,1)S(1)} %get-tuple-element.23), channel_id=1, source_target_pairs={{0,6},{1,7},{2,4},{3,5},{4,2},{5,3},{6,0},{7,1},{8,14},{9,15},{10,... | collective-permute-start | bytes 196616 | tf_op jit(solution)/shard_map/ppermute | solution.py:265
  53.2 3.2 %collective-permute-done.11.refs_2_ = bf16[2,4,16,256]{3,2,1,0:T(8,128)(2,1)S(1)} collective-permute-done((bf16[2,4,16,256]{3,2,1,0:T(8,128)(2,1)S(1)}, bf16[2,4,16,256]{3,2,1,0:T(8,128)(2,1)S(1)}, u32[]{:S(2)}, u32[]{:S(2)}) %collective-permute-start.11) | collective-permute-done | bytes 65568 | tf_op jit(solution)/shard_map/ppermute | solution.py:265
  56.4 0.0 collective-permute-done.12.refs_3_
  56.5 2.0 %collective-permute-done.15.refs_6_ = bf16[2,4,16,256]{3,2,1,0:T(8,128)(2,1)S(1)} collective-permute-done((bf16[2,4,16,256]{3,2,1,0:T(8,128)(2,1)S(1)}, bf16[2,4,16,256]{3,2,1,0:T(8,128)(2,1)S(1)}, u32[]{:S(2)}, u32[]{:S(2)}) %collective-permute-start.15) | collective-permute-done | bytes 65568 | tf_op jit(solution)/shard_map/ppermute | solution.py:265
  58.5 0.1 collective-permute-start.16
  58.6 1.5 %collective-permute-done.16.refs_8_ = bf16[8,4,16,256]{3,2,1,0:T(8,128)(2,1)S(1)} collective-permute-done((bf16[8,4,16,256]{3,2,1,0:T(8,128)(2,1)S(1)}, bf16[8,4,16,256]{3,2,1,0:T(8,128)(2,1)S(1)}, u32[]{:S(2)}, u32[]{:S(2)}) %collective-permute-start.16) | collective-permute-done | bytes 262176 | tf_op jit(solution)/shard_map/ppermute | solution.py:265
  60.1 0.9 %place_rows.1 = bf16[64,16,256]{2,1,0:T(8,128)(2,1)} custom-call(bf16[2,4,16,256]{3,2,1,0:T(8,128)(2,1)S(1)} %collective-permute-done.9.refs_0_, bf16[2,4,16,256]{3,2,1,0:T(8,128)(2,1)S(1)} %collective-permute-done.10.refs_1_, bf16[2,4,16,256]{3,2,1,0:T(8,128)(2,1)S(1)} %collective-permute-done.11.refs_2_, ...), custom_call_target="tpu_custom_call" | custom-call | tf_op jit(solution)/shard_map/place_rows/pallas_call | solution.py:293
  (32 shorter events, 0.1 us)
Async XLA Ops:
  0.0 15.2 %copy-start.3 = (bf16[64,16,256]{2,1,0:T(8,128)(2,1)S(1)}, bf16[64,16,256]{2,1,0:T(8,128)(2,1)}, u32[]{:S(2)}) copy-start(bf16[64,16,256]{2,1,0:T(8,128)(2,1)} %refs_0_.2) | copy-start | bytes 1572868
  0.0 15.2 %copy-start.4 = (s32[6,64]{1,0:T(8,128)S(1)}, s32[6,64]{1,0:T(8,128)}, u32[]{:S(2)}) copy-start(s32[6,64]{1,0:T(8,128)} %pairs_ref.1) | copy-start | bytes 4612
  0.0 15.2 %copy-start.9 = (s32[6]{0:T(128)S(1)}, s32[6]{0:T(128)}, u32[]{:S(2)}) copy-start(s32[6]{0:T(128)} %first_ref.1) | copy-start | bytes 76
  0.0 15.2 %copy-start.10 = (bf16[256]{0:T(256)(128)(2,1)S(1)}, bf16[256]{0:T(256)(128)(2,1)}, u32[]{:S(2)}) copy-start(bf16[256]{0:T(256)(128)(2,1)} %gap_ref.1) | copy-start | bytes 1540
  0.0 15.1 %collective-permute-start = (bf16[64,16,256]{2,1,0:T(8,128)(2,1)}, bf16[64,16,256]{2,1,0:T(8,128)(2,1)S(1)}, u32[]{:S(2)}, u32[]{:S(2)}) collective-permute-start(bf16[64,16,256]{2,1,0:T(8,128)(2,1)} %refs_0_.2), channel_id=1, source_target_pairs={{0,16},{16,0},{1,17},{17,1},{2,18},{18,2},{3,19},{19,3},{4,20},{20... | collective-permute-start | bytes 1572872 | tf_op jit(solution)/shard_map/ppermute | solution.py:324
  3.0 8.2 %collective-permute-start.1 = (bf16[1,8,16,256]{3,2,1,0:T(8,128)(2,1)}, bf16[1,8,16,256]{3,2,1,0:T(8,128)(2,1)S(1)}, u32[]{:S(2)}, u32[]{:S(2)}) collective-permute-start(bf16[1,8,16,256]{3,2,1,0:T(8,128)(2,1)} %bitcast.10), channel_id=1, source_target_pairs={{0,8},{1,9},{2,10},{3,11},{4,12},{5,13},{6,14},{7,15},{8,0},{9,1},... | collective-permute-start | bytes 196616 | tf_op jit(solution)/shard_map/ppermute | solution.py:107
  5.6 6.2 %collective-permute-start.2 = (bf16[1,8,16,256]{3,2,1,0:T(8,128)(2,1)}, bf16[1,8,16,256]{3,2,1,0:T(8,128)(2,1)S(1)}, u32[]{:S(2)}, u32[]{:S(2)}) collective-permute-start(bf16[1,8,16,256]{3,2,1,0:T(8,128)(2,1)} %bitcast.11), channel_id=1, source_target_pairs={{0,4},{1,5},{2,6},{3,7},{4,0},{5,1},{6,2},{7,3},{8,12},{9,13},{10,... | collective-permute-start | bytes 196616 | tf_op jit(solution)/shard_map/ppermute | solution.py:107
  7.2 6.3 %collective-permute-start.3 = (bf16[1,8,16,256]{3,2,1,0:T(8,128)(2,1)}, bf16[1,8,16,256]{3,2,1,0:T(8,128)(2,1)S(1)}, u32[]{:S(2)}, u32[]{:S(2)}) collective-permute-start(bf16[1,8,16,256]{3,2,1,0:T(8,128)(2,1)} %bitcast.12), channel_id=1, source_target_pairs={{0,12},{1,13},{2,14},{3,15},{4,8},{5,9},{6,10},{7,11},{8,4},{9,5},... | collective-permute-start | bytes 196616 | tf_op jit(solution)/shard_map/ppermute | solution.py:107
  7.4 15.8 %collective-permute-start.4 = (bf16[1,8,16,256]{3,2,1,0:T(8,128)(2,1)}, bf16[1,8,16,256]{3,2,1,0:T(8,128)(2,1)S(1)}, u32[]{:S(2)}, u32[]{:S(2)}) collective-permute-start(bf16[1,8,16,256]{3,2,1,0:T(8,128)(2,1)} %bitcast.13), channel_id=1, source_target_pairs={{0,2},{1,3},{2,0},{3,1},{4,6},{5,7},{6,4},{7,5},{8,10},{9,11},{10,... | collective-permute-start | bytes 196616 | tf_op jit(solution)/shard_map/ppermute | solution.py:107
  11.2 14.1 %copy-start.2 = (bf16[256,256]{1,0:T(8,128)(2,1)S(1)}, bf16[256,256]{1,0:T(8,128)(2,1)}, u32[]{:S(2)}) copy-start(bf16[256,256]{1,0:T(8,128)(2,1)} %out_weight_ref.1) | copy-start | bytes 393220
  11.2 14.1 %copy-start.5 = (bf16[256]{0:T(256)(128)(2,1)S(1)}, bf16[256]{0:T(256)(128)(2,1)}, u32[]{:S(2)}) copy-start(bf16[256]{0:T(256)(128)(2,1)} %refs_0_.3) | copy-start | bytes 1540
  11.2 14.1 %copy-start.6 = (bf16[256]{0:T(256)(128)(2,1)S(1)}, bf16[256]{0:T(256)(128)(2,1)}, u32[]{:S(2)}) copy-start(bf16[256]{0:T(256)(128)(2,1)} %refs_1_.1) | copy-start | bytes 1540
  11.2 12.0 %collective-permute-start.5 = (bf16[1,8,16,256]{3,2,1,0:T(8,128)(2,1)S(1)}, bf16[1,8,16,256]{3,2,1,0:T(8,128)(2,1)S(1)}, u32[]{:S(2)}, u32[]{:S(2)}) collective-permute-start(bf16[1,8,16,256]{3,2,1,0:T(8,128)(2,1)S(1)} %collective-permute-done.1), channel_id=1, source_target_pairs={{0,2},{1,3},{2,0},{3,1},{4,6},{5,7},{6,4},{7,5},{8,10},{9,11},{10,... | collective-permute-start | bytes 196616 | tf_op jit(solution)/shard_map/ppermute | solution.py:107
  11.8 11.4 %collective-permute-start.6 = (bf16[1,8,16,256]{3,2,1,0:T(8,128)(2,1)S(1)}, bf16[1,8,16,256]{3,2,1,0:T(8,128)(2,1)S(1)}, u32[]{:S(2)}, u32[]{:S(2)}) collective-permute-start(bf16[1,8,16,256]{3,2,1,0:T(8,128)(2,1)S(1)} %collective-permute-done.2), channel_id=1, source_target_pairs={{0,2},{1,3},{2,0},{3,1},{4,6},{5,7},{6,4},{7,5},{8,10},{9,11},{10,... | collective-permute-start | bytes 196616 | tf_op jit(solution)/shard_map/ppermute | solution.py:107
  13.5 9.8 %collective-permute-start.7 = (bf16[1,8,16,256]{3,2,1,0:T(8,128)(2,1)S(1)}, bf16[1,8,16,256]{3,2,1,0:T(8,128)(2,1)S(1)}, u32[]{:S(2)}, u32[]{:S(2)}) collective-permute-start(bf16[1,8,16,256]{3,2,1,0:T(8,128)(2,1)S(1)} %collective-permute-done.3), channel_id=1, source_target_pairs={{0,2},{1,3},{2,0},{3,1},{4,6},{5,7},{6,4},{7,5},{8,10},{9,11},{10,... | collective-permute-start | bytes 196616 | tf_op jit(solution)/shard_map/ppermute | solution.py:107
  17.0 20.7 %all-to-all-start = ((bf16[64,16,256]{2,1,0:T(8,128)(2,1)}), bf16[64,16,256]{2,1,0:T(8,128)(2,1)S(1)}, u32[]{:S(2)}, u32[]{:S(2)}) async-start(bf16[64,16,256]{2,1,0:T(8,128)(2,1)} %pick_joint.1), calls=%async_computation | async-start | bytes 1048576 | tf_op jit(solution)/shard_map/all_to_all | solution.py:330
  23.3 2.0 %collective-permute-start.8 = (bf16[8,8,16,256]{3,2,1,0:T(8,128)(2,1)S(1)}, bf16[8,8,16,256]{3,2,1,0:T(8,128)(2,1)S(1)}, u32[]{:S(2)}, u32[]{:S(2)}) collective-permute-start(bf16[8,8,16,256]{3,2,1,0:T(8,128)(2,1)S(1)} %constant_dynamic-update-slice_fusion.near_ref), channel_id=1, source_target_pairs={{0,1},{1,0},{2,3},{3,2},{4,5},{5,4},{6,7},{7,6},{8,9},{9,8},{10,11... | collective-permute-start | bytes 1572872 | tf_op jit(solution)/shard_map/ppermute | solution.py:107
  23.7 0.8 %copy-start = (bf16[8,8,16,256]{3,2,1,0:T(8,128)(2,1)}, bf16[8,8,16,256]{3,2,1,0:T(8,128)(2,1)S(1)}, u32[]{:S(2)}) copy-start(bf16[8,8,16,256]{3,2,1,0:T(8,128)(2,1)S(1)} %constant_dynamic-update-slice_fusion.near_ref) | copy-start | bytes 1572868
  25.3 1.0 %copy-start.1 = (bf16[8,8,16,256]{3,2,1,0:T(8,128)(2,1)S(1)}, bf16[8,8,16,256]{3,2,1,0:T(8,128)(2,1)}, u32[]{:S(2)}) copy-start(bf16[8,8,16,256]{3,2,1,0:T(8,128)(2,1)} %copy-done) | copy-start | bytes 1572868
  26.3 0.7 %copy-start.7 = (bf16[256]{0:T(256)(128)(2,1)S(1)}, bf16[256]{0:T(256)(128)(2,1)}, u32[]{:S(2)}) copy-start(bf16[256]{0:T(256)(128)(2,1)} %refs_2_.1) | copy-start | bytes 1540
  27.0 0.7 %copy-start.8 = (bf16[256]{0:T(256)(128)(2,1)S(1)}, bf16[256]{0:T(256)(128)(2,1)}, u32[]{:S(2)}) copy-start(bf16[256]{0:T(256)(128)(2,1)} %refs_3_.1) | copy-start | bytes 1540
  42.0 8.1 %collective-permute-start.9 = (bf16[2,4,16,256]{3,2,1,0:T(8,128)(2,1)S(1)}, bf16[2,4,16,256]{3,2,1,0:T(8,128)(2,1)S(1)}, u32[]{:S(2)}, u32[]{:S(2)}) collective-permute-start(bf16[2,4,16,256]{3,2,1,0:T(8,128)(2,1)S(1)} %get-tuple-element.17), channel_id=1, source_target_pairs={{0,2},{1,3},{2,0},{3,1},{4,6},{5,7},{6,4},{7,5},{8,10},{9,11},{10,... | collective-permute-start | bytes 196616 | tf_op jit(solution)/shard_map/ppermute | solution.py:265
  42.5 9.3 %collective-permute-start.10 = (bf16[2,4,16,256]{3,2,1,0:T(8,128)(2,1)S(1)}, bf16[2,4,16,256]{3,2,1,0:T(8,128)(2,1)S(1)}, u32[]{:S(2)}, u32[]{:S(2)}) collective-permute-start(bf16[2,4,16,256]{3,2,1,0:T(8,128)(2,1)S(1)} %get-tuple-element.18), channel_id=1, source_target_pairs={{0,8},{1,9},{2,10},{3,11},{4,12},{5,13},{6,14},{7,15},{8,0},{9,1},... | collective-permute-start | bytes 196616 | tf_op jit(solution)/shard_map/ppermute | solution.py:265
  44.4 12.0 %collective-permute-start.11 = (bf16[2,4,16,256]{3,2,1,0:T(8,128)(2,1)S(1)}, bf16[2,4,16,256]{3,2,1,0:T(8,128)(2,1)S(1)}, u32[]{:S(2)}, u32[]{:S(2)}) collective-permute-start(bf16[2,4,16,256]{3,2,1,0:T(8,128)(2,1)S(1)} %get-tuple-element.19), channel_id=1, source_target_pairs={{0,10},{1,11},{2,8},{3,9},{4,14},{5,15},{6,12},{7,13},{8,2},{9,3},... | collective-permute-start | bytes 196616 | tf_op jit(solution)/shard_map/ppermute | solution.py:265
  46.5 9.9 %collective-permute-start.12 = (bf16[2,4,16,256]{3,2,1,0:T(8,128)(2,1)S(1)}, bf16[2,4,16,256]{3,2,1,0:T(8,128)(2,1)S(1)}, u32[]{:S(2)}, u32[]{:S(2)}) collective-permute-start(bf16[2,4,16,256]{3,2,1,0:T(8,128)(2,1)S(1)} %get-tuple-element.20), channel_id=1, source_target_pairs={{0,12},{1,13},{2,14},{3,15},{4,8},{5,9},{6,10},{7,11},{8,4},{9,5},... | collective-permute-start | bytes 196616 | tf_op jit(solution)/shard_map/ppermute | solution.py:265
  47.8 8.6 %collective-permute-start.13 = (bf16[2,4,16,256]{3,2,1,0:T(8,128)(2,1)S(1)}, bf16[2,4,16,256]{3,2,1,0:T(8,128)(2,1)S(1)}, u32[]{:S(2)}, u32[]{:S(2)}) collective-permute-start(bf16[2,4,16,256]{3,2,1,0:T(8,128)(2,1)S(1)} %get-tuple-element.21), channel_id=1, source_target_pairs={{0,14},{1,15},{2,12},{3,13},{4,10},{5,11},{6,8},{7,9},{8,6},{9,7},... | collective-permute-start | bytes 196616 | tf_op jit(solution)/shard_map/ppermute | solution.py:265
  50.1 6.3 %collective-permute-start.14 = (bf16[2,4,16,256]{3,2,1,0:T(8,128)(2,1)S(1)}, bf16[2,4,16,256]{3,2,1,0:T(8,128)(2,1)S(1)}, u32[]{:S(2)}, u32[]{:S(2)}) collective-permute-start(bf16[2,4,16,256]{3,2,1,0:T(8,128)(2,1)S(1)} %get-tuple-element.22), channel_id=1, source_target_pairs={{0,4},{1,5},{2,6},{3,7},{4,0},{5,1},{6,2},{7,3},{8,12},{9,13},{10,... | collective-permute-start | bytes 196616 | tf_op jit(solution)/shard_map/ppermute | solution.py:265
  51.7 6.7 %collective-permute-start.15 = (bf16[2,4,16,256]{3,2,1,0:T(8,128)(2,1)S(1)}, bf16[2,4,16,256]{3,2,1,0:T(8,128)(2,1)S(1)}, u32[]{:S(2)}, u32[]{:S(2)}) collective-permute-start(bf16[2,4,16,256]{3,2,1,0:T(8,128)(2,1)S(1)} %get-tuple-element.23), channel_id=1, source_target_pairs={{0,6},{1,7},{2,4},{3,5},{4,2},{5,3},{6,0},{7,1},{8,14},{9,15},{10,... | collective-permute-start | bytes 196616 | tf_op jit(solution)/shard_map/ppermute | solution.py:265
  58.5 1.6 %collective-permute-start.16 = (bf16[8,4,16,256]{3,2,1,0:T(8,128)(2,1)S(1)}, bf16[8,4,16,256]{3,2,1,0:T(8,128)(2,1)S(1)}, u32[]{:S(2)}, u32[]{:S(2)}) collective-permute-start(bf16[8,4,16,256]{3,2,1,0:T(8,128)(2,1)S(1)} %constant_dynamic-update-slice_fusion.8), channel_id=1, source_target_pairs={{0,1},{1,0},{2,3},{3,2},{4,5},{5,4},{6,7},{7,6},{8,9},{9,8},{10,11... | collective-permute-start | bytes 786440 | tf_op jit(solution)/shard_map/ppermute | solution.py:265

commit v4 on v3

--- a/solution.py
+++ b/solution.py
@@ -267,7 +267,8 @@
 
 def spread(pieces):
     half = len(pieces) // 2
-    order = [1, *range(half, len(pieces)), *range(2, half), 0]
+    line = half // 2
+    order = [line, *range(half, 2 * half), *range(line + 1, half), *range(1, line), 0]
     arrived = [swap(pieces[chip], chip * cores) if chip else pieces[0] for chip in order]
     return order, arrived, swap(jnp.stack([piece[1] for piece in arrived]), 1)
 

time: 61.4 us -> 61.5 us (level)
  waiting for transfers between devices: 17.8 us -> 18.7 us
  starting transfers between devices: 29 us -> 28.3 us
    ppermute x8, waiting for transfers between devices: 8.14 us -> 8.98 us  [swap(): return lax.ppermute(array, 'res', [(i, i ^ flip) for i in range(members)])]
    ppermute x8, starting transfers between devices: 9.85 us -> 9.14 us  [swap(): return lax.ppermute(array, 'res', [(i, i ^ flip) for i in range(members)])]
  transfers between devices with their start and end apart: 18 -> 18, of which waited for: 8 -> 9; matrix products, arithmetic and copies ran while one was open for 3% -> 3% of each run, Pallas kernels for 5% -> 5%
where the time goes in v4:
time: 61.5 us; the launch traced here: 61.1 us
  starting transfers between devices  28.3 us (46%)
  waiting for transfers between devices  18.7 us (30%)
  Pallas kernels  8.6 us (14%)
  local copies, waits for them, and re-layouts  5.27 us (9%)
    ppermute x8, starting transfers between devices, swap(): return lax.ppermute(piece, 'res', [(i, i ^ flip) for i in range(members)])  9.99 us
    ppermute x8, starting transfers between devices, swap(): return lax.ppermute(array, 'res', [(i, i ^ flip) for i in range(members)])  9.14 us
    ppermute x8, waiting for transfers between devices, swap(): return lax.ppermute(array, 'res', [(i, i ^ flip) for i in range(members)])  8.98 us
    all_to_all x1, waiting for transfers between devices, local(): lax.all_to_all(joint, 'res', split_axis=0, concat_axis=0, tiled=True)  8.66 us
    all_to_all x1, starting transfers between devices, local(): lax.all_to_all(joint, 'res', split_axis=0, concat_axis=0, tiled=True)  6.2 us
    unnamed x37, local copies, waits for them, and re-layouts  5.26 us
    pallas_call x1, Pallas kernels, attend(): pl.pallas_call(attend_kernel, out_shape=[piece] * (senders // cores), in_...  4.37 us
    ppermute x1, starting transfers between devices, local(): lax.ppermute(source_alignment_rows, 'rows', [(i, (i + hop) % owners) for...  3.01 us
  transfers between devices with their start and end apart: 18, of which 9 were waited for; matrix products, arithmetic and copies ran while one was open for 3% of the time, Pallas kernels for 5%

profile of v4, /device:TPU:0, one launch (start us, length us, event | category | flops | bytes accessed | tf_op | source)
XLA Modules:
  0.0 61.1 jit_solution(18403464552157347951)
XLA Ops:
  0.0 3.0 %collective-permute-start = (bf16[64,16,256]{2,1,0:T(8,128)(2,1)}, bf16[64,16,256]{2,1,0:T(8,128)(2,1)S(1)}, u32[]{:S(2)}, u32[]{:S(2)}) collective-permute-start(bf16[64,16,256]{2,1,0:T(8,128)(2,1)} %refs_0_.2), channel_id=1, source_target_pairs={{0,16},{16,0},{1,17},{17,1},{2,18},{18,2},{3,19},{19,3},{4,20},{20... | collective-permute-start | bytes 1572872 | tf_op jit(solution)/shard_map/ppermute | solution.py:325
  3.0 2.6 %collective-permute-start.1 = (bf16[1,8,16,256]{3,2,1,0:T(8,128)(2,1)}, bf16[1,8,16,256]{3,2,1,0:T(8,128)(2,1)S(1)}, u32[]{:S(2)}, u32[]{:S(2)}) collective-permute-start(bf16[1,8,16,256]{3,2,1,0:T(8,128)(2,1)} %bitcast.10), channel_id=1, source_target_pairs={{0,8},{1,9},{2,10},{3,11},{4,12},{5,13},{6,14},{7,15},{8,0},{9,1},... | collective-permute-start | bytes 196616 | tf_op jit(solution)/shard_map/ppermute | solution.py:107
  5.6 1.6 %collective-permute-start.2 = (bf16[1,8,16,256]{3,2,1,0:T(8,128)(2,1)}, bf16[1,8,16,256]{3,2,1,0:T(8,128)(2,1)S(1)}, u32[]{:S(2)}, u32[]{:S(2)}) collective-permute-start(bf16[1,8,16,256]{3,2,1,0:T(8,128)(2,1)} %bitcast.11), channel_id=1, source_target_pairs={{0,4},{1,5},{2,6},{3,7},{4,0},{5,1},{6,2},{7,3},{8,12},{9,13},{10,... | collective-permute-start | bytes 196616 | tf_op jit(solution)/shard_map/ppermute | solution.py:107
  7.2 0.2 collective-permute-start.3
  7.4 1.5 %collective-permute-start.4 = (bf16[1,8,16,256]{3,2,1,0:T(8,128)(2,1)}, bf16[1,8,16,256]{3,2,1,0:T(8,128)(2,1)S(1)}, u32[]{:S(2)}, u32[]{:S(2)}) collective-permute-start(bf16[1,8,16,256]{3,2,1,0:T(8,128)(2,1)} %bitcast.13), channel_id=1, source_target_pairs={{0,2},{1,3},{2,0},{3,1},{4,6},{5,7},{6,4},{7,5},{8,10},{9,11},{10,... | collective-permute-start | bytes 196616 | tf_op jit(solution)/shard_map/ppermute | solution.py:107
  8.9 0.9 %constant_dynamic-update-slice_fusion.7 = bf16[8,8,16,256]{3,2,1,0:T(8,128)(2,1)S(1)} fusion(bf16[8,16,256]{2,1,0:T(8,128)(2,1)} %param.19), kind=kLoop, calls=%fused_computation.8 | loop fusion | bytes 131072
  9.8 1.1 %copy.14 = bf16[32,8,8,128]{3,1,2,0:T(8,128)(2,1)S(1)} copy(bf16[32,8,8,128]{3,2,1,0:T(8,128)(2,1)} %bitcast.9) | data formatting | bytes 1048576
  10.9 0.2 turn_weights.1.refs_2_.refs_4_.weights_ref
  11.2 0.0 copy-start.2
  11.2 0.0 copy-start.5
  11.2 0.0 copy-start.6
  11.2 0.0 collective-permute-done.1
  11.2 0.6 collective-permute-start.5
  11.8 0.0 collective-permute-done.2
  11.8 1.5 %collective-permute-start.6 = (bf16[1,8,16,256]{3,2,1,0:T(8,128)(2,1)S(1)}, bf16[1,8,16,256]{3,2,1,0:T(8,128)(2,1)S(1)}, u32[]{:S(2)}, u32[]{:S(2)}) collective-permute-start(bf16[1,8,16,256]{3,2,1,0:T(8,128)(2,1)S(1)} %collective-permute-done.2), channel_id=1, source_target_pairs={{0,2},{1,3},{2,0},{3,1},{4,6},{5,7},{6,4},{7,5},{8,10},{9,11},{10,... | collective-permute-start | bytes 196616 | tf_op jit(solution)/shard_map/ppermute | solution.py:107
  13.3 0.1 collective-permute-done.3
  13.5 1.5 %collective-permute-start.7 = (bf16[1,8,16,256]{3,2,1,0:T(8,128)(2,1)S(1)}, bf16[1,8,16,256]{3,2,1,0:T(8,128)(2,1)S(1)}, u32[]{:S(2)}, u32[]{:S(2)}) collective-permute-start(bf16[1,8,16,256]{3,2,1,0:T(8,128)(2,1)S(1)} %collective-permute-done.3), channel_id=1, source_target_pairs={{0,2},{1,3},{2,0},{3,1},{4,6},{5,7},{6,4},{7,5},{8,10},{9,11},{10,... | collective-permute-start | bytes 196616 | tf_op jit(solution)/shard_map/ppermute | solution.py:107
  15.0 0.2 collective-permute-done.refs_1_
  15.2 1.8 %pick_joint.1 = bf16[64,16,256]{2,1,0:T(8,128)(2,1)} custom-call(s32[6,64]{1,0:T(8,128)S(1)} %copy-done.4, s32[6]{0:T(128)S(1)} %copy-done.9, bf16[256]{0:T(256)(128)(2,1)S(1)} %copy-done.10, bf16[64,16,256]{2,1,0:T(8,128)(2,1)S(1)} %copy-done.3, bf16[64,16,256]{2,1,0:T(8,128)(2,1)S(1)} %collective-permute-done.refs_1_, ...), custom_call_target="tpu_custom_call" | custom-call | tf_op jit(solution)/shard_map/pick_joint/pallas_call | solution.py:71
  17.0 6.2 %all-to-all-start = ((bf16[64,16,256]{2,1,0:T(8,128)(2,1)}), bf16[64,16,256]{2,1,0:T(8,128)(2,1)S(1)}, u32[]{:S(2)}, u32[]{:S(2)}) async-start(bf16[64,16,256]{2,1,0:T(8,128)(2,1)} %pick_joint.1), calls=%async_computation | async-start | bytes 1048576 | tf_op jit(solution)/shard_map/all_to_all | solution.py:331
  23.2 0.0 collective-permute-done.4
  23.2 0.0 collective-permute-done.5
  23.2 0.0 collective-permute-done.6
  23.3 0.0 collective-permute-done.7
  23.3 0.5 collective-permute-start.8
  23.7 0.8 %copy-done = bf16[8,8,16,256]{3,2,1,0:T(8,128)(2,1)} copy-done((bf16[8,8,16,256]{3,2,1,0:T(8,128)(2,1)}, bf16[8,8,16,256]{3,2,1,0:T(8,128)(2,1)S(1)}, u32[]{:S(2)}) %copy-start) | copy-done | bytes 524312
  24.6 0.7 %collective-permute-done.8.far_ref = bf16[8,8,16,256]{3,2,1,0:T(8,128)(2,1)S(1)} collective-permute-done((bf16[8,8,16,256]{3,2,1,0:T(8,128)(2,1)S(1)}, bf16[8,8,16,256]{3,2,1,0:T(8,128)(2,1)S(1)}, u32[]{:S(2)}, u32[]{:S(2)}) %collective-permute-start.8) | collective-permute-done | bytes 524320 | tf_op jit(solution)/shard_map/ppermute | solution.py:107
  25.3 1.0 %copy-done.1 = bf16[8,8,16,256]{3,2,1,0:T(8,128)(2,1)S(1)} copy-done((bf16[8,8,16,256]{3,2,1,0:T(8,128)(2,1)S(1)}, bf16[8,8,16,256]{3,2,1,0:T(8,128)(2,1)}, u32[]{:S(2)}) %copy-start.1) | copy-done | bytes 524312
  26.3 0.7 %copy-done.7 = bf16[256]{0:T(256)(128)(2,1)S(1)} copy-done((bf16[256]{0:T(256)(128)(2,1)S(1)}, bf16[256]{0:T(256)(128)(2,1)}, u32[]{:S(2)}) %copy-start.7) | copy-done | bytes 536
  27.0 0.7 %copy-done.8 = bf16[256]{0:T(256)(128)(2,1)S(1)} copy-done((bf16[256]{0:T(256)(128)(2,1)S(1)}, bf16[256]{0:T(256)(128)(2,1)}, u32[]{:S(2)}) %copy-start.8) | copy-done | bytes 536
  27.6 1.3 %order_bias.1 = (f32[8,256,256]{2,1,0:T(8,128)S(1)}, f32[264,256]{1,0:T(8,128)S(1)}) custom-call(bf16[8,8,16,256]{3,2,1,0:T(8,128)(2,1)S(1)} %copy-done.1, bf16[8,8,16,256]{3,2,1,0:T(8,128)(2,1)S(1)} %collective-permute-done.8.far_ref, bf16[256]{0:T(256)(128)(2,1)S(1)} %copy-done.5, bf16[256]{0:T(256)(128)(2,1)S(1)} %copy-done.6, ...), custom_call_target="tpu_custom_call" | custom-call | tf_op jit(solution)/shard_map/order_bias/pallas_call | solution.py:130
  29.0 8.7 %all-to-all-done = bf16[64,16,256]{2,1,0:T(8,128)(2,1)S(1)} async-done(((bf16[64,16,256]{2,1,0:T(8,128)(2,1)}), bf16[64,16,256]{2,1,0:T(8,128)(2,1)S(1)}, u32[]{:S(2)}, u32[]{:S(2)}) %all-to-all-start) | async-done | bytes 524320 | tf_op jit(solution)/shard_map/all_to_all | solution.py:331
  37.6 4.4 %attend_rows.1 = (bf16[2,4,16,256]{3,2,1,0:T(8,128)(2,1)S(1)}, bf16[2,4,16,256]{3,2,1,0:T(8,128)(2,1)S(1)}, bf16[2,4,16,256]{3,2,1,0:T(8,128)(2,1)S(1)}, bf16[2,...) custom-call(bf16[16,4,16,256]{3,2,1,0:T(8,128)(2,1)S(1)} %bitcast.7,, ...), custom_call_target="tpu_custom_call" | custom-call | tf_op jit(solution)/shard_map/attend_rows/pallas_call | solution.py:249
  42.0 1.2 %collective-permute-start.9 = (bf16[2,4,16,256]{3,2,1,0:T(8,128)(2,1)S(1)}, bf16[2,4,16,256]{3,2,1,0:T(8,128)(2,1)S(1)}, u32[]{:S(2)}, u32[]{:S(2)}) collective-permute-start(bf16[2,4,16,256]{3,2,1,0:T(8,128)(2,1)S(1)} %get-tuple-element.17), channel_id=1, source_target_pairs={{0,4},{1,5},{2,6},{3,7},{4,0},{5,1},{6,2},{7,3},{8,12},{9,13},{10,... | collective-permute-start | bytes 196616 | tf_op jit(solution)/shard_map/ppermute | solution.py:265
  43.2 1.2 %collective-permute-start.10 = (bf16[2,4,16,256]{3,2,1,0:T(8,128)(2,1)S(1)}, bf16[2,4,16,256]{3,2,1,0:T(8,128)(2,1)S(1)}, u32[]{:S(2)}, u32[]{:S(2)}) collective-permute-start(bf16[2,4,16,256]{3,2,1,0:T(8,128)(2,1)S(1)} %get-tuple-element.18), channel_id=1, source_target_pairs={{0,8},{1,9},{2,10},{3,11},{4,12},{5,13},{6,14},{7,15},{8,0},{9,1},... | collective-permute-start | bytes 196616 | tf_op jit(solution)/shard_map/ppermute | solution.py:265
  44.4 2.4 %collective-permute-start.11 = (bf16[2,4,16,256]{3,2,1,0:T(8,128)(2,1)S(1)}, bf16[2,4,16,256]{3,2,1,0:T(8,128)(2,1)S(1)}, u32[]{:S(2)}, u32[]{:S(2)}) collective-permute-start(bf16[2,4,16,256]{3,2,1,0:T(8,128)(2,1)S(1)} %get-tuple-element.19), channel_id=1, source_target_pairs={{0,10},{1,11},{2,8},{3,9},{4,14},{5,15},{6,12},{7,13},{8,2},{9,3},... | collective-permute-start | bytes 196616 | tf_op jit(solution)/shard_map/ppermute | solution.py:265
  46.8 1.0 %collective-permute-start.12 = (bf16[2,4,16,256]{3,2,1,0:T(8,128)(2,1)S(1)}, bf16[2,4,16,256]{3,2,1,0:T(8,128)(2,1)S(1)}, u32[]{:S(2)}, u32[]{:S(2)}) collective-permute-start(bf16[2,4,16,256]{3,2,1,0:T(8,128)(2,1)S(1)} %get-tuple-element.20), channel_id=1, source_target_pairs={{0,12},{1,13},{2,14},{3,15},{4,8},{5,9},{6,10},{7,11},{8,4},{9,5},... | collective-permute-start | bytes 196616 | tf_op jit(solution)/shard_map/ppermute | solution.py:265
  47.8 3.0 %collective-permute-start.13 = (bf16[2,4,16,256]{3,2,1,0:T(8,128)(2,1)S(1)}, bf16[2,4,16,256]{3,2,1,0:T(8,128)(2,1)S(1)}, u32[]{:S(2)}, u32[]{:S(2)}) collective-permute-start(bf16[2,4,16,256]{3,2,1,0:T(8,128)(2,1)S(1)} %get-tuple-element.21), channel_id=1, source_target_pairs={{0,14},{1,15},{2,12},{3,13},{4,10},{5,11},{6,8},{7,9},{8,6},{9,7},... | collective-permute-start | bytes 196616 | tf_op jit(solution)/shard_map/ppermute | solution.py:265
  50.8 0.0 collective-permute-done.9.refs_0_
  50.8 0.0 collective-permute-start.14
  50.8 1.1 %collective-permute-done.10.refs_1_ = bf16[2,4,16,256]{3,2,1,0:T(8,128)(2,1)S(1)} collective-permute-done((bf16[2,4,16,256]{3,2,1,0:T(8,128)(2,1)S(1)}, bf16[2,4,16,256]{3,2,1,0:T(8,128)(2,1)S(1)}, u32[]{:S(2)}, u32[]{:S(2)}) %collective-permute-start.10) | collective-permute-done | bytes 65568 | tf_op jit(solution)/shard_map/ppermute | solution.py:265
  51.9 0.2 collective-permute-start.15
  52.2 3.8 %collective-permute-done.11.refs_2_ = bf16[2,4,16,256]{3,2,1,0:T(8,128)(2,1)S(1)} collective-permute-done((bf16[2,4,16,256]{3,2,1,0:T(8,128)(2,1)S(1)}, bf16[2,4,16,256]{3,2,1,0:T(8,128)(2,1)S(1)}, u32[]{:S(2)}, u32[]{:S(2)}) %collective-permute-start.11) | collective-permute-done | bytes 65568 | tf_op jit(solution)/shard_map/ppermute | solution.py:265
  56.0 1.3 %collective-permute-done.14.refs_5_ = bf16[2,4,16,256]{3,2,1,0:T(8,128)(2,1)S(1)} collective-permute-done((bf16[2,4,16,256]{3,2,1,0:T(8,128)(2,1)S(1)}, bf16[2,4,16,256]{3,2,1,0:T(8,128)(2,1)S(1)}, u32[]{:S(2)}, u32[]{:S(2)}) %collective-permute-start.14) | collective-permute-done | bytes 65568 | tf_op jit(solution)/shard_map/ppermute | solution.py:265
  57.3 1.3 %collective-permute-done.15.refs_6_ = bf16[2,4,16,256]{3,2,1,0:T(8,128)(2,1)S(1)} collective-permute-done((bf16[2,4,16,256]{3,2,1,0:T(8,128)(2,1)S(1)}, bf16[2,4,16,256]{3,2,1,0:T(8,128)(2,1)S(1)}, u32[]{:S(2)}, u32[]{:S(2)}) %collective-permute-start.15) | collective-permute-done | bytes 65568 | tf_op jit(solution)/shard_map/ppermute | solution.py:265
  58.6 0.1 collective-permute-start.16
  58.7 1.5 %collective-permute-done.16.refs_8_ = bf16[8,4,16,256]{3,2,1,0:T(8,128)(2,1)S(1)} collective-permute-done((bf16[8,4,16,256]{3,2,1,0:T(8,128)(2,1)S(1)}, bf16[8,4,16,256]{3,2,1,0:T(8,128)(2,1)S(1)}, u32[]{:S(2)}, u32[]{:S(2)}) %collective-permute-start.16) | collective-permute-done | bytes 262176 | tf_op jit(solution)/shard_map/ppermute | solution.py:265
  60.2 0.9 %place_rows.1 = bf16[64,16,256]{2,1,0:T(8,128)(2,1)} custom-call(bf16[2,4,16,256]{3,2,1,0:T(8,128)(2,1)S(1)} %collective-permute-done.9.refs_0_, bf16[2,4,16,256]{3,2,1,0:T(8,128)(2,1)S(1)} %collective-permute-done.10.refs_1_, bf16[2,4,16,256]{3,2,1,0:T(8,128)(2,1)S(1)} %collective-permute-done.11.refs_2_, ...), custom_call_target="tpu_custom_call" | custom-call | tf_op jit(solution)/shard_map/place_rows/pallas_call | solution.py:294
  (32 shorter events, 0.1 us)
Async XLA Ops:
  0.0 15.2 %copy-start.3 = (bf16[64,16,256]{2,1,0:T(8,128)(2,1)S(1)}, bf16[64,16,256]{2,1,0:T(8,128)(2,1)}, u32[]{:S(2)}) copy-start(bf16[64,16,256]{2,1,0:T(8,128)(2,1)} %refs_0_.2) | copy-start | bytes 1572868
  0.0 15.2 %copy-start.4 = (s32[6,64]{1,0:T(8,128)S(1)}, s32[6,64]{1,0:T(8,128)}, u32[]{:S(2)}) copy-start(s32[6,64]{1,0:T(8,128)} %pairs_ref.1) | copy-start | bytes 4612
  0.0 15.2 %copy-start.9 = (s32[6]{0:T(128)S(1)}, s32[6]{0:T(128)}, u32[]{:S(2)}) copy-start(s32[6]{0:T(128)} %first_ref.1) | copy-start | bytes 76
  0.0 15.2 %copy-start.10 = (bf16[256]{0:T(256)(128)(2,1)S(1)}, bf16[256]{0:T(256)(128)(2,1)}, u32[]{:S(2)}) copy-start(bf16[256]{0:T(256)(128)(2,1)} %gap_ref.1) | copy-start | bytes 1540
  0.0 15.1 %collective-permute-start = (bf16[64,16,256]{2,1,0:T(8,128)(2,1)}, bf16[64,16,256]{2,1,0:T(8,128)(2,1)S(1)}, u32[]{:S(2)}, u32[]{:S(2)}) collective-permute-start(bf16[64,16,256]{2,1,0:T(8,128)(2,1)} %refs_0_.2), channel_id=1, source_target_pairs={{0,16},{16,0},{1,17},{17,1},{2,18},{18,2},{3,19},{19,3},{4,20},{20... | collective-permute-start | bytes 1572872 | tf_op jit(solution)/shard_map/ppermute | solution.py:325
  3.0 8.2 %collective-permute-start.1 = (bf16[1,8,16,256]{3,2,1,0:T(8,128)(2,1)}, bf16[1,8,16,256]{3,2,1,0:T(8,128)(2,1)S(1)}, u32[]{:S(2)}, u32[]{:S(2)}) collective-permute-start(bf16[1,8,16,256]{3,2,1,0:T(8,128)(2,1)} %bitcast.10), channel_id=1, source_target_pairs={{0,8},{1,9},{2,10},{3,11},{4,12},{5,13},{6,14},{7,15},{8,0},{9,1},... | collective-permute-start | bytes 196616 | tf_op jit(solution)/shard_map/ppermute | solution.py:107
  5.6 6.2 %collective-permute-start.2 = (bf16[1,8,16,256]{3,2,1,0:T(8,128)(2,1)}, bf16[1,8,16,256]{3,2,1,0:T(8,128)(2,1)S(1)}, u32[]{:S(2)}, u32[]{:S(2)}) collective-permute-start(bf16[1,8,16,256]{3,2,1,0:T(8,128)(2,1)} %bitcast.11), channel_id=1, source_target_pairs={{0,4},{1,5},{2,6},{3,7},{4,0},{5,1},{6,2},{7,3},{8,12},{9,13},{10,... | collective-permute-start | bytes 196616 | tf_op jit(solution)/shard_map/ppermute | solution.py:107
  7.2 6.3 %collective-permute-start.3 = (bf16[1,8,16,256]{3,2,1,0:T(8,128)(2,1)}, bf16[1,8,16,256]{3,2,1,0:T(8,128)(2,1)S(1)}, u32[]{:S(2)}, u32[]{:S(2)}) collective-permute-start(bf16[1,8,16,256]{3,2,1,0:T(8,128)(2,1)} %bitcast.12), channel_id=1, source_target_pairs={{0,12},{1,13},{2,14},{3,15},{4,8},{5,9},{6,10},{7,11},{8,4},{9,5},... | collective-permute-start | bytes 196616 | tf_op jit(solution)/shard_map/ppermute | solution.py:107
  7.4 15.8 %collective-permute-start.4 = (bf16[1,8,16,256]{3,2,1,0:T(8,128)(2,1)}, bf16[1,8,16,256]{3,2,1,0:T(8,128)(2,1)S(1)}, u32[]{:S(2)}, u32[]{:S(2)}) collective-permute-start(bf16[1,8,16,256]{3,2,1,0:T(8,128)(2,1)} %bitcast.13), channel_id=1, source_target_pairs={{0,2},{1,3},{2,0},{3,1},{4,6},{5,7},{6,4},{7,5},{8,10},{9,11},{10,... | collective-permute-start | bytes 196616 | tf_op jit(solution)/shard_map/ppermute | solution.py:107
  11.2 14.1 %copy-start.2 = (bf16[256,256]{1,0:T(8,128)(2,1)S(1)}, bf16[256,256]{1,0:T(8,128)(2,1)}, u32[]{:S(2)}) copy-start(bf16[256,256]{1,0:T(8,128)(2,1)} %out_weight_ref.1) | copy-start | bytes 393220
  11.2 14.1 %copy-start.5 = (bf16[256]{0:T(256)(128)(2,1)S(1)}, bf16[256]{0:T(256)(128)(2,1)}, u32[]{:S(2)}) copy-start(bf16[256]{0:T(256)(128)(2,1)} %refs_0_.3) | copy-start | bytes 1540
  11.2 14.1 %copy-start.6 = (bf16[256]{0:T(256)(128)(2,1)S(1)}, bf16[256]{0:T(256)(128)(2,1)}, u32[]{:S(2)}) copy-start(bf16[256]{0:T(256)(128)(2,1)} %refs_1_.1) | copy-start | bytes 1540
  11.2 12.0 %collective-permute-start.5 = (bf16[1,8,16,256]{3,2,1,0:T(8,128)(2,1)S(1)}, bf16[1,8,16,256]{3,2,1,0:T(8,128)(2,1)S(1)}, u32[]{:S(2)}, u32[]{:S(2)}) collective-permute-start(bf16[1,8,16,256]{3,2,1,0:T(8,128)(2,1)S(1)} %collective-permute-done.1), channel_id=1, source_target_pairs={{0,2},{1,3},{2,0},{3,1},{4,6},{5,7},{6,4},{7,5},{8,10},{9,11},{10,... | collective-permute-start | bytes 196616 | tf_op jit(solution)/shard_map/ppermute | solution.py:107
  11.8 11.4 %collective-permute-start.6 = (bf16[1,8,16,256]{3,2,1,0:T(8,128)(2,1)S(1)}, bf16[1,8,16,256]{3,2,1,0:T(8,128)(2,1)S(1)}, u32[]{:S(2)}, u32[]{:S(2)}) collective-permute-start(bf16[1,8,16,256]{3,2,1,0:T(8,128)(2,1)S(1)} %collective-permute-done.2), channel_id=1, source_target_pairs={{0,2},{1,3},{2,0},{3,1},{4,6},{5,7},{6,4},{7,5},{8,10},{9,11},{10,... | collective-permute-start | bytes 196616 | tf_op jit(solution)/shard_map/ppermute | solution.py:107
  13.5 9.8 %collective-permute-start.7 = (bf16[1,8,16,256]{3,2,1,0:T(8,128)(2,1)S(1)}, bf16[1,8,16,256]{3,2,1,0:T(8,128)(2,1)S(1)}, u32[]{:S(2)}, u32[]{:S(2)}) collective-permute-start(bf16[1,8,16,256]{3,2,1,0:T(8,128)(2,1)S(1)} %collective-permute-done.3), channel_id=1, source_target_pairs={{0,2},{1,3},{2,0},{3,1},{4,6},{5,7},{6,4},{7,5},{8,10},{9,11},{10,... | collective-permute-start | bytes 196616 | tf_op jit(solution)/shard_map/ppermute | solution.py:107
  17.0 20.7 %all-to-all-start = ((bf16[64,16,256]{2,1,0:T(8,128)(2,1)}), bf16[64,16,256]{2,1,0:T(8,128)(2,1)S(1)}, u32[]{:S(2)}, u32[]{:S(2)}) async-start(bf16[64,16,256]{2,1,0:T(8,128)(2,1)} %pick_joint.1), calls=%async_computation | async-start | bytes 1048576 | tf_op jit(solution)/shard_map/all_to_all | solution.py:331
  23.3 2.0 %collective-permute-start.8 = (bf16[8,8,16,256]{3,2,1,0:T(8,128)(2,1)S(1)}, bf16[8,8,16,256]{3,2,1,0:T(8,128)(2,1)S(1)}, u32[]{:S(2)}, u32[]{:S(2)}) collective-permute-start(bf16[8,8,16,256]{3,2,1,0:T(8,128)(2,1)S(1)} %constant_dynamic-update-slice_fusion.near_ref), channel_id=1, source_target_pairs={{0,1},{1,0},{2,3},{3,2},{4,5},{5,4},{6,7},{7,6},{8,9},{9,8},{10,11... | collective-permute-start | bytes 1572872 | tf_op jit(solution)/shard_map/ppermute | solution.py:107
  23.7 0.8 %copy-start = (bf16[8,8,16,256]{3,2,1,0:T(8,128)(2,1)}, bf16[8,8,16,256]{3,2,1,0:T(8,128)(2,1)S(1)}, u32[]{:S(2)}) copy-start(bf16[8,8,16,256]{3,2,1,0:T(8,128)(2,1)S(1)} %constant_dynamic-update-slice_fusion.near_ref) | copy-start | bytes 1572868
  25.3 1.0 %copy-start.1 = (bf16[8,8,16,256]{3,2,1,0:T(8,128)(2,1)S(1)}, bf16[8,8,16,256]{3,2,1,0:T(8,128)(2,1)}, u32[]{:S(2)}) copy-start(bf16[8,8,16,256]{3,2,1,0:T(8,128)(2,1)} %copy-done) | copy-start | bytes 1572868
  26.3 0.7 %copy-start.7 = (bf16[256]{0:T(256)(128)(2,1)S(1)}, bf16[256]{0:T(256)(128)(2,1)}, u32[]{:S(2)}) copy-start(bf16[256]{0:T(256)(128)(2,1)} %refs_2_.1) | copy-start | bytes 1540
  27.0 0.7 %copy-start.8 = (bf16[256]{0:T(256)(128)(2,1)S(1)}, bf16[256]{0:T(256)(128)(2,1)}, u32[]{:S(2)}) copy-start(bf16[256]{0:T(256)(128)(2,1)} %refs_3_.1) | copy-start | bytes 1540
  42.0 8.8 %collective-permute-start.9 = (bf16[2,4,16,256]{3,2,1,0:T(8,128)(2,1)S(1)}, bf16[2,4,16,256]{3,2,1,0:T(8,128)(2,1)S(1)}, u32[]{:S(2)}, u32[]{:S(2)}) collective-permute-start(bf16[2,4,16,256]{3,2,1,0:T(8,128)(2,1)S(1)} %get-tuple-element.17), channel_id=1, source_target_pairs={{0,4},{1,5},{2,6},{3,7},{4,0},{5,1},{6,2},{7,3},{8,12},{9,13},{10,... | collective-permute-start | bytes 196616 | tf_op jit(solution)/shard_map/ppermute | solution.py:265
  43.2 8.8 %collective-permute-start.10 = (bf16[2,4,16,256]{3,2,1,0:T(8,128)(2,1)S(1)}, bf16[2,4,16,256]{3,2,1,0:T(8,128)(2,1)S(1)}, u32[]{:S(2)}, u32[]{:S(2)}) collective-permute-start(bf16[2,4,16,256]{3,2,1,0:T(8,128)(2,1)S(1)} %get-tuple-element.18), channel_id=1, source_target_pairs={{0,8},{1,9},{2,10},{3,11},{4,12},{5,13},{6,14},{7,15},{8,0},{9,1},... | collective-permute-start | bytes 196616 | tf_op jit(solution)/shard_map/ppermute | solution.py:265
  44.4 11.6 %collective-permute-start.11 = (bf16[2,4,16,256]{3,2,1,0:T(8,128)(2,1)S(1)}, bf16[2,4,16,256]{3,2,1,0:T(8,128)(2,1)S(1)}, u32[]{:S(2)}, u32[]{:S(2)}) collective-permute-start(bf16[2,4,16,256]{3,2,1,0:T(8,128)(2,1)S(1)} %get-tuple-element.19), channel_id=1, source_target_pairs={{0,10},{1,11},{2,8},{3,9},{4,14},{5,15},{6,12},{7,13},{8,2},{9,3},... | collective-permute-start | bytes 196616 | tf_op jit(solution)/shard_map/ppermute | solution.py:265
  46.8 9.2 %collective-permute-start.12 = (bf16[2,4,16,256]{3,2,1,0:T(8,128)(2,1)S(1)}, bf16[2,4,16,256]{3,2,1,0:T(8,128)(2,1)S(1)}, u32[]{:S(2)}, u32[]{:S(2)}) collective-permute-start(bf16[2,4,16,256]{3,2,1,0:T(8,128)(2,1)S(1)} %get-tuple-element.20), channel_id=1, source_target_pairs={{0,12},{1,13},{2,14},{3,15},{4,8},{5,9},{6,10},{7,11},{8,4},{9,5},... | collective-permute-start | bytes 196616 | tf_op jit(solution)/shard_map/ppermute | solution.py:265
  47.8 8.2 %collective-permute-start.13 = (bf16[2,4,16,256]{3,2,1,0:T(8,128)(2,1)S(1)}, bf16[2,4,16,256]{3,2,1,0:T(8,128)(2,1)S(1)}, u32[]{:S(2)}, u32[]{:S(2)}) collective-permute-start(bf16[2,4,16,256]{3,2,1,0:T(8,128)(2,1)S(1)} %get-tuple-element.21), channel_id=1, source_target_pairs={{0,14},{1,15},{2,12},{3,13},{4,10},{5,11},{6,8},{7,9},{8,6},{9,7},... | collective-permute-start | bytes 196616 | tf_op jit(solution)/shard_map/ppermute | solution.py:265
  50.8 6.4 %collective-permute-start.14 = (bf16[2,4,16,256]{3,2,1,0:T(8,128)(2,1)S(1)}, bf16[2,4,16,256]{3,2,1,0:T(8,128)(2,1)S(1)}, u32[]{:S(2)}, u32[]{:S(2)}) collective-permute-start(bf16[2,4,16,256]{3,2,1,0:T(8,128)(2,1)S(1)} %get-tuple-element.22), channel_id=1, source_target_pairs={{0,6},{1,7},{2,4},{3,5},{4,2},{5,3},{6,0},{7,1},{8,14},{9,15},{10,... | collective-permute-start | bytes 196616 | tf_op jit(solution)/shard_map/ppermute | solution.py:265
  51.9 6.6 %collective-permute-start.15 = (bf16[2,4,16,256]{3,2,1,0:T(8,128)(2,1)S(1)}, bf16[2,4,16,256]{3,2,1,0:T(8,128)(2,1)S(1)}, u32[]{:S(2)}, u32[]{:S(2)}) collective-permute-start(bf16[2,4,16,256]{3,2,1,0:T(8,128)(2,1)S(1)} %get-tuple-element.23), channel_id=1, source_target_pairs={{0,2},{1,3},{2,0},{3,1},{4,6},{5,7},{6,4},{7,5},{8,10},{9,11},{10,... | collective-permute-start | bytes 196616 | tf_op jit(solution)/shard_map/ppermute | solution.py:265
  58.6 1.6 %collective-permute-start.16 = (bf16[8,4,16,256]{3,2,1,0:T(8,128)(2,1)S(1)}, bf16[8,4,16,256]{3,2,1,0:T(8,128)(2,1)S(1)}, u32[]{:S(2)}, u32[]{:S(2)}) collective-permute-start(bf16[8,4,16,256]{3,2,1,0:T(8,128)(2,1)S(1)} %constant_dynamic-update-slice_fusion.8), channel_id=1, source_target_pairs={{0,1},{1,0},{2,3},{3,2},{4,5},{5,4},{6,7},{7,6},{8,9},{9,8},{10,11... | collective-permute-start | bytes 786440 | tf_op jit(solution)/shard_map/ppermute | solution.py:265

commit v5 on v3

--- a/solution.py
+++ b/solution.py
@@ -1,5 +1,4 @@
 import functools
-import math
 
 import jax
 import jax.numpy as jnp
@@ -9,11 +8,10 @@
 from jax.sharding import PartitionSpec as P
 
 norm_eps = 1e-05
-log2e = math.log2(math.e)
 cores = 2
 
 
-def pick_kernel(owners, first_row, pairs_ref, first_ref, gap_ref, *refs):
+def pick_kernel(owners, pairs_ref, first_ref, gap_ref, *refs):
     blocks, (out_ref, held, sems) = refs[:owners], refs[-3:]
     local_rows, local_columns, channels = blocks[0].shape
     part_rows = out_ref.shape[0]
@@ -42,34 +40,29 @@
             found = jnp.where(owner == names[k], blocks[k][within].astype(jnp.float32), found)
         return jnp.where(row >= 0, found, gap)
 
-    def one_row(s, carry):
-        row = first_row + s
-        picked = jnp.where(in_high, cells(pairs_ref[high, row]), cells(pairs_ref[low, row]))
-        held[s] = picked.astype(jnp.bfloat16)
-        return carry
-
     copies = []
     for k in range(pieces):
         rows = pl.ds(k * piece_rows, piece_rows)
-        lax.fori_loop(k * piece_rows, (k + 1) * piece_rows, one_row, 0, unroll=piece_rows)
+        for row in range(k * piece_rows, (k + 1) * piece_rows):
+            both = jnp.where(in_high, cells(pairs_ref[high, row]), cells(pairs_ref[low, row]))
+            held[row] = both.astype(jnp.bfloat16)
         copies.append(pltpu.make_async_copy(held.at[rows], out_ref.at[rows], sems.at[k]))
         copies[-1].start()
     for copy in copies:
         copy.wait()
 
 
-def pick(part, parts, pairs, chain_first_residue, gap, blocks, earlier):
+def pick(pairs, chain_first_residue, gap, blocks, earlier):
     owners = len(blocks)
     local_rows, local_columns, channels = blocks[0].shape
-    part_rows = local_rows // parts
-    pieces = part_rows // 16
+    pieces = 2
     smem = pl.BlockSpec(memory_space=pltpu.SMEM)
     vmem = pl.BlockSpec(memory_space=pltpu.VMEM)
     anywhere = pl.BlockSpec(memory_space=pl.ANY)
     block_bytes = local_rows * local_columns * channels * 2
-    shape = (part_rows, local_columns, channels)
-    return pl.pallas_call(
-        functools.partial(pick_kernel, owners, part * part_rows),
+    shape = blocks[0].shape
+    return pl.pallas_call(
+        functools.partial(pick_kernel, owners),
         out_shape=jax.ShapeDtypeStruct(shape, jnp.bfloat16),
         in_specs=[smem, smem, vmem] + [vmem] * owners + [anywhere] * len(earlier),
         out_specs=anywhere,
@@ -89,7 +82,7 @@
         held[:, pl.ds(first, block), :] = source[place % half].astype(jnp.float32)
 
     def one_head(h, carry):
-        out_ref[h] = held[h].T * log2e
+        out_ref[h] = held[h].T
         return carry
 
     lax.fori_loop(0, heads, one_head, 0)
@@ -168,7 +161,7 @@
 
 
 def attend_kernel(cells_ref, weights_ref, out_weight_ref, vectors_ref, bias_ref, *refs):
-    out_refs, (staged_ref, scores_ref) = refs[:-2], refs[-2:]
+    near_refs, far_refs, (staged_ref, scores_ref) = refs[:2], refs[2:-2], refs[-2:]
     senders, rows, block, channels = cells_ref.shape
     me = lax.axis_index("res")
     residues = senders * block
@@ -194,7 +187,7 @@
             weights_ref[: 3 * width], normed, (((1,), (1,)), ((), ())),
             preferred_element_type=jnp.float32,
         )
-        queries = (rest[:width] * (depth**-0.5 * log2e)).astype(jnp.bfloat16)
+        queries = (rest[:width] * depth**-0.5).astype(jnp.bfloat16)
         values = rest[width : 2 * width].astype(jnp.bfloat16)
         keys = keys.astype(jnp.bfloat16)
         for k in range(width // group):
@@ -212,7 +205,7 @@
         first = low % group // depth * residues
         scores = scores_ref[r % 2, low // group, first : first + residues] + bias_ref[h]
         highest = jnp.max(scores, axis=0, keepdims=True)
-        lifted = jnp.exp2(scores - highest).astype(jnp.bfloat16)
+        lifted = jnp.exp(scores - highest).astype(jnp.bfloat16)
         left = jnp.concatenate([values[low:high], ones], axis=0)
         summed = jnp.dot(left, lifted, preferred_element_type=jnp.float32)
         inverse = 1.0 / summed[depth : depth + 1]
@@ -224,7 +217,11 @@
         update = (update + vectors_ref[2:3]).astype(jnp.bfloat16)
         staged_ref[...] = update.reshape(senders, block, channels)
         for flip in range(senders):
-            out_refs[flip // cores][flip % cores, r] = staged_ref[me ^ flip]
+            chip, core = flip // cores, flip % cores
+            if chip < 4:
+                near_refs[chip // 2][chip % 2, core, r] = staged_ref[me ^ flip]
+            else:
+                far_refs[chip - 4][core, r] = staged_ref[me ^ flip]
 
     begun = {0: begin(0)}
     done = {r: [] for r in range(rows)}
@@ -245,12 +242,13 @@
     group = min(128, width)
     vmem = pl.BlockSpec(memory_space=pltpu.VMEM)
     score_shape = (2, width // group, heads * group // width * residues, residues)
-    piece = jax.ShapeDtypeStruct((cores, rows, block, channels), jnp.bfloat16)
+    one = (cores, rows, block, channels)
+    shapes = [(2, *one)] * 2 + [one] * (senders // cores - 4)
     return pl.pallas_call(
         attend_kernel,
-        out_shape=[piece] * (senders // cores),
+        out_shape=[jax.ShapeDtypeStruct(shape, jnp.bfloat16) for shape in shapes],
         in_specs=[vmem] * 5,
-        out_specs=[vmem] * (senders // cores),
+        out_specs=[vmem] * len(shapes),
         scratch_shapes=[
             pltpu.VMEM((senders, block, channels), jnp.bfloat16),
             pltpu.VMEM(score_shape, jnp.float32),
@@ -266,19 +264,27 @@
 
 
 def spread(pieces):
-    half = len(pieces) // 2
-    order = [1, *range(half, len(pieces)), *range(2, half), 0]
-    arrived = [swap(pieces[chip], chip * cores) if chip else pieces[0] for chip in order]
-    return order, arrived, swap(jnp.stack([piece[1] for piece in arrived]), 1)
+    here, there, far = pieces[0], pieces[1], pieces[2:]
+    far = [swap(piece, (4 + k) * cores) for k, piece in enumerate(far)]
+    there = swap(there, 2 * cores)
+    hop = swap(jnp.stack([here[1], there[1]]), cores)
+    middle = len(far) // 2
+    arrived = [(4 + k, far[k]) for k in range(middle)] + [(2, there[0])]
+    arrived += [(4 + k, far[k]) for k in range(middle, len(far))]
+    arrived += [(1, hop[0]), (3, hop[1]), (0, here[0])]
+    other = swap(jnp.stack([blocks[1] for _, blocks in arrived]), 1)
+    return [chip for chip, _ in arrived], far, there, hop, here, other
 
 
 def place_kernel(order, *refs):
-    piece_refs, (other_ref, out_ref, sems) = refs[:-3], refs[-3:]
+    far_refs, (there_ref, hop_ref, here_ref, other_ref, out_ref, sems) = refs[:-6], refs[-6:]
     me = lax.axis_index("res")
     rows = other_ref.shape[1]
+    near = [here_ref.at[0, 0], hop_ref.at[0, 0], there_ref.at[0, 0], hop_ref.at[1, 0]]
     copies = []
     for k, chip in enumerate(order):
-        for core, source in enumerate((piece_refs[k].at[0], other_ref.at[k])):
+        same = near[chip] if chip < 4 else far_refs[chip - 4].at[0]
+        for core, source in enumerate((same, other_ref.at[k])):
             first = (me ^ (chip * cores + core)) * rows
             target = out_ref.at[pl.ds(first, rows)]
             copies.append(pltpu.make_async_copy(source, target, sems.at[len(copies)]))
@@ -288,17 +294,17 @@
         copy.wait()
 
 
-def place(order, pieces, other, shape):
+def place(order, far, there, hop, here, other, shape):
     vmem = pl.BlockSpec(memory_space=pltpu.VMEM)
     return pl.pallas_call(
         functools.partial(place_kernel, order),
         out_shape=jax.ShapeDtypeStruct(shape, jnp.bfloat16),
-        in_specs=[vmem] * (len(pieces) + 1),
+        in_specs=[vmem] * (len(far) + 4),
         out_specs=pl.BlockSpec(memory_space=pl.ANY),
-        scratch_shapes=[pltpu.SemaphoreType.DMA((cores * len(pieces),))],
+        scratch_shapes=[pltpu.SemaphoreType.DMA((cores * len(order),))],
         compiler_params=pltpu.CompilerParams(vmem_limit_bytes=8 << 20),
         name="place_rows",
-    )(*pieces, other)
+    )(*far, there, hop, here, other)
 
 
 def local(
@@ -326,7 +332,7 @@
             )
         )
     weights = turn_weights(projection_weight)
-    joint = pick(0, 1, pairs, chain_first_residue, gap_embedding, blocks, (weights,))
+    joint = pick(pairs, chain_first_residue, gap_embedding, blocks, (weights,))
     cells = lax.all_to_all(joint, "res", split_axis=0, concat_axis=0, tiled=True)
     bias, vectors = order_bias(
         near,
@@ -336,8 +342,8 @@
         (weights, output_weight),
     )
     cells = cells.reshape(members, local_rows // members, local_columns, channels)
-    arrived = spread(attend(cells, weights, output_weight, vectors, bias))
-    return place(*arrived, (local_rows, local_columns, channels))
+    pieces = attend(cells, weights, output_weight, vectors, bias)
+    return place(*spread(pieces), (local_rows, local_columns, channels))
 
 
 def solution(mesh):

time: 61.4 us -> 61.2 us (level)
  waiting for transfers between devices: 17.8 us -> 16.7 us
  starting transfers between devices: 29 us -> 29.8 us
    ppermute x8 -> x7, waiting for transfers between devices: 8.14 us -> 7 us  [swap(): return lax.ppermute(array, 'res', [(i, i ^ flip) for i in range(members)])]
    ppermute x8 -> x7, starting transfers between devices: 9.85 us -> 10.6 us  [swap(): return lax.ppermute(array, 'res', [(i, i ^ flip) for i in range(members)])]
  transfers between devices with their start and end apart: 18 -> 17, of which waited for: 8 -> 10; matrix products, arithmetic and copies ran while one was open for 3% -> 3% of each run, Pallas kernels for 5% -> 5%
where the time goes in v5:
time: 61.2 us; the launch traced here: 60.8 us
  starting transfers between devices  29.8 us (49%)
  waiting for transfers between devices  16.7 us (27%)
  Pallas kernels  8.77 us (14%)
  local copies, waits for them, and re-layouts  5.3 us (9%)
    ppermute x7, starting transfers between devices, swap(): return lax.ppermute(array, 'res', [(i, i ^ flip) for i in range(members)])  10.6 us
    ppermute x8, starting transfers between devices, swap(): return lax.ppermute(piece, 'res', [(i, i ^ flip) for i in range(members)])  9.99 us
    all_to_all x1, waiting for transfers between devices, local(): lax.all_to_all(joint, 'res', split_axis=0, concat_axis=0, tiled=True)  8.69 us
    ppermute x7, waiting for transfers between devices, swap(): return lax.ppermute(array, 'res', [(i, i ^ flip) for i in range(members)])  7 us
    all_to_all x1, starting transfers between devices, local(): lax.all_to_all(joint, 'res', split_axis=0, concat_axis=0, tiled=True)  6.2 us
    unnamed x37, local copies, waits for them, and re-layouts  5.28 us
    pallas_call x1, Pallas kernels, attend(): pl.pallas_call(attend_kernel, out_shape=[jax.ShapeDtypeStruct(shape, jnp....  4.53 us
    ppermute x1, starting transfers between devices, local(): lax.ppermute(source_alignment_rows, 'rows', [(i, (i + hop) % owners) for...  3.01 us
  transfers between devices with their start and end apart: 17, of which 10 were waited for; matrix products, arithmetic and copies ran while one was open for 3% of the time, Pallas kernels for 5%

profile of v5, /device:TPU:0, one launch (start us, length us, event | category | flops | bytes accessed | tf_op | source)
XLA Modules:
  0.0 60.8 jit_solution(16275210557984687235)
XLA Ops:
  0.0 3.0 %collective-permute-start = (bf16[64,16,256]{2,1,0:T(8,128)(2,1)}, bf16[64,16,256]{2,1,0:T(8,128)(2,1)S(1)}, u32[]{:S(2)}, u32[]{:S(2)}) collective-permute-start(bf16[64,16,256]{2,1,0:T(8,128)(2,1)} %refs_0_.2), channel_id=1, source_target_pairs={{0,16},{16,0},{1,17},{17,1},{2,18},{18,2},{3,19},{19,3},{4,20},{20... | collective-permute-start | bytes 1572872 | tf_op jit(solution)/shard_map/ppermute | solution.py:330
  3.0 2.6 %collective-permute-start.1 = (bf16[1,8,16,256]{3,2,1,0:T(8,128)(2,1)}, bf16[1,8,16,256]{3,2,1,0:T(8,128)(2,1)S(1)}, u32[]{:S(2)}, u32[]{:S(2)}) collective-permute-start(bf16[1,8,16,256]{3,2,1,0:T(8,128)(2,1)} %bitcast.24), channel_id=1, source_target_pairs={{0,8},{1,9},{2,10},{3,11},{4,12},{5,13},{6,14},{7,15},{8,0},{9,1},... | collective-permute-start | bytes 196616 | tf_op jit(solution)/shard_map/ppermute | solution.py:100
  5.6 1.6 %collective-permute-start.2 = (bf16[1,8,16,256]{3,2,1,0:T(8,128)(2,1)}, bf16[1,8,16,256]{3,2,1,0:T(8,128)(2,1)S(1)}, u32[]{:S(2)}, u32[]{:S(2)}) collective-permute-start(bf16[1,8,16,256]{3,2,1,0:T(8,128)(2,1)} %bitcast.25), channel_id=1, source_target_pairs={{0,4},{1,5},{2,6},{3,7},{4,0},{5,1},{6,2},{7,3},{8,12},{9,13},{10,... | collective-permute-start | bytes 196616 | tf_op jit(solution)/shard_map/ppermute | solution.py:100
  7.2 0.2 collective-permute-start.3
  7.4 1.5 %collective-permute-start.4 = (bf16[1,8,16,256]{3,2,1,0:T(8,128)(2,1)}, bf16[1,8,16,256]{3,2,1,0:T(8,128)(2,1)S(1)}, u32[]{:S(2)}, u32[]{:S(2)}) collective-permute-start(bf16[1,8,16,256]{3,2,1,0:T(8,128)(2,1)} %bitcast.27), channel_id=1, source_target_pairs={{0,2},{1,3},{2,0},{3,1},{4,6},{5,7},{6,4},{7,5},{8,10},{9,11},{10,... | collective-permute-start | bytes 196616 | tf_op jit(solution)/shard_map/ppermute | solution.py:100
  8.9 0.9 %constant_dynamic-update-slice_fusion.7 = bf16[8,8,16,256]{3,2,1,0:T(8,128)(2,1)S(1)} fusion(bf16[8,16,256]{2,1,0:T(8,128)(2,1)} %param.19), kind=kLoop, calls=%fused_computation.9 | loop fusion | bytes 131072
  9.8 1.1 %copy.14 = bf16[32,8,8,128]{3,1,2,0:T(8,128)(2,1)S(1)} copy(bf16[32,8,8,128]{3,2,1,0:T(8,128)(2,1)} %bitcast.23) | data formatting | bytes 1048576
  10.9 0.2 turn_weights.1.refs_2_.refs_4_.weights_ref
  11.2 0.0 copy-start.2
  11.2 0.0 copy-start.5
  11.2 0.0 copy-start.6
  11.2 0.0 collective-permute-done.1
  11.2 0.6 collective-permute-start.5
  11.8 0.0 collective-permute-done.2
  11.8 1.5 %collective-permute-start.6 = (bf16[1,8,16,256]{3,2,1,0:T(8,128)(2,1)S(1)}, bf16[1,8,16,256]{3,2,1,0:T(8,128)(2,1)S(1)}, u32[]{:S(2)}, u32[]{:S(2)}) collective-permute-start(bf16[1,8,16,256]{3,2,1,0:T(8,128)(2,1)S(1)} %collective-permute-done.2), channel_id=1, source_target_pairs={{0,2},{1,3},{2,0},{3,1},{4,6},{5,7},{6,4},{7,5},{8,10},{9,11},{10,... | collective-permute-start | bytes 196616 | tf_op jit(solution)/shard_map/ppermute | solution.py:100
  13.3 0.1 collective-permute-done.3
  13.5 1.5 %collective-permute-start.7 = (bf16[1,8,16,256]{3,2,1,0:T(8,128)(2,1)S(1)}, bf16[1,8,16,256]{3,2,1,0:T(8,128)(2,1)S(1)}, u32[]{:S(2)}, u32[]{:S(2)}) collective-permute-start(bf16[1,8,16,256]{3,2,1,0:T(8,128)(2,1)S(1)} %collective-permute-done.3), channel_id=1, source_target_pairs={{0,2},{1,3},{2,0},{3,1},{4,6},{5,7},{6,4},{7,5},{8,10},{9,11},{10,... | collective-permute-start | bytes 196616 | tf_op jit(solution)/shard_map/ppermute | solution.py:100
  15.0 0.2 collective-permute-done.refs_1_
  15.2 1.8 %pick_joint.1 = bf16[64,16,256]{2,1,0:T(8,128)(2,1)} custom-call(s32[6,64]{1,0:T(8,128)S(1)} %copy-done.4, s32[6]{0:T(128)S(1)} %copy-done.9, bf16[256]{0:T(256)(128)(2,1)S(1)} %copy-done.10, bf16[64,16,256]{2,1,0:T(8,128)(2,1)S(1)} %copy-done.3, bf16[64,16,256]{2,1,0:T(8,128)(2,1)S(1)} %collective-permute-done.refs_1_, ...), custom_call_target="tpu_custom_call" | custom-call | tf_op jit(solution)/shard_map/pick_joint/pallas_call | solution.py:64
  17.0 6.2 %all-to-all-start = ((bf16[64,16,256]{2,1,0:T(8,128)(2,1)}), bf16[64,16,256]{2,1,0:T(8,128)(2,1)S(1)}, u32[]{:S(2)}, u32[]{:S(2)}) async-start(bf16[64,16,256]{2,1,0:T(8,128)(2,1)} %pick_joint.1), calls=%async_computation | async-start | bytes 1048576 | tf_op jit(solution)/shard_map/all_to_all | solution.py:336
  23.2 0.0 collective-permute-done.4
  23.2 0.0 collective-permute-done.5
  23.3 0.0 collective-permute-done.6
  23.3 0.0 collective-permute-done.7
  23.3 0.5 collective-permute-start.8
  23.8 0.8 %copy-done = bf16[8,8,16,256]{3,2,1,0:T(8,128)(2,1)} copy-done((bf16[8,8,16,256]{3,2,1,0:T(8,128)(2,1)}, bf16[8,8,16,256]{3,2,1,0:T(8,128)(2,1)S(1)}, u32[]{:S(2)}) %copy-start) | copy-done | bytes 524312
  24.6 0.7 %collective-permute-done.8.far_ref = bf16[8,8,16,256]{3,2,1,0:T(8,128)(2,1)S(1)} collective-permute-done((bf16[8,8,16,256]{3,2,1,0:T(8,128)(2,1)S(1)}, bf16[8,8,16,256]{3,2,1,0:T(8,128)(2,1)S(1)}, u32[]{:S(2)}, u32[]{:S(2)}) %collective-permute-start.8) | collective-permute-done | bytes 524320 | tf_op jit(solution)/shard_map/ppermute | solution.py:100
  25.3 1.0 %copy-done.1 = bf16[8,8,16,256]{3,2,1,0:T(8,128)(2,1)S(1)} copy-done((bf16[8,8,16,256]{3,2,1,0:T(8,128)(2,1)S(1)}, bf16[8,8,16,256]{3,2,1,0:T(8,128)(2,1)}, u32[]{:S(2)}) %copy-start.1) | copy-done | bytes 524312
  26.4 0.7 %copy-done.7 = bf16[256]{0:T(256)(128)(2,1)S(1)} copy-done((bf16[256]{0:T(256)(128)(2,1)S(1)}, bf16[256]{0:T(256)(128)(2,1)}, u32[]{:S(2)}) %copy-start.7) | copy-done | bytes 536
  27.0 0.7 %copy-done.8 = bf16[256]{0:T(256)(128)(2,1)S(1)} copy-done((bf16[256]{0:T(256)(128)(2,1)S(1)}, bf16[256]{0:T(256)(128)(2,1)}, u32[]{:S(2)}) %copy-start.8) | copy-done | bytes 536
  27.7 1.3 %order_bias.1 = (f32[8,256,256]{2,1,0:T(8,128)S(1)}, f32[264,256]{1,0:T(8,128)S(1)}) custom-call(bf16[8,8,16,256]{3,2,1,0:T(8,128)(2,1)S(1)} %copy-done.1, bf16[8,8,16,256]{3,2,1,0:T(8,128)(2,1)S(1)} %collective-permute-done.8.far_ref, bf16[256]{0:T(256)(128)(2,1)S(1)} %copy-done.5, bf16[256]{0:T(256)(128)(2,1)S(1)} %copy-done.6, ...), custom_call_target="tpu_custom_call" | custom-call | tf_op jit(solution)/shard_map/order_bias/pallas_call | solution.py:123
  29.0 8.7 %all-to-all-done = bf16[64,16,256]{2,1,0:T(8,128)(2,1)S(1)} async-done(((bf16[64,16,256]{2,1,0:T(8,128)(2,1)}), bf16[64,16,256]{2,1,0:T(8,128)(2,1)S(1)}, u32[]{:S(2)}, u32[]{:S(2)}) %all-to-all-start) | async-done | bytes 524320 | tf_op jit(solution)/shard_map/all_to_all | solution.py:336
  37.7 4.5 %attend_rows.1 = (bf16[2,2,4,16,256]{4,3,2,1,0:T(8,128)(2,1)S(1)}, bf16[2,2,4,16,256]{4,3,2,1,0:T(8,128)(2,1)S(1)}, bf16[2,4,16,256]{3,2,1,0:T(8,128)(2,1)S(1)},...) custom-call(bf16[16,4,16,256]{3,2,1,0:T(8,128)(2,1)S(1)} %bitcast.21, ...), custom_call_target="tpu_custom_call" | custom-call | tf_op jit(solution)/shard_map/attend_rows/pallas_call | solution.py:247
  42.2 2.3 %collective-permute-start.9 = (bf16[2,4,16,256]{3,2,1,0:T(8,128)(2,1)S(1)}, bf16[2,4,16,256]{3,2,1,0:T(8,128)(2,1)S(1)}, u32[]{:S(2)}, u32[]{:S(2)}) collective-permute-start(bf16[2,4,16,256]{3,2,1,0:T(8,128)(2,1)S(1)} %get-tuple-element.15), channel_id=1, source_target_pairs={{0,8},{1,9},{2,10},{3,11},{4,12},{5,13},{6,14},{7,15},{8,0},{9,1},... | collective-permute-start | bytes 196616 | tf_op jit(solution)/shard_map/ppermute | solution.py:263
  44.5 0.5 collective-permute-start.10
  45.0 2.0 %collective-permute-start.13 = (bf16[2,2,4,16,256]{4,3,2,1,0:T(8,128)(2,1)S(1)}, bf16[2,2,4,16,256]{4,3,2,1,0:T(8,128)(2,1)S(1)}, u32[]{:S(2)}, u32[]{:S(2)}) collective-permute-start(bf16[2,2,4,16,256]{4,3,2,1,0:T(8,128)(2,1)S(1)} %get-tuple-element.19), channel_id=1, source_target_pairs={{0,4},{1,5},{2,6},{3,7},{4,0},{5,1},{6,2},{7,3},{8,12},{9,13},{10,... | collective-permute-start | bytes 393224 | tf_op jit(solution)/shard_map/ppermute | solution.py:263
  47.0 1.0 %collective-permute-start.11 = (bf16[2,4,16,256]{3,2,1,0:T(8,128)(2,1)S(1)}, bf16[2,4,16,256]{3,2,1,0:T(8,128)(2,1)S(1)}, u32[]{:S(2)}, u32[]{:S(2)}) collective-permute-start(bf16[2,4,16,256]{3,2,1,0:T(8,128)(2,1)S(1)} %get-tuple-element.17), channel_id=1, source_target_pairs={{0,12},{1,13},{2,14},{3,15},{4,8},{5,9},{6,10},{7,11},{8,4},{9,5},... | collective-permute-start | bytes 196616 | tf_op jit(solution)/shard_map/ppermute | solution.py:263
  48.0 3.0 %collective-permute-start.12 = (bf16[2,4,16,256]{3,2,1,0:T(8,128)(2,1)S(1)}, bf16[2,4,16,256]{3,2,1,0:T(8,128)(2,1)S(1)}, u32[]{:S(2)}, u32[]{:S(2)}) collective-permute-start(bf16[2,4,16,256]{3,2,1,0:T(8,128)(2,1)S(1)} %get-tuple-element.18), channel_id=1, source_target_pairs={{0,14},{1,15},{2,12},{3,13},{4,10},{5,11},{6,8},{7,9},{8,6},{9,7},... | collective-permute-start | bytes 196616 | tf_op jit(solution)/shard_map/ppermute | solution.py:263
  51.0 0.0 collective-permute-done.9.refs_0_
  51.0 1.7 %collective-permute-done.10.refs_1_ = bf16[2,4,16,256]{3,2,1,0:T(8,128)(2,1)S(1)} collective-permute-done((bf16[2,4,16,256]{3,2,1,0:T(8,128)(2,1)S(1)}, bf16[2,4,16,256]{3,2,1,0:T(8,128)(2,1)S(1)}, u32[]{:S(2)}, u32[]{:S(2)}) %collective-permute-start.10) | collective-permute-done | bytes 65568 | tf_op jit(solution)/shard_map/ppermute | solution.py:263
  52.8 0.1 collective-permute-done.13.refs_4_
  52.9 1.7 %collective-permute-start.14 = (bf16[2,2,4,16,256]{4,3,2,1,0:T(8,128)(2,1)S(1)}, bf16[2,2,4,16,256]{4,3,2,1,0:T(8,128)(2,1)S(1)}, u32[]{:S(2)}, u32[]{:S(2)}) collective-permute-start(bf16[2,2,4,16,256]{4,3,2,1,0:T(8,128)(2,1)S(1)} %pad_maximum_fusion), channel_id=1, source_target_pairs={{0,2},{1,3},{2,0},{3,1},{4,6},{5,7},{6,4},{7,5},{8,10},{9,11},{10,... | collective-permute-start | bytes 393224 | tf_op jit(solution)/shard_map/ppermute | solution.py:263
  54.6 0.3 collective-permute-done.11.refs_2_
  54.9 1.0 %collective-permute-done.12.refs_3_ = bf16[2,4,16,256]{3,2,1,0:T(8,128)(2,1)S(1)} collective-permute-done((bf16[2,4,16,256]{3,2,1,0:T(8,128)(2,1)S(1)}, bf16[2,4,16,256]{3,2,1,0:T(8,128)(2,1)S(1)}, u32[]{:S(2)}, u32[]{:S(2)}) %collective-permute-start.12) | collective-permute-done | bytes 65568 | tf_op jit(solution)/shard_map/ppermute | solution.py:263
  56.0 2.3 %collective-permute-done.14.refs_5_ = bf16[2,2,4,16,256]{4,3,2,1,0:T(8,128)(2,1)S(1)} collective-permute-done((bf16[2,2,4,16,256]{4,3,2,1,0:T(8,128)(2,1)S(1)}, bf16[2,2,4,16,256]{4,3,2,1,0:T(8,128)(2,1)S(1)}, u32[]{:S(2)}, u32[]{:S(2)}) %collective-permute-start.14) | collective-permute-done | bytes 131104 | tf_op jit(solution)/shard_map/ppermute | solution.py:263
  58.3 0.1 collective-permute-start.15
  58.4 1.5 %collective-permute-done.15.refs_7_ = bf16[8,4,16,256]{3,2,1,0:T(8,128)(2,1)S(1)} collective-permute-done((bf16[8,4,16,256]{3,2,1,0:T(8,128)(2,1)S(1)}, bf16[8,4,16,256]{3,2,1,0:T(8,128)(2,1)S(1)}, u32[]{:S(2)}, u32[]{:S(2)}) %collective-permute-start.15) | collective-permute-done | bytes 262176 | tf_op jit(solution)/shard_map/ppermute | solution.py:263
  59.9 0.9 %place_rows.1 = bf16[64,16,256]{2,1,0:T(8,128)(2,1)} custom-call(bf16[2,4,16,256]{3,2,1,0:T(8,128)(2,1)S(1)} %collective-permute-done.9.refs_0_, bf16[2,4,16,256]{3,2,1,0:T(8,128)(2,1)S(1)} %collective-permute-done.10.refs_1_, bf16[2,4,16,256]{3,2,1,0:T(8,128)(2,1)S(1)} %collective-permute-done.11.refs_2_, ...), custom_call_target="tpu_custom_call" | custom-call | tf_op jit(solution)/shard_map/place_rows/pallas_call | solution.py:299
  (33 shorter events, 0.1 us)
Async XLA Ops:
  0.0 15.2 %copy-start.3 = (bf16[64,16,256]{2,1,0:T(8,128)(2,1)S(1)}, bf16[64,16,256]{2,1,0:T(8,128)(2,1)}, u32[]{:S(2)}) copy-start(bf16[64,16,256]{2,1,0:T(8,128)(2,1)} %refs_0_.2) | copy-start | bytes 1572868
  0.0 15.2 %copy-start.4 = (s32[6,64]{1,0:T(8,128)S(1)}, s32[6,64]{1,0:T(8,128)}, u32[]{:S(2)}) copy-start(s32[6,64]{1,0:T(8,128)} %pairs_ref.1) | copy-start | bytes 4612
  0.0 15.2 %copy-start.9 = (s32[6]{0:T(128)S(1)}, s32[6]{0:T(128)}, u32[]{:S(2)}) copy-start(s32[6]{0:T(128)} %first_ref.1) | copy-start | bytes 76
  0.0 15.2 %copy-start.10 = (bf16[256]{0:T(256)(128)(2,1)S(1)}, bf16[256]{0:T(256)(128)(2,1)}, u32[]{:S(2)}) copy-start(bf16[256]{0:T(256)(128)(2,1)} %gap_ref.1) | copy-start | bytes 1540
  0.0 15.1 %collective-permute-start = (bf16[64,16,256]{2,1,0:T(8,128)(2,1)}, bf16[64,16,256]{2,1,0:T(8,128)(2,1)S(1)}, u32[]{:S(2)}, u32[]{:S(2)}) collective-permute-start(bf16[64,16,256]{2,1,0:T(8,128)(2,1)} %refs_0_.2), channel_id=1, source_target_pairs={{0,16},{16,0},{1,17},{17,1},{2,18},{18,2},{3,19},{19,3},{4,20},{20... | collective-permute-start | bytes 1572872 | tf_op jit(solution)/shard_map/ppermute | solution.py:330
  3.0 8.2 %collective-permute-start.1 = (bf16[1,8,16,256]{3,2,1,0:T(8,128)(2,1)}, bf16[1,8,16,256]{3,2,1,0:T(8,128)(2,1)S(1)}, u32[]{:S(2)}, u32[]{:S(2)}) collective-permute-start(bf16[1,8,16,256]{3,2,1,0:T(8,128)(2,1)} %bitcast.24), channel_id=1, source_target_pairs={{0,8},{1,9},{2,10},{3,11},{4,12},{5,13},{6,14},{7,15},{8,0},{9,1},... | collective-permute-start | bytes 196616 | tf_op jit(solution)/shard_map/ppermute | solution.py:100
  5.6 6.2 %collective-permute-start.2 = (bf16[1,8,16,256]{3,2,1,0:T(8,128)(2,1)}, bf16[1,8,16,256]{3,2,1,0:T(8,128)(2,1)S(1)}, u32[]{:S(2)}, u32[]{:S(2)}) collective-permute-start(bf16[1,8,16,256]{3,2,1,0:T(8,128)(2,1)} %bitcast.25), channel_id=1, source_target_pairs={{0,4},{1,5},{2,6},{3,7},{4,0},{5,1},{6,2},{7,3},{8,12},{9,13},{10,... | collective-permute-start | bytes 196616 | tf_op jit(solution)/shard_map/ppermute | solution.py:100
  7.2 6.3 %collective-permute-start.3 = (bf16[1,8,16,256]{3,2,1,0:T(8,128)(2,1)}, bf16[1,8,16,256]{3,2,1,0:T(8,128)(2,1)S(1)}, u32[]{:S(2)}, u32[]{:S(2)}) collective-permute-start(bf16[1,8,16,256]{3,2,1,0:T(8,128)(2,1)} %bitcast.26), channel_id=1, source_target_pairs={{0,12},{1,13},{2,14},{3,15},{4,8},{5,9},{6,10},{7,11},{8,4},{9,5},... | collective-permute-start | bytes 196616 | tf_op jit(solution)/shard_map/ppermute | solution.py:100
  7.4 15.8 %collective-permute-start.4 = (bf16[1,8,16,256]{3,2,1,0:T(8,128)(2,1)}, bf16[1,8,16,256]{3,2,1,0:T(8,128)(2,1)S(1)}, u32[]{:S(2)}, u32[]{:S(2)}) collective-permute-start(bf16[1,8,16,256]{3,2,1,0:T(8,128)(2,1)} %bitcast.27), channel_id=1, source_target_pairs={{0,2},{1,3},{2,0},{3,1},{4,6},{5,7},{6,4},{7,5},{8,10},{9,11},{10,... | collective-permute-start | bytes 196616 | tf_op jit(solution)/shard_map/ppermute | solution.py:100
  11.2 14.1 %copy-start.2 = (bf16[256,256]{1,0:T(8,128)(2,1)S(1)}, bf16[256,256]{1,0:T(8,128)(2,1)}, u32[]{:S(2)}) copy-start(bf16[256,256]{1,0:T(8,128)(2,1)} %out_weight_ref.1) | copy-start | bytes 393220
  11.2 14.1 %copy-start.5 = (bf16[256]{0:T(256)(128)(2,1)S(1)}, bf16[256]{0:T(256)(128)(2,1)}, u32[]{:S(2)}) copy-start(bf16[256]{0:T(256)(128)(2,1)} %refs_0_.3) | copy-start | bytes 1540
  11.2 14.1 %copy-start.6 = (bf16[256]{0:T(256)(128)(2,1)S(1)}, bf16[256]{0:T(256)(128)(2,1)}, u32[]{:S(2)}) copy-start(bf16[256]{0:T(256)(128)(2,1)} %refs_1_.1) | copy-start | bytes 1540
  11.2 12.0 %collective-permute-start.5 = (bf16[1,8,16,256]{3,2,1,0:T(8,128)(2,1)S(1)}, bf16[1,8,16,256]{3,2,1,0:T(8,128)(2,1)S(1)}, u32[]{:S(2)}, u32[]{:S(2)}) collective-permute-start(bf16[1,8,16,256]{3,2,1,0:T(8,128)(2,1)S(1)} %collective-permute-done.1), channel_id=1, source_target_pairs={{0,2},{1,3},{2,0},{3,1},{4,6},{5,7},{6,4},{7,5},{8,10},{9,11},{10,... | collective-permute-start | bytes 196616 | tf_op jit(solution)/shard_map/ppermute | solution.py:100
  11.8 11.4 %collective-permute-start.6 = (bf16[1,8,16,256]{3,2,1,0:T(8,128)(2,1)S(1)}, bf16[1,8,16,256]{3,2,1,0:T(8,128)(2,1)S(1)}, u32[]{:S(2)}, u32[]{:S(2)}) collective-permute-start(bf16[1,8,16,256]{3,2,1,0:T(8,128)(2,1)S(1)} %collective-permute-done.2), channel_id=1, source_target_pairs={{0,2},{1,3},{2,0},{3,1},{4,6},{5,7},{6,4},{7,5},{8,10},{9,11},{10,... | collective-permute-start | bytes 196616 | tf_op jit(solution)/shard_map/ppermute | solution.py:100
  13.5 9.8 %collective-permute-start.7 = (bf16[1,8,16,256]{3,2,1,0:T(8,128)(2,1)S(1)}, bf16[1,8,16,256]{3,2,1,0:T(8,128)(2,1)S(1)}, u32[]{:S(2)}, u32[]{:S(2)}) collective-permute-start(bf16[1,8,16,256]{3,2,1,0:T(8,128)(2,1)S(1)} %collective-permute-done.3), channel_id=1, source_target_pairs={{0,2},{1,3},{2,0},{3,1},{4,6},{5,7},{6,4},{7,5},{8,10},{9,11},{10,... | collective-permute-start | bytes 196616 | tf_op jit(solution)/shard_map/ppermute | solution.py:100
  17.0 20.7 %all-to-all-start = ((bf16[64,16,256]{2,1,0:T(8,128)(2,1)}), bf16[64,16,256]{2,1,0:T(8,128)(2,1)S(1)}, u32[]{:S(2)}, u32[]{:S(2)}) async-start(bf16[64,16,256]{2,1,0:T(8,128)(2,1)} %pick_joint.1), calls=%async_computation | async-start | bytes 1048576 | tf_op jit(solution)/shard_map/all_to_all | solution.py:336
  23.3 2.0 %collective-permute-start.8 = (bf16[8,8,16,256]{3,2,1,0:T(8,128)(2,1)S(1)}, bf16[8,8,16,256]{3,2,1,0:T(8,128)(2,1)S(1)}, u32[]{:S(2)}, u32[]{:S(2)}) collective-permute-start(bf16[8,8,16,256]{3,2,1,0:T(8,128)(2,1)S(1)} %constant_dynamic-update-slice_fusion.near_ref), channel_id=1, source_target_pairs={{0,1},{1,0},{2,3},{3,2},{4,5},{5,4},{6,7},{7,6},{8,9},{9,8},{10,11... | collective-permute-start | bytes 1572872 | tf_op jit(solution)/shard_map/ppermute | solution.py:100
  23.8 0.8 %copy-start = (bf16[8,8,16,256]{3,2,1,0:T(8,128)(2,1)}, bf16[8,8,16,256]{3,2,1,0:T(8,128)(2,1)S(1)}, u32[]{:S(2)}) copy-start(bf16[8,8,16,256]{3,2,1,0:T(8,128)(2,1)S(1)} %constant_dynamic-update-slice_fusion.near_ref) | copy-start | bytes 1572868
  25.3 1.0 %copy-start.1 = (bf16[8,8,16,256]{3,2,1,0:T(8,128)(2,1)S(1)}, bf16[8,8,16,256]{3,2,1,0:T(8,128)(2,1)}, u32[]{:S(2)}) copy-start(bf16[8,8,16,256]{3,2,1,0:T(8,128)(2,1)} %copy-done) | copy-start | bytes 1572868
  26.4 0.7 %copy-start.7 = (bf16[256]{0:T(256)(128)(2,1)S(1)}, bf16[256]{0:T(256)(128)(2,1)}, u32[]{:S(2)}) copy-start(bf16[256]{0:T(256)(128)(2,1)} %refs_2_.1) | copy-start | bytes 1540
  27.0 0.7 %copy-start.8 = (bf16[256]{0:T(256)(128)(2,1)S(1)}, bf16[256]{0:T(256)(128)(2,1)}, u32[]{:S(2)}) copy-start(bf16[256]{0:T(256)(128)(2,1)} %refs_3_.1) | copy-start | bytes 1540
  42.2 8.8 %collective-permute-start.9 = (bf16[2,4,16,256]{3,2,1,0:T(8,128)(2,1)S(1)}, bf16[2,4,16,256]{3,2,1,0:T(8,128)(2,1)S(1)}, u32[]{:S(2)}, u32[]{:S(2)}) collective-permute-start(bf16[2,4,16,256]{3,2,1,0:T(8,128)(2,1)S(1)} %get-tuple-element.15), channel_id=1, source_target_pairs={{0,8},{1,9},{2,10},{3,11},{4,12},{5,13},{6,14},{7,15},{8,0},{9,1},... | collective-permute-start | bytes 196616 | tf_op jit(solution)/shard_map/ppermute | solution.py:263
  44.5 8.2 %collective-permute-start.10 = (bf16[2,4,16,256]{3,2,1,0:T(8,128)(2,1)S(1)}, bf16[2,4,16,256]{3,2,1,0:T(8,128)(2,1)S(1)}, u32[]{:S(2)}, u32[]{:S(2)}) collective-permute-start(bf16[2,4,16,256]{3,2,1,0:T(8,128)(2,1)S(1)} %get-tuple-element.16), channel_id=1, source_target_pairs={{0,10},{1,11},{2,8},{3,9},{4,14},{5,15},{6,12},{7,13},{8,2},{9,3},... | collective-permute-start | bytes 196616 | tf_op jit(solution)/shard_map/ppermute | solution.py:263
  45.0 7.9 %collective-permute-start.13 = (bf16[2,2,4,16,256]{4,3,2,1,0:T(8,128)(2,1)S(1)}, bf16[2,2,4,16,256]{4,3,2,1,0:T(8,128)(2,1)S(1)}, u32[]{:S(2)}, u32[]{:S(2)}) collective-permute-start(bf16[2,2,4,16,256]{4,3,2,1,0:T(8,128)(2,1)S(1)} %get-tuple-element.19), channel_id=1, source_target_pairs={{0,4},{1,5},{2,6},{3,7},{4,0},{5,1},{6,2},{7,3},{8,12},{9,13},{10,... | collective-permute-start | bytes 393224 | tf_op jit(solution)/shard_map/ppermute | solution.py:263
  47.0 7.9 %collective-permute-start.11 = (bf16[2,4,16,256]{3,2,1,0:T(8,128)(2,1)S(1)}, bf16[2,4,16,256]{3,2,1,0:T(8,128)(2,1)S(1)}, u32[]{:S(2)}, u32[]{:S(2)}) collective-permute-start(bf16[2,4,16,256]{3,2,1,0:T(8,128)(2,1)S(1)} %get-tuple-element.17), channel_id=1, source_target_pairs={{0,12},{1,13},{2,14},{3,15},{4,8},{5,9},{6,10},{7,11},{8,4},{9,5},... | collective-permute-start | bytes 196616 | tf_op jit(solution)/shard_map/ppermute | solution.py:263
  48.0 8.0 %collective-permute-start.12 = (bf16[2,4,16,256]{3,2,1,0:T(8,128)(2,1)S(1)}, bf16[2,4,16,256]{3,2,1,0:T(8,128)(2,1)S(1)}, u32[]{:S(2)}, u32[]{:S(2)}) collective-permute-start(bf16[2,4,16,256]{3,2,1,0:T(8,128)(2,1)S(1)} %get-tuple-element.18), channel_id=1, source_target_pairs={{0,14},{1,15},{2,12},{3,13},{4,10},{5,11},{6,8},{7,9},{8,6},{9,7},... | collective-permute-start | bytes 196616 | tf_op jit(solution)/shard_map/ppermute | solution.py:263
  52.9 5.3 %collective-permute-start.14 = (bf16[2,2,4,16,256]{4,3,2,1,0:T(8,128)(2,1)S(1)}, bf16[2,2,4,16,256]{4,3,2,1,0:T(8,128)(2,1)S(1)}, u32[]{:S(2)}, u32[]{:S(2)}) collective-permute-start(bf16[2,2,4,16,256]{4,3,2,1,0:T(8,128)(2,1)S(1)} %pad_maximum_fusion), channel_id=1, source_target_pairs={{0,2},{1,3},{2,0},{3,1},{4,6},{5,7},{6,4},{7,5},{8,10},{9,11},{10,... | collective-permute-start | bytes 393224 | tf_op jit(solution)/shard_map/ppermute | solution.py:263
  58.3 1.6 %collective-permute-start.15 = (bf16[8,4,16,256]{3,2,1,0:T(8,128)(2,1)S(1)}, bf16[8,4,16,256]{3,2,1,0:T(8,128)(2,1)S(1)}, u32[]{:S(2)}, u32[]{:S(2)}) collective-permute-start(bf16[8,4,16,256]{3,2,1,0:T(8,128)(2,1)S(1)} %constant_dynamic-update-slice_fusion.8), channel_id=1, source_target_pairs={{0,1},{1,0},{2,3},{3,2},{4,5},{5,4},{6,7},{7,6},{8,9},{9,8},{10,11... | collective-permute-start | bytes 786440 | tf_op jit(solution)/shard_map/ppermute | solution.py:263

commit v6 on v5

--- a/solution.py
+++ b/solution.py
@@ -268,9 +268,7 @@
     far = [swap(piece, (4 + k) * cores) for k, piece in enumerate(far)]
     there = swap(there, 2 * cores)
     hop = swap(jnp.stack([here[1], there[1]]), cores)
-    middle = len(far) // 2
-    arrived = [(4 + k, far[k]) for k in range(middle)] + [(2, there[0])]
-    arrived += [(4 + k, far[k]) for k in range(middle, len(far))]
+    arrived = [(2, there[0]), *((4 + k, piece) for k, piece in enumerate(far))]
     arrived += [(1, hop[0]), (3, hop[1]), (0, here[0])]
     other = swap(jnp.stack([blocks[1] for _, blocks in arrived]), 1)
     return [chip for chip, _ in arrived], far, there, hop, here, other

time: 61.2 us -> 61.1 us (level)
  transfers between devices with their start and end apart: 17 -> 17, of which waited for: 10 -> 8; matrix products, arithmetic and copies ran while one was open for 3% -> 3% of each run, Pallas kernels for 5% -> 5%
where the time goes in v6:
time: 61.1 us; the launch traced here: 60.7 us
  starting transfers between devices  29.4 us (48%)
  waiting for transfers between devices  17 us (28%)
  Pallas kernels  8.77 us (14%)
  local copies, waits for them, and re-layouts  5.3 us (9%)
    ppermute x7, starting transfers between devices, swap(): return lax.ppermute(array, 'res', [(i, i ^ flip) for i in range(members)])  10.2 us
    ppermute x8, starting transfers between devices, swap(): return lax.ppermute(piece, 'res', [(i, i ^ flip) for i in range(members)])  9.99 us
    all_to_all x1, waiting for transfers between devices, local(): lax.all_to_all(joint, 'res', split_axis=0, concat_axis=0, tiled=True)  8.69 us
    ppermute x7, waiting for transfers between devices, swap(): return lax.ppermute(array, 'res', [(i, i ^ flip) for i in range(members)])  7.25 us
    all_to_all x1, starting transfers between devices, local(): lax.all_to_all(joint, 'res', split_axis=0, concat_axis=0, tiled=True)  6.2 us
    unnamed x37, local copies, waits for them, and re-layouts  5.28 us
    pallas_call x1, Pallas kernels, attend(): pl.pallas_call(attend_kernel, out_shape=[jax.ShapeDtypeStruct(shape, jnp....  4.53 us
    ppermute x1, starting transfers between devices, local(): lax.ppermute(source_alignment_rows, 'rows', [(i, (i + hop) % owners) for...  3.01 us
  transfers between devices with their start and end apart: 17, of which 8 were waited for; matrix products, arithmetic and copies ran while one was open for 3% of the time, Pallas kernels for 5%

profile of v6, /device:TPU:0, one launch (start us, length us, event | category | flops | bytes accessed | tf_op | source)
XLA Modules:
  0.0 60.7 jit_solution(11277246011298231580)
XLA Ops:
  0.0 3.0 %collective-permute-start = (bf16[64,16,256]{2,1,0:T(8,128)(2,1)}, bf16[64,16,256]{2,1,0:T(8,128)(2,1)S(1)}, u32[]{:S(2)}, u32[]{:S(2)}) collective-permute-start(bf16[64,16,256]{2,1,0:T(8,128)(2,1)} %refs_0_.2), channel_id=1, source_target_pairs={{0,16},{16,0},{1,17},{17,1},{2,18},{18,2},{3,19},{19,3},{4,20},{20... | collective-permute-start | bytes 1572872 | tf_op jit(solution)/shard_map/ppermute | solution.py:328
  3.0 2.6 %collective-permute-start.1 = (bf16[1,8,16,256]{3,2,1,0:T(8,128)(2,1)}, bf16[1,8,16,256]{3,2,1,0:T(8,128)(2,1)S(1)}, u32[]{:S(2)}, u32[]{:S(2)}) collective-permute-start(bf16[1,8,16,256]{3,2,1,0:T(8,128)(2,1)} %bitcast.24), channel_id=1, source_target_pairs={{0,8},{1,9},{2,10},{3,11},{4,12},{5,13},{6,14},{7,15},{8,0},{9,1},... | collective-permute-start | bytes 196616 | tf_op jit(solution)/shard_map/ppermute | solution.py:100
  5.6 1.6 %collective-permute-start.2 = (bf16[1,8,16,256]{3,2,1,0:T(8,128)(2,1)}, bf16[1,8,16,256]{3,2,1,0:T(8,128)(2,1)S(1)}, u32[]{:S(2)}, u32[]{:S(2)}) collective-permute-start(bf16[1,8,16,256]{3,2,1,0:T(8,128)(2,1)} %bitcast.25), channel_id=1, source_target_pairs={{0,4},{1,5},{2,6},{3,7},{4,0},{5,1},{6,2},{7,3},{8,12},{9,13},{10,... | collective-permute-start | bytes 196616 | tf_op jit(solution)/shard_map/ppermute | solution.py:100
  7.2 0.2 collective-permute-start.3
  7.4 1.5 %collective-permute-start.4 = (bf16[1,8,16,256]{3,2,1,0:T(8,128)(2,1)}, bf16[1,8,16,256]{3,2,1,0:T(8,128)(2,1)S(1)}, u32[]{:S(2)}, u32[]{:S(2)}) collective-permute-start(bf16[1,8,16,256]{3,2,1,0:T(8,128)(2,1)} %bitcast.27), channel_id=1, source_target_pairs={{0,2},{1,3},{2,0},{3,1},{4,6},{5,7},{6,4},{7,5},{8,10},{9,11},{10,... | collective-permute-start | bytes 196616 | tf_op jit(solution)/shard_map/ppermute | solution.py:100
  8.9 0.9 %constant_dynamic-update-slice_fusion.7 = bf16[8,8,16,256]{3,2,1,0:T(8,128)(2,1)S(1)} fusion(bf16[8,16,256]{2,1,0:T(8,128)(2,1)} %param.19), kind=kLoop, calls=%fused_computation.9 | loop fusion | bytes 131072
  9.8 1.1 %copy.14 = bf16[32,8,8,128]{3,1,2,0:T(8,128)(2,1)S(1)} copy(bf16[32,8,8,128]{3,2,1,0:T(8,128)(2,1)} %bitcast.23) | data formatting | bytes 1048576
  10.9 0.2 turn_weights.1.refs_2_.refs_4_.weights_ref
  11.2 0.0 copy-start.2
  11.2 0.0 copy-start.5
  11.2 0.0 copy-start.6
  11.2 0.0 collective-permute-done.1
  11.2 0.6 collective-permute-start.5
  11.8 0.0 collective-permute-done.2
  11.8 1.5 %collective-permute-start.6 = (bf16[1,8,16,256]{3,2,1,0:T(8,128)(2,1)S(1)}, bf16[1,8,16,256]{3,2,1,0:T(8,128)(2,1)S(1)}, u32[]{:S(2)}, u32[]{:S(2)}) collective-permute-start(bf16[1,8,16,256]{3,2,1,0:T(8,128)(2,1)S(1)} %collective-permute-done.2), channel_id=1, source_target_pairs={{0,2},{1,3},{2,0},{3,1},{4,6},{5,7},{6,4},{7,5},{8,10},{9,11},{10,... | collective-permute-start | bytes 196616 | tf_op jit(solution)/shard_map/ppermute | solution.py:100
  13.3 0.1 collective-permute-done.3
  13.5 1.5 %collective-permute-start.7 = (bf16[1,8,16,256]{3,2,1,0:T(8,128)(2,1)S(1)}, bf16[1,8,16,256]{3,2,1,0:T(8,128)(2,1)S(1)}, u32[]{:S(2)}, u32[]{:S(2)}) collective-permute-start(bf16[1,8,16,256]{3,2,1,0:T(8,128)(2,1)S(1)} %collective-permute-done.3), channel_id=1, source_target_pairs={{0,2},{1,3},{2,0},{3,1},{4,6},{5,7},{6,4},{7,5},{8,10},{9,11},{10,... | collective-permute-start | bytes 196616 | tf_op jit(solution)/shard_map/ppermute | solution.py:100
  15.0 0.2 collective-permute-done.refs_1_
  15.2 1.8 %pick_joint.1 = bf16[64,16,256]{2,1,0:T(8,128)(2,1)} custom-call(s32[6,64]{1,0:T(8,128)S(1)} %copy-done.4, s32[6]{0:T(128)S(1)} %copy-done.9, bf16[256]{0:T(256)(128)(2,1)S(1)} %copy-done.10, bf16[64,16,256]{2,1,0:T(8,128)(2,1)S(1)} %copy-done.3, bf16[64,16,256]{2,1,0:T(8,128)(2,1)S(1)} %collective-permute-done.refs_1_, ...), custom_call_target="tpu_custom_call" | custom-call | tf_op jit(solution)/shard_map/pick_joint/pallas_call | solution.py:64
  17.0 6.2 %all-to-all-start = ((bf16[64,16,256]{2,1,0:T(8,128)(2,1)}), bf16[64,16,256]{2,1,0:T(8,128)(2,1)S(1)}, u32[]{:S(2)}, u32[]{:S(2)}) async-start(bf16[64,16,256]{2,1,0:T(8,128)(2,1)} %pick_joint.1), calls=%async_computation | async-start | bytes 1048576 | tf_op jit(solution)/shard_map/all_to_all | solution.py:334
  23.2 0.0 collective-permute-done.4
  23.2 0.0 collective-permute-done.5
  23.3 0.0 collective-permute-done.6
  23.3 0.0 collective-permute-done.7
  23.3 0.5 collective-permute-start.8
  23.8 0.8 %copy-done = bf16[8,8,16,256]{3,2,1,0:T(8,128)(2,1)} copy-done((bf16[8,8,16,256]{3,2,1,0:T(8,128)(2,1)}, bf16[8,8,16,256]{3,2,1,0:T(8,128)(2,1)S(1)}, u32[]{:S(2)}) %copy-start) | copy-done | bytes 524312
  24.6 0.7 %collective-permute-done.8.far_ref = bf16[8,8,16,256]{3,2,1,0:T(8,128)(2,1)S(1)} collective-permute-done((bf16[8,8,16,256]{3,2,1,0:T(8,128)(2,1)S(1)}, bf16[8,8,16,256]{3,2,1,0:T(8,128)(2,1)S(1)}, u32[]{:S(2)}, u32[]{:S(2)}) %collective-permute-start.8) | collective-permute-done | bytes 524320 | tf_op jit(solution)/shard_map/ppermute | solution.py:100
  25.3 1.0 %copy-done.1 = bf16[8,8,16,256]{3,2,1,0:T(8,128)(2,1)S(1)} copy-done((bf16[8,8,16,256]{3,2,1,0:T(8,128)(2,1)S(1)}, bf16[8,8,16,256]{3,2,1,0:T(8,128)(2,1)}, u32[]{:S(2)}) %copy-start.1) | copy-done | bytes 524312
  26.4 0.7 %copy-done.7 = bf16[256]{0:T(256)(128)(2,1)S(1)} copy-done((bf16[256]{0:T(256)(128)(2,1)S(1)}, bf16[256]{0:T(256)(128)(2,1)}, u32[]{:S(2)}) %copy-start.7) | copy-done | bytes 536
  27.0 0.7 %copy-done.8 = bf16[256]{0:T(256)(128)(2,1)S(1)} copy-done((bf16[256]{0:T(256)(128)(2,1)S(1)}, bf16[256]{0:T(256)(128)(2,1)}, u32[]{:S(2)}) %copy-start.8) | copy-done | bytes 536
  27.7 1.3 %order_bias.1 = (f32[8,256,256]{2,1,0:T(8,128)S(1)}, f32[264,256]{1,0:T(8,128)S(1)}) custom-call(bf16[8,8,16,256]{3,2,1,0:T(8,128)(2,1)S(1)} %copy-done.1, bf16[8,8,16,256]{3,2,1,0:T(8,128)(2,1)S(1)} %collective-permute-done.8.far_ref, bf16[256]{0:T(256)(128)(2,1)S(1)} %copy-done.5, bf16[256]{0:T(256)(128)(2,1)S(1)} %copy-done.6, ...), custom_call_target="tpu_custom_call" | custom-call | tf_op jit(solution)/shard_map/order_bias/pallas_call | solution.py:123
  29.0 8.7 %all-to-all-done = bf16[64,16,256]{2,1,0:T(8,128)(2,1)S(1)} async-done(((bf16[64,16,256]{2,1,0:T(8,128)(2,1)}), bf16[64,16,256]{2,1,0:T(8,128)(2,1)S(1)}, u32[]{:S(2)}, u32[]{:S(2)}) %all-to-all-start) | async-done | bytes 524320 | tf_op jit(solution)/shard_map/all_to_all | solution.py:334
  37.7 4.5 %attend_rows.1 = (bf16[2,2,4,16,256]{4,3,2,1,0:T(8,128)(2,1)S(1)}, bf16[2,2,4,16,256]{4,3,2,1,0:T(8,128)(2,1)S(1)}, bf16[2,4,16,256]{3,2,1,0:T(8,128)(2,1)S(1)},...) custom-call(bf16[16,4,16,256]{3,2,1,0:T(8,128)(2,1)S(1)} %bitcast.21, ...), custom_call_target="tpu_custom_call" | custom-call | tf_op jit(solution)/shard_map/attend_rows/pallas_call | solution.py:247
  42.2 1.2 %collective-permute-start.13 = (bf16[2,2,4,16,256]{4,3,2,1,0:T(8,128)(2,1)S(1)}, bf16[2,2,4,16,256]{4,3,2,1,0:T(8,128)(2,1)S(1)}, u32[]{:S(2)}, u32[]{:S(2)}) collective-permute-start(bf16[2,2,4,16,256]{4,3,2,1,0:T(8,128)(2,1)S(1)} %get-tuple-element.19), channel_id=1, source_target_pairs={{0,4},{1,5},{2,6},{3,7},{4,0},{5,1},{6,2},{7,3},{8,12},{9,13},{10,... | collective-permute-start | bytes 393224 | tf_op jit(solution)/shard_map/ppermute | solution.py:263
  43.4 1.2 %collective-permute-start.9 = (bf16[2,4,16,256]{3,2,1,0:T(8,128)(2,1)S(1)}, bf16[2,4,16,256]{3,2,1,0:T(8,128)(2,1)S(1)}, u32[]{:S(2)}, u32[]{:S(2)}) collective-permute-start(bf16[2,4,16,256]{3,2,1,0:T(8,128)(2,1)S(1)} %get-tuple-element.15), channel_id=1, source_target_pairs={{0,8},{1,9},{2,10},{3,11},{4,12},{5,13},{6,14},{7,15},{8,0},{9,1},... | collective-permute-start | bytes 196616 | tf_op jit(solution)/shard_map/ppermute | solution.py:263
  44.6 2.4 %collective-permute-start.10 = (bf16[2,4,16,256]{3,2,1,0:T(8,128)(2,1)S(1)}, bf16[2,4,16,256]{3,2,1,0:T(8,128)(2,1)S(1)}, u32[]{:S(2)}, u32[]{:S(2)}) collective-permute-start(bf16[2,4,16,256]{3,2,1,0:T(8,128)(2,1)S(1)} %get-tuple-element.16), channel_id=1, source_target_pairs={{0,10},{1,11},{2,8},{3,9},{4,14},{5,15},{6,12},{7,13},{8,2},{9,3},... | collective-permute-start | bytes 196616 | tf_op jit(solution)/shard_map/ppermute | solution.py:263
  47.0 1.0 %collective-permute-start.11 = (bf16[2,4,16,256]{3,2,1,0:T(8,128)(2,1)S(1)}, bf16[2,4,16,256]{3,2,1,0:T(8,128)(2,1)S(1)}, u32[]{:S(2)}, u32[]{:S(2)}) collective-permute-start(bf16[2,4,16,256]{3,2,1,0:T(8,128)(2,1)S(1)} %get-tuple-element.17), channel_id=1, source_target_pairs={{0,12},{1,13},{2,14},{3,15},{4,8},{5,9},{6,10},{7,11},{8,4},{9,5},... | collective-permute-start | bytes 196616 | tf_op jit(solution)/shard_map/ppermute | solution.py:263
  48.0 3.0 %collective-permute-start.12 = (bf16[2,4,16,256]{3,2,1,0:T(8,128)(2,1)S(1)}, bf16[2,4,16,256]{3,2,1,0:T(8,128)(2,1)S(1)}, u32[]{:S(2)}, u32[]{:S(2)}) collective-permute-start(bf16[2,4,16,256]{3,2,1,0:T(8,128)(2,1)S(1)} %get-tuple-element.18), channel_id=1, source_target_pairs={{0,14},{1,15},{2,12},{3,13},{4,10},{5,11},{6,8},{7,9},{8,6},{9,7},... | collective-permute-start | bytes 196616 | tf_op jit(solution)/shard_map/ppermute | solution.py:263
  51.0 0.0 collective-permute-done.13.refs_4_
  51.1 1.3 %collective-permute-start.14 = (bf16[2,2,4,16,256]{4,3,2,1,0:T(8,128)(2,1)S(1)}, bf16[2,2,4,16,256]{4,3,2,1,0:T(8,128)(2,1)S(1)}, u32[]{:S(2)}, u32[]{:S(2)}) collective-permute-start(bf16[2,2,4,16,256]{4,3,2,1,0:T(8,128)(2,1)S(1)} %pad_maximum_fusion), channel_id=1, source_target_pairs={{0,2},{1,3},{2,0},{3,1},{4,6},{5,7},{6,4},{7,5},{8,10},{9,11},{10,... | collective-permute-start | bytes 393224 | tf_op jit(solution)/shard_map/ppermute | solution.py:263
  52.4 1.4 %collective-permute-done.9.refs_0_ = bf16[2,4,16,256]{3,2,1,0:T(8,128)(2,1)S(1)} collective-permute-done((bf16[2,4,16,256]{3,2,1,0:T(8,128)(2,1)S(1)}, bf16[2,4,16,256]{3,2,1,0:T(8,128)(2,1)S(1)}, u32[]{:S(2)}, u32[]{:S(2)}) %collective-permute-start.9) | collective-permute-done | bytes 65568 | tf_op jit(solution)/shard_map/ppermute | solution.py:263
  53.8 3.1 %collective-permute-done.10.refs_1_ = bf16[2,4,16,256]{3,2,1,0:T(8,128)(2,1)S(1)} collective-permute-done((bf16[2,4,16,256]{3,2,1,0:T(8,128)(2,1)S(1)}, bf16[2,4,16,256]{3,2,1,0:T(8,128)(2,1)S(1)}, u32[]{:S(2)}, u32[]{:S(2)}) %collective-permute-start.10) | collective-permute-done | bytes 65568 | tf_op jit(solution)/shard_map/ppermute | solution.py:263
  56.9 0.0 collective-permute-done.11.refs_2_
  56.9 0.0 collective-permute-done.12.refs_3_
  56.9 1.2 %collective-permute-done.14.refs_5_ = bf16[2,2,4,16,256]{4,3,2,1,0:T(8,128)(2,1)S(1)} collective-permute-done((bf16[2,2,4,16,256]{4,3,2,1,0:T(8,128)(2,1)S(1)}, bf16[2,2,4,16,256]{4,3,2,1,0:T(8,128)(2,1)S(1)}, u32[]{:S(2)}, u32[]{:S(2)}) %collective-permute-start.14) | collective-permute-done | bytes 131104 | tf_op jit(solution)/shard_map/ppermute | solution.py:263
  58.2 0.1 collective-permute-start.15
  58.3 1.5 %collective-permute-done.15.refs_7_ = bf16[8,4,16,256]{3,2,1,0:T(8,128)(2,1)S(1)} collective-permute-done((bf16[8,4,16,256]{3,2,1,0:T(8,128)(2,1)S(1)}, bf16[8,4,16,256]{3,2,1,0:T(8,128)(2,1)S(1)}, u32[]{:S(2)}, u32[]{:S(2)}) %collective-permute-start.15) | collective-permute-done | bytes 262176 | tf_op jit(solution)/shard_map/ppermute | solution.py:263
  59.8 0.9 %place_rows.1 = bf16[64,16,256]{2,1,0:T(8,128)(2,1)} custom-call(bf16[2,4,16,256]{3,2,1,0:T(8,128)(2,1)S(1)} %collective-permute-done.9.refs_0_, bf16[2,4,16,256]{3,2,1,0:T(8,128)(2,1)S(1)} %collective-permute-done.10.refs_1_, bf16[2,4,16,256]{3,2,1,0:T(8,128)(2,1)S(1)} %collective-permute-done.11.refs_2_, ...), custom_call_target="tpu_custom_call" | custom-call | tf_op jit(solution)/shard_map/place_rows/pallas_call | solution.py:297
  (33 shorter events, 0.1 us)
Async XLA Ops:
  0.0 15.2 %copy-start.3 = (bf16[64,16,256]{2,1,0:T(8,128)(2,1)S(1)}, bf16[64,16,256]{2,1,0:T(8,128)(2,1)}, u32[]{:S(2)}) copy-start(bf16[64,16,256]{2,1,0:T(8,128)(2,1)} %refs_0_.2) | copy-start | bytes 1572868
  0.0 15.2 %copy-start.4 = (s32[6,64]{1,0:T(8,128)S(1)}, s32[6,64]{1,0:T(8,128)}, u32[]{:S(2)}) copy-start(s32[6,64]{1,0:T(8,128)} %pairs_ref.1) | copy-start | bytes 4612
  0.0 15.2 %copy-start.9 = (s32[6]{0:T(128)S(1)}, s32[6]{0:T(128)}, u32[]{:S(2)}) copy-start(s32[6]{0:T(128)} %first_ref.1) | copy-start | bytes 76
  0.0 15.2 %copy-start.10 = (bf16[256]{0:T(256)(128)(2,1)S(1)}, bf16[256]{0:T(256)(128)(2,1)}, u32[]{:S(2)}) copy-start(bf16[256]{0:T(256)(128)(2,1)} %gap_ref.1) | copy-start | bytes 1540
  0.0 15.1 %collective-permute-start = (bf16[64,16,256]{2,1,0:T(8,128)(2,1)}, bf16[64,16,256]{2,1,0:T(8,128)(2,1)S(1)}, u32[]{:S(2)}, u32[]{:S(2)}) collective-permute-start(bf16[64,16,256]{2,1,0:T(8,128)(2,1)} %refs_0_.2), channel_id=1, source_target_pairs={{0,16},{16,0},{1,17},{17,1},{2,18},{18,2},{3,19},{19,3},{4,20},{20... | collective-permute-start | bytes 1572872 | tf_op jit(solution)/shard_map/ppermute | solution.py:328
  3.0 8.2 %collective-permute-start.1 = (bf16[1,8,16,256]{3,2,1,0:T(8,128)(2,1)}, bf16[1,8,16,256]{3,2,1,0:T(8,128)(2,1)S(1)}, u32[]{:S(2)}, u32[]{:S(2)}) collective-permute-start(bf16[1,8,16,256]{3,2,1,0:T(8,128)(2,1)} %bitcast.24), channel_id=1, source_target_pairs={{0,8},{1,9},{2,10},{3,11},{4,12},{5,13},{6,14},{7,15},{8,0},{9,1},... | collective-permute-start | bytes 196616 | tf_op jit(solution)/shard_map/ppermute | solution.py:100
  5.6 6.2 %collective-permute-start.2 = (bf16[1,8,16,256]{3,2,1,0:T(8,128)(2,1)}, bf16[1,8,16,256]{3,2,1,0:T(8,128)(2,1)S(1)}, u32[]{:S(2)}, u32[]{:S(2)}) collective-permute-start(bf16[1,8,16,256]{3,2,1,0:T(8,128)(2,1)} %bitcast.25), channel_id=1, source_target_pairs={{0,4},{1,5},{2,6},{3,7},{4,0},{5,1},{6,2},{7,3},{8,12},{9,13},{10,... | collective-permute-start | bytes 196616 | tf_op jit(solution)/shard_map/ppermute | solution.py:100
  7.2 6.3 %collective-permute-start.3 = (bf16[1,8,16,256]{3,2,1,0:T(8,128)(2,1)}, bf16[1,8,16,256]{3,2,1,0:T(8,128)(2,1)S(1)}, u32[]{:S(2)}, u32[]{:S(2)}) collective-permute-start(bf16[1,8,16,256]{3,2,1,0:T(8,128)(2,1)} %bitcast.26), channel_id=1, source_target_pairs={{0,12},{1,13},{2,14},{3,15},{4,8},{5,9},{6,10},{7,11},{8,4},{9,5},... | collective-permute-start | bytes 196616 | tf_op jit(solution)/shard_map/ppermute | solution.py:100
  7.4 15.8 %collective-permute-start.4 = (bf16[1,8,16,256]{3,2,1,0:T(8,128)(2,1)}, bf16[1,8,16,256]{3,2,1,0:T(8,128)(2,1)S(1)}, u32[]{:S(2)}, u32[]{:S(2)}) collective-permute-start(bf16[1,8,16,256]{3,2,1,0:T(8,128)(2,1)} %bitcast.27), channel_id=1, source_target_pairs={{0,2},{1,3},{2,0},{3,1},{4,6},{5,7},{6,4},{7,5},{8,10},{9,11},{10,... | collective-permute-start | bytes 196616 | tf_op jit(solution)/shard_map/ppermute | solution.py:100
  11.2 14.1 %copy-start.2 = (bf16[256,256]{1,0:T(8,128)(2,1)S(1)}, bf16[256,256]{1,0:T(8,128)(2,1)}, u32[]{:S(2)}) copy-start(bf16[256,256]{1,0:T(8,128)(2,1)} %out_weight_ref.1) | copy-start | bytes 393220
  11.2 14.1 %copy-start.5 = (bf16[256]{0:T(256)(128)(2,1)S(1)}, bf16[256]{0:T(256)(128)(2,1)}, u32[]{:S(2)}) copy-start(bf16[256]{0:T(256)(128)(2,1)} %refs_0_.3) | copy-start | bytes 1540
  11.2 14.1 %copy-start.6 = (bf16[256]{0:T(256)(128)(2,1)S(1)}, bf16[256]{0:T(256)(128)(2,1)}, u32[]{:S(2)}) copy-start(bf16[256]{0:T(256)(128)(2,1)} %refs_1_.1) | copy-start | bytes 1540
  11.2 12.0 %collective-permute-start.5 = (bf16[1,8,16,256]{3,2,1,0:T(8,128)(2,1)S(1)}, bf16[1,8,16,256]{3,2,1,0:T(8,128)(2,1)S(1)}, u32[]{:S(2)}, u32[]{:S(2)}) collective-permute-start(bf16[1,8,16,256]{3,2,1,0:T(8,128)(2,1)S(1)} %collective-permute-done.1), channel_id=1, source_target_pairs={{0,2},{1,3},{2,0},{3,1},{4,6},{5,7},{6,4},{7,5},{8,10},{9,11},{10,... | collective-permute-start | bytes 196616 | tf_op jit(solution)/shard_map/ppermute | solution.py:100
  11.8 11.4 %collective-permute-start.6 = (bf16[1,8,16,256]{3,2,1,0:T(8,128)(2,1)S(1)}, bf16[1,8,16,256]{3,2,1,0:T(8,128)(2,1)S(1)}, u32[]{:S(2)}, u32[]{:S(2)}) collective-permute-start(bf16[1,8,16,256]{3,2,1,0:T(8,128)(2,1)S(1)} %collective-permute-done.2), channel_id=1, source_target_pairs={{0,2},{1,3},{2,0},{3,1},{4,6},{5,7},{6,4},{7,5},{8,10},{9,11},{10,... | collective-permute-start | bytes 196616 | tf_op jit(solution)/shard_map/ppermute | solution.py:100
  13.5 9.8 %collective-permute-start.7 = (bf16[1,8,16,256]{3,2,1,0:T(8,128)(2,1)S(1)}, bf16[1,8,16,256]{3,2,1,0:T(8,128)(2,1)S(1)}, u32[]{:S(2)}, u32[]{:S(2)}) collective-permute-start(bf16[1,8,16,256]{3,2,1,0:T(8,128)(2,1)S(1)} %collective-permute-done.3), channel_id=1, source_target_pairs={{0,2},{1,3},{2,0},{3,1},{4,6},{5,7},{6,4},{7,5},{8,10},{9,11},{10,... | collective-permute-start | bytes 196616 | tf_op jit(solution)/shard_map/ppermute | solution.py:100
  17.0 20.7 %all-to-all-start = ((bf16[64,16,256]{2,1,0:T(8,128)(2,1)}), bf16[64,16,256]{2,1,0:T(8,128)(2,1)S(1)}, u32[]{:S(2)}, u32[]{:S(2)}) async-start(bf16[64,16,256]{2,1,0:T(8,128)(2,1)} %pick_joint.1), calls=%async_computation | async-start | bytes 1048576 | tf_op jit(solution)/shard_map/all_to_all | solution.py:334
  23.3 2.0 %collective-permute-start.8 = (bf16[8,8,16,256]{3,2,1,0:T(8,128)(2,1)S(1)}, bf16[8,8,16,256]{3,2,1,0:T(8,128)(2,1)S(1)}, u32[]{:S(2)}, u32[]{:S(2)}) collective-permute-start(bf16[8,8,16,256]{3,2,1,0:T(8,128)(2,1)S(1)} %constant_dynamic-update-slice_fusion.near_ref), channel_id=1, source_target_pairs={{0,1},{1,0},{2,3},{3,2},{4,5},{5,4},{6,7},{7,6},{8,9},{9,8},{10,11... | collective-permute-start | bytes 1572872 | tf_op jit(solution)/shard_map/ppermute | solution.py:100
  23.8 0.8 %copy-start = (bf16[8,8,16,256]{3,2,1,0:T(8,128)(2,1)}, bf16[8,8,16,256]{3,2,1,0:T(8,128)(2,1)S(1)}, u32[]{:S(2)}) copy-start(bf16[8,8,16,256]{3,2,1,0:T(8,128)(2,1)S(1)} %constant_dynamic-update-slice_fusion.near_ref) | copy-start | bytes 1572868
  25.3 1.0 %copy-start.1 = (bf16[8,8,16,256]{3,2,1,0:T(8,128)(2,1)S(1)}, bf16[8,8,16,256]{3,2,1,0:T(8,128)(2,1)}, u32[]{:S(2)}) copy-start(bf16[8,8,16,256]{3,2,1,0:T(8,128)(2,1)} %copy-done) | copy-start | bytes 1572868
  26.4 0.7 %copy-start.7 = (bf16[256]{0:T(256)(128)(2,1)S(1)}, bf16[256]{0:T(256)(128)(2,1)}, u32[]{:S(2)}) copy-start(bf16[256]{0:T(256)(128)(2,1)} %refs_2_.1) | copy-start | bytes 1540
  27.0 0.7 %copy-start.8 = (bf16[256]{0:T(256)(128)(2,1)S(1)}, bf16[256]{0:T(256)(128)(2,1)}, u32[]{:S(2)}) copy-start(bf16[256]{0:T(256)(128)(2,1)} %refs_3_.1) | copy-start | bytes 1540
  42.2 8.8 %collective-permute-start.13 = (bf16[2,2,4,16,256]{4,3,2,1,0:T(8,128)(2,1)S(1)}, bf16[2,2,4,16,256]{4,3,2,1,0:T(8,128)(2,1)S(1)}, u32[]{:S(2)}, u32[]{:S(2)}) collective-permute-start(bf16[2,2,4,16,256]{4,3,2,1,0:T(8,128)(2,1)S(1)} %get-tuple-element.19), channel_id=1, source_target_pairs={{0,4},{1,5},{2,6},{3,7},{4,0},{5,1},{6,2},{7,3},{8,12},{9,13},{10,... | collective-permute-start | bytes 393224 | tf_op jit(solution)/shard_map/ppermute | solution.py:263
  43.4 10.5 %collective-permute-start.9 = (bf16[2,4,16,256]{3,2,1,0:T(8,128)(2,1)S(1)}, bf16[2,4,16,256]{3,2,1,0:T(8,128)(2,1)S(1)}, u32[]{:S(2)}, u32[]{:S(2)}) collective-permute-start(bf16[2,4,16,256]{3,2,1,0:T(8,128)(2,1)S(1)} %get-tuple-element.15), channel_id=1, source_target_pairs={{0,8},{1,9},{2,10},{3,11},{4,12},{5,13},{6,14},{7,15},{8,0},{9,1},... | collective-permute-start | bytes 196616 | tf_op jit(solution)/shard_map/ppermute | solution.py:263
  44.6 12.3 %collective-permute-start.10 = (bf16[2,4,16,256]{3,2,1,0:T(8,128)(2,1)S(1)}, bf16[2,4,16,256]{3,2,1,0:T(8,128)(2,1)S(1)}, u32[]{:S(2)}, u32[]{:S(2)}) collective-permute-start(bf16[2,4,16,256]{3,2,1,0:T(8,128)(2,1)S(1)} %get-tuple-element.16), channel_id=1, source_target_pairs={{0,10},{1,11},{2,8},{3,9},{4,14},{5,15},{6,12},{7,13},{8,2},{9,3},... | collective-permute-start | bytes 196616 | tf_op jit(solution)/shard_map/ppermute | solution.py:263
  47.0 9.9 %collective-permute-start.11 = (bf16[2,4,16,256]{3,2,1,0:T(8,128)(2,1)S(1)}, bf16[2,4,16,256]{3,2,1,0:T(8,128)(2,1)S(1)}, u32[]{:S(2)}, u32[]{:S(2)}) collective-permute-start(bf16[2,4,16,256]{3,2,1,0:T(8,128)(2,1)S(1)} %get-tuple-element.17), channel_id=1, source_target_pairs={{0,12},{1,13},{2,14},{3,15},{4,8},{5,9},{6,10},{7,11},{8,4},{9,5},... | collective-permute-start | bytes 196616 | tf_op jit(solution)/shard_map/ppermute | solution.py:263
  48.0 8.9 %collective-permute-start.12 = (bf16[2,4,16,256]{3,2,1,0:T(8,128)(2,1)S(1)}, bf16[2,4,16,256]{3,2,1,0:T(8,128)(2,1)S(1)}, u32[]{:S(2)}, u32[]{:S(2)}) collective-permute-start(bf16[2,4,16,256]{3,2,1,0:T(8,128)(2,1)S(1)} %get-tuple-element.18), channel_id=1, source_target_pairs={{0,14},{1,15},{2,12},{3,13},{4,10},{5,11},{6,8},{7,9},{8,6},{9,7},... | collective-permute-start | bytes 196616 | tf_op jit(solution)/shard_map/ppermute | solution.py:263
  51.1 7.1 %collective-permute-start.14 = (bf16[2,2,4,16,256]{4,3,2,1,0:T(8,128)(2,1)S(1)}, bf16[2,2,4,16,256]{4,3,2,1,0:T(8,128)(2,1)S(1)}, u32[]{:S(2)}, u32[]{:S(2)}) collective-permute-start(bf16[2,2,4,16,256]{4,3,2,1,0:T(8,128)(2,1)S(1)} %pad_maximum_fusion), channel_id=1, source_target_pairs={{0,2},{1,3},{2,0},{3,1},{4,6},{5,7},{6,4},{7,5},{8,10},{9,11},{10,... | collective-permute-start | bytes 393224 | tf_op jit(solution)/shard_map/ppermute | solution.py:263
  58.2 1.6 %collective-permute-start.15 = (bf16[8,4,16,256]{3,2,1,0:T(8,128)(2,1)S(1)}, bf16[8,4,16,256]{3,2,1,0:T(8,128)(2,1)S(1)}, u32[]{:S(2)}, u32[]{:S(2)}) collective-permute-start(bf16[8,4,16,256]{3,2,1,0:T(8,128)(2,1)S(1)} %constant_dynamic-update-slice_fusion.8), channel_id=1, source_target_pairs={{0,1},{1,0},{2,3},{3,2},{4,5},{5,4},{6,7},{7,6},{8,9},{9,8},{10,11... | collective-permute-start | bytes 786440 | tf_op jit(solution)/shard_map/ppermute | solution.py:263

commit v7 on v6

--- a/solution.py
+++ b/solution.py
@@ -11,17 +11,29 @@
 cores = 2
 
 
-def pick_kernel(owners, pairs_ref, first_ref, gap_ref, *refs):
-    blocks, (out_ref, held, sems) = refs[:owners], refs[-3:]
+def piece_of(refs, flip):
+    chip, core = flip // cores, flip % cores
+    if chip < 4:
+        return refs[chip // 2].at[chip % 2, core]
+    return refs[chip - 2].at[core]
+
+
+def piece_shapes(members, rows, block, channels):
+    one = (cores, rows, block, channels)
+    shapes = [(2, *one)] * 2 + [one] * (members // cores - 4)
+    return [jax.ShapeDtypeStruct(shape, jnp.bfloat16) for shape in shapes]
+
+
+def pick_kernel(owners, members, pairs_ref, first_ref, gap_ref, *refs):
+    blocks, out_refs = refs[:owners], refs[-(members // cores - 2) :]
     local_rows, local_columns, channels = blocks[0].shape
-    part_rows = out_ref.shape[0]
-    pieces = sems.shape[0]
-    piece_rows = part_rows // pieces
+    rows = local_rows // members
     chains = first_ref.shape[0]
     shift = local_rows.bit_length() - 1
     assert local_rows == 1 << shift
     me = lax.axis_index("rows")
-    start = lax.axis_index("res") * local_columns
+    place = lax.axis_index("res")
+    start = place * local_columns
     low, high = jnp.int32(0), jnp.int32(0)
     for k in range(1, chains):
         low += (first_ref[k] <= start).astype(jnp.int32)
@@ -40,33 +52,27 @@
             found = jnp.where(owner == names[k], blocks[k][within].astype(jnp.float32), found)
         return jnp.where(row >= 0, found, gap)
 
-    copies = []
-    for k in range(pieces):
-        rows = pl.ds(k * piece_rows, piece_rows)
-        for row in range(k * piece_rows, (k + 1) * piece_rows):
+    for flip in range(members):
+        first_row = (place ^ flip) * rows
+        for i in range(rows):
+            row = first_row + i
             both = jnp.where(in_high, cells(pairs_ref[high, row]), cells(pairs_ref[low, row]))
-            held[row] = both.astype(jnp.bfloat16)
-        copies.append(pltpu.make_async_copy(held.at[rows], out_ref.at[rows], sems.at[k]))
-        copies[-1].start()
-    for copy in copies:
-        copy.wait()
-
-
-def pick(pairs, chain_first_residue, gap, blocks, earlier):
+            piece_of(out_refs, flip)[i] = both.astype(jnp.bfloat16)
+
+
+def pick(members, pairs, chain_first_residue, gap, blocks, earlier):
     owners = len(blocks)
     local_rows, local_columns, channels = blocks[0].shape
-    pieces = 2
     smem = pl.BlockSpec(memory_space=pltpu.SMEM)
     vmem = pl.BlockSpec(memory_space=pltpu.VMEM)
     anywhere = pl.BlockSpec(memory_space=pl.ANY)
     block_bytes = local_rows * local_columns * channels * 2
-    shape = blocks[0].shape
-    return pl.pallas_call(
-        functools.partial(pick_kernel, owners),
-        out_shape=jax.ShapeDtypeStruct(shape, jnp.bfloat16),
+    shapes = piece_shapes(members, local_rows // members, local_columns, channels)
+    return pl.pallas_call(
+        functools.partial(pick_kernel, owners, members),
+        out_shape=shapes,
         in_specs=[smem, smem, vmem] + [vmem] * owners + [anywhere] * len(earlier),
-        out_specs=anywhere,
-        scratch_shapes=[pltpu.VMEM(shape, jnp.bfloat16), pltpu.SemaphoreType.DMA((pieces,))],
+        out_specs=[vmem] * len(shapes),
         compiler_params=pltpu.CompilerParams(vmem_limit_bytes=(owners + 4) * block_bytes),
         name="pick_joint",
     )(pairs, chain_first_residue, gap, *blocks, *earlier)
@@ -75,14 +81,16 @@
 def bias_kernel(order, near_ref, far_ref, *refs):
     rows, gate_ref, (out_ref, vectors_ref, held) = refs[:3], refs[3], refs[-3:]
     me = lax.axis_index("res")
-    half, heads, block, _ = near_ref.shape
+    half, heads, block, keys = near_ref.shape
     for place, flip in enumerate(order):
         source = near_ref if place < half else far_ref
-        first = pl.multiple_of((me ^ flip) * block, block)
-        held[:, pl.ds(first, block), :] = source[place % half].astype(jnp.float32)
+        held[:, flip * block : (flip + 1) * block, :] = source[place % half].astype(jnp.float32)
 
     def one_head(h, carry):
-        out_ref[h] = held[h].T
+        turned = held[h].T
+        for owner in range(keys // block):
+            first = pl.multiple_of((me ^ owner) * block, block)
+            out_ref[h, pl.ds(first, block), :] = turned[owner * block : (owner + 1) * block]
         return carry
 
     lax.fori_loop(0, heads, one_head, 0)
@@ -93,26 +101,36 @@
     vectors_ref[8:] = jnp.broadcast_to(gate, (width, width)).T
 
 
-def gather_bias(shard):
-    members = lax.axis_size("res")
-
-    def swap(piece, flip):
-        return lax.ppermute(piece, "res", [(i, i ^ flip) for i in range(members)])
-
-    far, next_far = members // 2, members // 4
+def gather_lines(shard):
+    far, next_far = lax.axis_size("res") // 2, lax.axis_size("res") // 4
     shard = shard[None]
-    pieces = [shard]
-    order = [0]
-    for flip in (far, next_far, far + next_far):
-        pieces.append(swap(shard, flip))
-        order.append(flip)
-    flip = members // 8
-    while flip > 1:
-        pieces += [swap(piece, flip) for piece in pieces]
-        order += [place ^ flip for place in order]
+    order = [0, far, next_far, far + next_far]
+    return jnp.concatenate([shard, *(swap(shard, flip) for flip in order[1:])], axis=0), order
+
+
+def gather_bias(held, order):
+    flip = lax.axis_size("res") // 8
+    while flip >= cores:
+        held = jnp.concatenate([held, swap(held, flip)], axis=0)
+        order = order + [flip ^ place for place in order]
         flip //= 2
-    near = jnp.concatenate(pieces, axis=0)
-    return near, swap(near, 1), order + [place ^ 1 for place in order]
+    return held, swap(held, 1), order + [1 ^ place for place in order]
+
+
+def same_kernel(*refs):
+    pass
+
+
+def after(array, *earlier):
+    anywhere = pl.BlockSpec(memory_space=pl.ANY)
+    return pl.pallas_call(
+        same_kernel,
+        out_shape=jax.ShapeDtypeStruct(array.shape, array.dtype),
+        in_specs=[anywhere] * (1 + len(earlier)),
+        out_specs=anywhere,
+        input_output_aliases={0: 0},
+        name="same_cells",
+    )(array, *earlier)
 
 
 def order_bias(near, other, order, vectors, earlier):
@@ -160,10 +178,21 @@
     )(projection_weight.reshape(channels, heads * four))
 
 
-def attend_kernel(cells_ref, weights_ref, out_weight_ref, vectors_ref, bias_ref, *refs):
-    near_refs, far_refs, (staged_ref, scores_ref) = refs[:2], refs[2:-2], refs[-2:]
-    senders, rows, block, channels = cells_ref.shape
-    me = lax.axis_index("res")
+def arrived_from(order, refs, flip):
+    far_refs, (there_ref, hop_ref, here_ref, other_ref) = refs[:-4], refs[-4:]
+    chip, core = flip // cores, flip % cores
+    if core:
+        return other_ref.at[order.index(chip)]
+    if chip >= 4:
+        return far_refs[chip - 4].at[0]
+    near = (here_ref.at[0, 0], hop_ref.at[0, 0], there_ref.at[0, 0], hop_ref.at[1, 0])
+    return near[chip]
+
+
+def attend_kernel(order, weights_ref, out_weight_ref, vectors_ref, bias_ref, *refs):
+    arrived, out_refs, scores_ref = refs[: len(order)], refs[len(order) : -1], refs[-1]
+    senders = len(order) * cores
+    rows, block, channels = arrived_from(order, arrived, 0).shape
     residues = senders * block
     heads = bias_ref.shape[0]
     width = weights_ref.shape[0] // 4
@@ -174,7 +203,8 @@
     masks = [(head_of == h).astype(jnp.bfloat16) for h in range(group // depth)]
 
     def begin(r):
-        wide = cells_ref[:, r].reshape(residues, channels).astype(jnp.float32)
+        wide = [arrived_from(order, arrived, flip)[r] for flip in range(senders)]
+        wide = jnp.concatenate(wide, axis=0).astype(jnp.float32)
         center = jnp.mean(wide, axis=-1, keepdims=True)
         wide = wide - center
         spread = jnp.mean(jnp.square(wide), axis=-1, keepdims=True)
@@ -215,13 +245,8 @@
         attended = jnp.concatenate(heads_out, axis=0).T
         update = jnp.dot(attended, out_weight_ref[...], preferred_element_type=jnp.float32)
         update = (update + vectors_ref[2:3]).astype(jnp.bfloat16)
-        staged_ref[...] = update.reshape(senders, block, channels)
         for flip in range(senders):
-            chip, core = flip // cores, flip % cores
-            if chip < 4:
-                near_refs[chip // 2][chip % 2, core, r] = staged_ref[me ^ flip]
-            else:
-                far_refs[chip - 4][core, r] = staged_ref[me ^ flip]
+            piece_of(out_refs, flip)[r] = update[flip * block : (flip + 1) * block]
 
     begun = {0: begin(0)}
     done = {r: [] for r in range(rows)}
@@ -235,27 +260,23 @@
     finish(rows - 1, done[rows - 1])
 
 
-def attend(cells, weights, out_weight, vectors, bias):
+def attend(order, arrived, weights, out_weight, vectors, bias):
     heads, residues, _ = bias.shape
-    senders, rows, block, channels = cells.shape
+    rows, block, channels = arrived[-1].shape[1:]
     width = weights.shape[0] // 4
     group = min(128, width)
     vmem = pl.BlockSpec(memory_space=pltpu.VMEM)
     score_shape = (2, width // group, heads * group // width * residues, residues)
-    one = (cores, rows, block, channels)
-    shapes = [(2, *one)] * 2 + [one] * (senders // cores - 4)
-    return pl.pallas_call(
-        attend_kernel,
-        out_shape=[jax.ShapeDtypeStruct(shape, jnp.bfloat16) for shape in shapes],
-        in_specs=[vmem] * 5,
+    shapes = piece_shapes(residues // block, rows, block, channels)
+    return pl.pallas_call(
+        functools.partial(attend_kernel, order),
+        out_shape=shapes,
+        in_specs=[vmem] * (4 + len(arrived)),
         out_specs=[vmem] * len(shapes),
-        scratch_shapes=[
-            pltpu.VMEM((senders, block, channels), jnp.bfloat16),
-            pltpu.VMEM(score_shape, jnp.float32),
-        ],
+        scratch_shapes=[pltpu.VMEM(score_shape, jnp.float32)],
         compiler_params=pltpu.CompilerParams(vmem_limit_bytes=24 << 20),
         name="attend_rows",
-    )(cells, weights, out_weight, vectors, bias)
+    )(weights, out_weight, vectors, bias, *arrived)
 
 
 def swap(array, flip):
@@ -271,38 +292,38 @@
     arrived = [(2, there[0]), *((4 + k, piece) for k, piece in enumerate(far))]
     arrived += [(1, hop[0]), (3, hop[1]), (0, here[0])]
     other = swap(jnp.stack([blocks[1] for _, blocks in arrived]), 1)
-    return [chip for chip, _ in arrived], far, there, hop, here, other
+    return [chip for chip, _ in arrived], [*far, there, hop, here, other]
 
 
 def place_kernel(order, *refs):
-    far_refs, (there_ref, hop_ref, here_ref, other_ref, out_ref, sems) = refs[:-6], refs[-6:]
+    arrived, (out_ref, sems) = refs[:-2], refs[-2:]
     me = lax.axis_index("res")
-    rows = other_ref.shape[1]
-    near = [here_ref.at[0, 0], hop_ref.at[0, 0], there_ref.at[0, 0], hop_ref.at[1, 0]]
-    copies = []
-    for k, chip in enumerate(order):
-        same = near[chip] if chip < 4 else far_refs[chip - 4].at[0]
-        for core, source in enumerate((same, other_ref.at[k])):
-            first = (me ^ (chip * cores + core)) * rows
-            target = out_ref.at[pl.ds(first, rows)]
-            copies.append(pltpu.make_async_copy(source, target, sems.at[len(copies)]))
+    rows = arrived[-1].shape[1]
+    copies = [
+        pltpu.make_async_copy(
+            arrived_from(order, arrived, flip),
+            out_ref.at[pl.ds((me ^ flip) * rows, rows)],
+            sems.at[flip],
+        )
+        for flip in range(len(order) * cores)
+    ]
     for copy in copies:
         copy.start()
     for copy in copies:
         copy.wait()
 
 
-def place(order, far, there, hop, here, other, shape):
+def place(order, arrived, shape):
     vmem = pl.BlockSpec(memory_space=pltpu.VMEM)
     return pl.pallas_call(
         functools.partial(place_kernel, order),
         out_shape=jax.ShapeDtypeStruct(shape, jnp.bfloat16),
-        in_specs=[vmem] * (len(far) + 4),
+        in_specs=[vmem] * len(arrived),
         out_specs=pl.BlockSpec(memory_space=pl.ANY),
         scratch_shapes=[pltpu.SemaphoreType.DMA((cores * len(order),))],
         compiler_params=pltpu.CompilerParams(vmem_limit_bytes=8 << 20),
         name="place_rows",
-    )(*far, there, hop, here, other)
+    )(*arrived)
 
 
 def local(
@@ -321,7 +342,7 @@
     local_rows, local_columns, channels = source_alignment_rows.shape
     owners = lax.axis_size("rows")
     members = lax.axis_size("res")
-    near, other, order = gather_bias(pair_bias_logits)
+    held, lines = gather_lines(pair_bias_logits)
     blocks = [source_alignment_rows]
     for hop in range(1, owners):
         blocks.append(
@@ -330,8 +351,9 @@
             )
         )
     weights = turn_weights(projection_weight)
-    joint = pick(pairs, chain_first_residue, gap_embedding, blocks, (weights,))
-    cells = lax.all_to_all(joint, "res", split_axis=0, concat_axis=0, tiled=True)
+    picked = pick(members, pairs, chain_first_residue, gap_embedding, blocks, (weights,))
+    chips, cells = spread(picked)
+    near, other, order = gather_bias(after(held, picked[0]), lines)
     bias, vectors = order_bias(
         near,
         other,
@@ -339,8 +361,7 @@
         (layer_norm_gain, layer_norm_bias, output_bias, gate_bias_heads),
         (weights, output_weight),
     )
-    cells = cells.reshape(members, local_rows // members, local_columns, channels)
-    pieces = attend(cells, weights, output_weight, vectors, bias)
+    pieces = attend(chips, cells, weights, output_weight, vectors, bias)
     return place(*spread(pieces), (local_rows, local_columns, channels))
 
 

time: 61.1 us -> 61.2 us (level)
  local copies, waits for them, and re-layouts: 5.3 us -> 2.02 us
  other arithmetic: 0.02 us -> 1.77 us
  waiting for transfers between devices: 17 us -> 18.5 us
  starting transfers between devices: 29.4 us -> 30.1 us
    ppermute x7 -> x19, starting transfers between devices: 10.2 us -> 27.1 us  [swap(): return lax.ppermute(array, 'res', [(i, i ^ flip) for i in range(members)])]
    ppermute x8 -> x0, starting transfers between devices: 9.99 us -> none  [swap(): return lax.ppermute(piece, 'res', [(i, i ^ flip) for i in range(members)])]
    all_to_all x1 -> x0, waiting for transfers between devices: 8.69 us -> none  [local(): lax.all_to_all(joint, 'res', split_axis=0, concat_axis=0, tiled=True)]
    all_to_all x1 -> x0, starting transfers between devices: 6.2 us -> none  [local(): lax.all_to_all(joint, 'res', split_axis=0, concat_axis=0, tiled=True)]
    ppermute x1, waiting for transfers between devices: 0.16 us -> 6.3 us  [local(): lax.ppermute(source_alignment_rows, 'rows', [(i, (i + hop) % owners) for...]
    ppermute x7 -> x19, waiting for transfers between devices: 7.25 us -> 12.2 us  [swap(): return lax.ppermute(array, 'res', [(i, i ^ flip) for i in range(members)])]
    unnamed x37 -> x39, local copies, waits for them, and re-layouts: 5.28 us -> 1.24 us
    concatenate x0 -> x2, other arithmetic: none -> 1.74 us  [the longest x1 1 us: gather_bias(): held = jnp.concatenate([held, swap(held, flip)], axis=0)]
  transfers between devices with their start and end apart: 17 -> 20, of which waited for: 8 -> 10; matrix products, arithmetic and copies ran while one was open for 3% -> 6% of each run, Pallas kernels for 5% -> 5%
where the time goes in v7:
time: 61.2 us; the launch traced here: 61 us
  starting transfers between devices  30.1 us (49%)
  waiting for transfers between devices  18.5 us (30%)
  Pallas kernels  8.27 us (14%)
  local copies, waits for them, and re-layouts  2.02 us (3%)
  other arithmetic  1.77 us (3%)
    ppermute x19, starting transfers between devices, swap(): return lax.ppermute(array, 'res', [(i, i ^ flip) for i in range(members)])  27.1 us
    ppermute x19, waiting for transfers between devices, swap(): return lax.ppermute(array, 'res', [(i, i ^ flip) for i in range(members)])  12.2 us
    ppermute x1, waiting for transfers between devices, local(): lax.ppermute(source_alignment_rows, 'rows', [(i, (i + hop) % owners) for...  6.3 us
    pallas_call x1, Pallas kernels, attend(): pl.pallas_call(functools.partial(attend_kernel, order), out_shape=shapes,...  4.54 us
    ppermute x1, starting transfers between devices, local(): lax.ppermute(source_alignment_rows, 'rows', [(i, (i + hop) % owners) for...  3.02 us
    pallas_call x1, Pallas kernels, order_bias(): pl.pallas_call(functools.partial(bias_kernel, order), out_shape=[jax.Shap...  1.37 us
    unnamed x39, local copies, waits for them, and re-layouts  1.24 us
  transfers between devices with their start and end apart: 20, of which 10 were waited for; matrix products, arithmetic and copies ran while one was open for 6% of the time, Pallas kernels for 5%

profile of v7, /device:TPU:0, one launch (start us, length us, event | category | flops | bytes accessed | tf_op | source)
XLA Modules:
  0.0 61.0 jit_solution(2217492524730026540)
XLA Ops:
  0.0 3.0 %collective-permute-start.3 = (bf16[64,16,256]{2,1,0:T(8,128)(2,1)}, bf16[64,16,256]{2,1,0:T(8,128)(2,1)S(1)}, u32[]{:S(2)}, u32[]{:S(2)}) collective-permute-start(bf16[64,16,256]{2,1,0:T(8,128)(2,1)} %refs_0_.2), channel_id=1, source_target_pairs={{0,16},{16,0},{1,17},{17,1},{2,18},{18,2},{3,19},{19,3},{4,20},{20... | collective-permute-start | bytes 1572872 | tf_op jit(solution)/shard_map/ppermute | solution.py:349
  3.0 2.6 %collective-permute-start = (bf16[1,8,16,256]{3,2,1,0:T(8,128)(2,1)}, bf16[1,8,16,256]{3,2,1,0:T(8,128)(2,1)S(1)}, u32[]{:S(2)}, u32[]{:S(2)}) collective-permute-start(bf16[1,8,16,256]{3,2,1,0:T(8,128)(2,1)} %bitcast.35), channel_id=1, source_target_pairs={{0,8},{1,9},{2,10},{3,11},{4,12},{5,13},{6,14},{7,15},{8,0},{9,1},... | collective-permute-start | bytes 196616 | tf_op jit(solution)/shard_map/ppermute | solution.py:284
  5.6 1.6 %collective-permute-start.1 = (bf16[1,8,16,256]{3,2,1,0:T(8,128)(2,1)}, bf16[1,8,16,256]{3,2,1,0:T(8,128)(2,1)S(1)}, u32[]{:S(2)}, u32[]{:S(2)}) collective-permute-start(bf16[1,8,16,256]{3,2,1,0:T(8,128)(2,1)} %bitcast.36), channel_id=1, source_target_pairs={{0,4},{1,5},{2,6},{3,7},{4,0},{5,1},{6,2},{7,3},{8,12},{9,13},{10,... | collective-permute-start | bytes 196616 | tf_op jit(solution)/shard_map/ppermute | solution.py:284
  7.2 0.2 collective-permute-start.2
  7.4 1.1 %copy.15 = bf16[32,8,8,128]{3,1,2,0:T(8,128)(2,1)S(1)} copy(bf16[32,8,8,128]{3,2,1,0:T(8,128)(2,1)} %bitcast.34) | data formatting | bytes 1048576
  8.6 0.2 turn_weights.1.refs_2_.refs_4_.weights_ref
  8.8 0.0 copy-start.3
  8.8 0.0 copy-start.7
  8.8 0.0 copy-start.8
  8.8 0.0 copy-start.9
  8.9 0.0 copy-start.10
  8.9 6.3 %collective-permute-done.3.refs_1_ = bf16[64,16,256]{2,1,0:T(8,128)(2,1)S(1)} collective-permute-done((bf16[64,16,256]{2,1,0:T(8,128)(2,1)}, bf16[64,16,256]{2,1,0:T(8,128)(2,1)S(1)}, u32[]{:S(2)}, u32[]{:S(2)}) %collective-permute-start.3) | collective-permute-done | bytes 524320 | tf_op jit(solution)/shard_map/ppermute | solution.py:349
  15.2 1.2 %pick_joint.1 = (bf16[2,2,4,16,256]{4,3,2,1,0:T(8,128)(2,1)S(1)}, bf16[2,2,4,16,256]{4,3,2,1,0:T(8,128)(2,1)S(1)}, bf16[2,4,16,256]{3,2,1,0:T(8,128)(2,1)S(1)}, ...) custom-call(s32[6,64]{1,0:T(8,128)S(1)} %copy-done.4, ...), custom_call_target="tpu_custom_call" | custom-call | tf_op jit(solution)/shard_map/pick_joint/pallas_call | solution.py:71
  16.4 1.9 %collective-permute-start.10 = (bf16[2,2,4,16,256]{4,3,2,1,0:T(8,128)(2,1)S(1)}, bf16[2,2,4,16,256]{4,3,2,1,0:T(8,128)(2,1)S(1)}, u32[]{:S(2)}, u32[]{:S(2)}) collective-permute-start(bf16[2,2,4,16,256]{4,3,2,1,0:T(8,128)(2,1)S(1)} %get-tuple-element.26), channel_id=1, source_target_pairs={{0,4},{1,5},{2,6},{3,7},{4,0},{5,1},{6,2},{7,3},{8,12},{9,13},{10,... | collective-permute-start | bytes 393224 | tf_op jit(solution)/shard_map/ppermute | solution.py:284
  18.3 0.0 collective-permute-done.1
  18.3 0.0 collective-permute-done.2
  18.3 0.7 %pad_maximum_fusion.1.refs_0_ = bf16[4,8,16,256]{3,2,1,0:T(8,128)(2,1)} fusion(bf16[1,8,16,256]{3,2,1,0:T(8,128)(2,1)S(1)} %collective-permute-done.2, bf16[1,8,16,256]{3,2,1,0:T(8,128)(2,1)S(1)} %collective-permute-done.1, bf16[1,8,16,256]{3,2,1,0:T(8,128)(2,1)S(1)} %collective-permute-done, bf16[1,8,16,256]{3,2,1,0:T(8,128)(2,1)S(1)} %bitcast.38), kind=kLoop, calls=%fused_computation.2 | loop fusion | flops 393216 | bytes 524288 | tf_op jit(solution)/shard_map/concatenate | solution.py:108
  19.1 1.6 %collective-permute-start.4 = (bf16[4,8,16,256]{3,2,1,0:T(8,128)(2,1)}, bf16[4,8,16,256]{3,2,1,0:T(8,128)(2,1)S(1)}, u32[]{:S(2)}, u32[]{:S(2)}) collective-permute-start(bf16[4,8,16,256]{3,2,1,0:T(8,128)(2,1)} %same_cells.1), channel_id=1, source_target_pairs={{0,2},{1,3},{2,0},{3,1},{4,6},{5,7},{6,4},{7,5},{8,10},{9,11},{10,... | collective-permute-start | bytes 786440 | tf_op jit(solution)/shard_map/ppermute | solution.py:284
  20.7 2.6 %collective-permute-start.6 = (bf16[2,4,16,256]{3,2,1,0:T(8,128)(2,1)S(1)}, bf16[2,4,16,256]{3,2,1,0:T(8,128)(2,1)S(1)}, u32[]{:S(2)}, u32[]{:S(2)}) collective-permute-start(bf16[2,4,16,256]{3,2,1,0:T(8,128)(2,1)S(1)} %get-tuple-element.22), channel_id=1, source_target_pairs={{0,8},{1,9},{2,10},{3,11},{4,12},{5,13},{6,14},{7,15},{8,0},{9,1},... | collective-permute-start | bytes 196616 | tf_op jit(solution)/shard_map/ppermute | solution.py:284
  23.3 0.3 collective-permute-start.7
  23.5 2.5 %collective-permute-start.8 = (bf16[2,4,16,256]{3,2,1,0:T(8,128)(2,1)S(1)}, bf16[2,4,16,256]{3,2,1,0:T(8,128)(2,1)S(1)}, u32[]{:S(2)}, u32[]{:S(2)}) collective-permute-start(bf16[2,4,16,256]{3,2,1,0:T(8,128)(2,1)S(1)} %get-tuple-element.24), channel_id=1, source_target_pairs={{0,12},{1,13},{2,14},{3,15},{4,8},{5,9},{6,10},{7,11},{8,4},{9,5},... | collective-permute-start | bytes 196616 | tf_op jit(solution)/shard_map/ppermute | solution.py:284
  26.0 0.0 collective-permute-done.10.refs_4_
  26.0 2.3 %collective-permute-start.9 = (bf16[2,4,16,256]{3,2,1,0:T(8,128)(2,1)S(1)}, bf16[2,4,16,256]{3,2,1,0:T(8,128)(2,1)S(1)}, u32[]{:S(2)}, u32[]{:S(2)}) collective-permute-start(bf16[2,4,16,256]{3,2,1,0:T(8,128)(2,1)S(1)} %get-tuple-element.25), channel_id=1, source_target_pairs={{0,14},{1,15},{2,12},{3,13},{4,10},{5,11},{6,8},{7,9},{8,6},{9,7},... | collective-permute-start | bytes 196616 | tf_op jit(solution)/shard_map/ppermute | solution.py:284
  28.4 0.6 collective-permute-done.6.refs_0_
  29.0 0.0 collective-permute-start.11
  29.0 3.2 %collective-permute-done.7.refs_1_ = bf16[2,4,16,256]{3,2,1,0:T(8,128)(2,1)S(1)} collective-permute-done((bf16[2,4,16,256]{3,2,1,0:T(8,128)(2,1)S(1)}, bf16[2,4,16,256]{3,2,1,0:T(8,128)(2,1)S(1)}, u32[]{:S(2)}, u32[]{:S(2)}) %collective-permute-start.7) | collective-permute-done | bytes 65568 | tf_op jit(solution)/shard_map/ppermute | solution.py:284
  32.2 0.0 collective-permute-done.8.refs_2_
  32.2 1.0 %collective-permute-done.9.refs_3_ = bf16[2,4,16,256]{3,2,1,0:T(8,128)(2,1)S(1)} collective-permute-done((bf16[2,4,16,256]{3,2,1,0:T(8,128)(2,1)S(1)}, bf16[2,4,16,256]{3,2,1,0:T(8,128)(2,1)S(1)}, u32[]{:S(2)}, u32[]{:S(2)}) %collective-permute-start.9) | collective-permute-done | bytes 65568 | tf_op jit(solution)/shard_map/ppermute | solution.py:284
  33.2 1.0 %pad_maximum_fusion.near_ref = bf16[8,8,16,256]{3,2,1,0:T(8,128)(2,1)S(1)} fusion(bf16[4,8,16,256]{3,2,1,0:T(8,128)(2,1)S(1)} %collective-permute-done.4, bf16[4,8,16,256]{3,2,1,0:T(8,128)(2,1)} %same_cells.1), kind=kLoop, calls=%fused_computation.1 | loop fusion | flops 262144 | bytes 1048576 | tf_op jit(solution)/shard_map/concatenate | solution.py:114
  34.2 0.1 collective-permute-start.5
  34.2 0.3 collective-permute-done.11.refs_5_
  34.5 0.8 %constant_dynamic-update-slice_fusion = bf16[8,4,16,256]{3,2,1,0:T(8,128)(2,1)S(1)} fusion(bf16[8,4,16,256]{3,2,1,0:T(8,128)(2,1)S(1)} %constant_dynamic-update-slice_fusion.1, bf16[2,2,4,16,256]{4,3,2,1,0:T(8,128)(2,1)} %copy-done), kind=kLoop, calls=%fused_computation.5 | loop fusion | bytes 65536 | tf_op jit(solution)/shard_map/stack | solution.py:294
  35.3 0.2 collective-permute-start.12
  35.5 0.6 %collective-permute-done.5.far_ref = bf16[8,8,16,256]{3,2,1,0:T(8,128)(2,1)S(1)} collective-permute-done((bf16[8,8,16,256]{3,2,1,0:T(8,128)(2,1)S(1)}, bf16[8,8,16,256]{3,2,1,0:T(8,128)(2,1)S(1)}, u32[]{:S(2)}, u32[]{:S(2)}) %collective-permute-start.5) | collective-permute-done | bytes 524320 | tf_op jit(solution)/shard_map/ppermute | solution.py:284
  36.2 1.4 %order_bias.1 = (f32[8,256,256]{2,1,0:T(8,128)S(1)}, f32[264,256]{1,0:T(8,128)S(1)}) custom-call(bf16[8,8,16,256]{3,2,1,0:T(8,128)(2,1)S(1)} %pad_maximum_fusion.near_ref, bf16[8,8,16,256]{3,2,1,0:T(8,128)(2,1)S(1)} %collective-permute-done.5.far_ref, bf16[256]{0:T(256)(128)(2,1)S(1)} %copy-done.7, bf16[256]{0:T(256)(128)(2,1)S(1)} %copy-done.8, ...), custom_call_target="tpu_custom_call" | custom-call | tf_op jit(solution)/shard_map/order_bias/pallas_call | solution.py:141
  37.6 4.5 %attend_rows.1 = (bf16[2,2,4,16,256]{4,3,2,1,0:T(8,128)(2,1)S(1)}, bf16[2,2,4,16,256]{4,3,2,1,0:T(8,128)(2,1)S(1)}, bf16[2,4,16,256]{3,2,1,0:T(8,128)(2,1)S(1)},...) custom-call(bf16[1024,256]{1,0:T(8,128)(2,1)S(1)} %turn_weights.1.refs, ...), custom_call_target="tpu_custom_call" | custom-call | tf_op jit(solution)/shard_map/attend_rows/pallas_call | solution.py:271
  42.1 2.2 %collective-permute-start.17 = (bf16[2,2,4,16,256]{4,3,2,1,0:T(8,128)(2,1)S(1)}, bf16[2,2,4,16,256]{4,3,2,1,0:T(8,128)(2,1)S(1)}, u32[]{:S(2)}, u32[]{:S(2)}) collective-permute-start(bf16[2,2,4,16,256]{4,3,2,1,0:T(8,128)(2,1)S(1)} %get-tuple-element.31), channel_id=1, source_target_pairs={{0,4},{1,5},{2,6},{3,7},{4,0},{5,1},{6,2},{7,3},{8,12},{9,13},{10,... | collective-permute-start | bytes 393224 | tf_op jit(solution)/shard_map/ppermute | solution.py:284
  44.3 0.7 %collective-permute-start.13 = (bf16[2,4,16,256]{3,2,1,0:T(8,128)(2,1)S(1)}, bf16[2,4,16,256]{3,2,1,0:T(8,128)(2,1)S(1)}, u32[]{:S(2)}, u32[]{:S(2)}) collective-permute-start(bf16[2,4,16,256]{3,2,1,0:T(8,128)(2,1)S(1)} %get-tuple-element.27), channel_id=1, source_target_pairs={{0,8},{1,9},{2,10},{3,11},{4,12},{5,13},{6,14},{7,15},{8,0},{9,1},... | collective-permute-start | bytes 196616 | tf_op jit(solution)/shard_map/ppermute | solution.py:284
  45.0 2.9 %collective-permute-start.14 = (bf16[2,4,16,256]{3,2,1,0:T(8,128)(2,1)S(1)}, bf16[2,4,16,256]{3,2,1,0:T(8,128)(2,1)S(1)}, u32[]{:S(2)}, u32[]{:S(2)}) collective-permute-start(bf16[2,4,16,256]{3,2,1,0:T(8,128)(2,1)S(1)} %get-tuple-element.28), channel_id=1, source_target_pairs={{0,10},{1,11},{2,8},{3,9},{4,14},{5,15},{6,12},{7,13},{8,2},{9,3},... | collective-permute-start | bytes 196616 | tf_op jit(solution)/shard_map/ppermute | solution.py:284
  48.0 1.8 %collective-permute-start.15 = (bf16[2,4,16,256]{3,2,1,0:T(8,128)(2,1)S(1)}, bf16[2,4,16,256]{3,2,1,0:T(8,128)(2,1)S(1)}, u32[]{:S(2)}, u32[]{:S(2)}) collective-permute-start(bf16[2,4,16,256]{3,2,1,0:T(8,128)(2,1)S(1)} %get-tuple-element.29), channel_id=1, source_target_pairs={{0,12},{1,13},{2,14},{3,15},{4,8},{5,9},{6,10},{7,11},{8,4},{9,5},... | collective-permute-start | bytes 196616 | tf_op jit(solution)/shard_map/ppermute | solution.py:284
  49.8 2.2 %collective-permute-start.16 = (bf16[2,4,16,256]{3,2,1,0:T(8,128)(2,1)S(1)}, bf16[2,4,16,256]{3,2,1,0:T(8,128)(2,1)S(1)}, u32[]{:S(2)}, u32[]{:S(2)}) collective-permute-start(bf16[2,4,16,256]{3,2,1,0:T(8,128)(2,1)S(1)} %get-tuple-element.30), channel_id=1, source_target_pairs={{0,14},{1,15},{2,12},{3,13},{4,10},{5,11},{6,8},{7,9},{8,6},{9,7},... | collective-permute-start | bytes 196616 | tf_op jit(solution)/shard_map/ppermute | solution.py:284
  52.0 1.4 %collective-permute-start.18 = (bf16[2,2,4,16,256]{4,3,2,1,0:T(8,128)(2,1)S(1)}, bf16[2,2,4,16,256]{4,3,2,1,0:T(8,128)(2,1)S(1)}, u32[]{:S(2)}, u32[]{:S(2)}) collective-permute-start(bf16[2,2,4,16,256]{4,3,2,1,0:T(8,128)(2,1)S(1)} %pad_maximum_fusion.3), channel_id=1, source_target_pairs={{0,2},{1,3},{2,0},{3,1},{4,6},{5,7},{6,4},{7,5},{8,10},{9,11},{10,... | collective-permute-start | bytes 393224 | tf_op jit(solution)/shard_map/ppermute | solution.py:284
  53.4 1.7 %collective-permute-done.13.refs_0_ = bf16[2,4,16,256]{3,2,1,0:T(8,128)(2,1)S(1)} collective-permute-done((bf16[2,4,16,256]{3,2,1,0:T(8,128)(2,1)S(1)}, bf16[2,4,16,256]{3,2,1,0:T(8,128)(2,1)S(1)}, u32[]{:S(2)}, u32[]{:S(2)}) %collective-permute-start.13) | collective-permute-done | bytes 65568 | tf_op jit(solution)/shard_map/ppermute | solution.py:284
  55.1 2.9 %collective-permute-done.14.refs_1_ = bf16[2,4,16,256]{3,2,1,0:T(8,128)(2,1)S(1)} collective-permute-done((bf16[2,4,16,256]{3,2,1,0:T(8,128)(2,1)S(1)}, bf16[2,4,16,256]{3,2,1,0:T(8,128)(2,1)S(1)}, u32[]{:S(2)}, u32[]{:S(2)}) %collective-permute-start.14) | collective-permute-done | bytes 65568 | tf_op jit(solution)/shard_map/ppermute | solution.py:284
  58.0 0.5 collective-permute-done.18.refs_5_
  58.5 0.1 collective-permute-start.19
  58.5 1.5 %collective-permute-done.19.refs_7_ = bf16[8,4,16,256]{3,2,1,0:T(8,128)(2,1)S(1)} collective-permute-done((bf16[8,4,16,256]{3,2,1,0:T(8,128)(2,1)S(1)}, bf16[8,4,16,256]{3,2,1,0:T(8,128)(2,1)S(1)}, u32[]{:S(2)}, u32[]{:S(2)}) %collective-permute-start.19) | collective-permute-done | bytes 262176 | tf_op jit(solution)/shard_map/ppermute | solution.py:284
  60.1 0.9 %place_rows.1 = bf16[64,16,256]{2,1,0:T(8,128)(2,1)} custom-call(bf16[2,4,16,256]{3,2,1,0:T(8,128)(2,1)S(1)} %collective-permute-done.13.refs_0_, bf16[2,4,16,256]{3,2,1,0:T(8,128)(2,1)S(1)} %collective-permute-done.14.refs_1_, bf16[2,4,16,256]{3,2,1,0:T(8,128)(2,1)S(1)} %collective-permute-done.15.refs_2_, ...), custom_call_target="tpu_custom_call" | custom-call | tf_op jit(solution)/shard_map/place_rows/pallas_call | solution.py:318
  (47 shorter events, 0.2 us)
Async XLA Ops:
  0.0 15.2 %copy-start.2 = (bf16[64,16,256]{2,1,0:T(8,128)(2,1)S(1)}, bf16[64,16,256]{2,1,0:T(8,128)(2,1)}, u32[]{:S(2)}) copy-start(bf16[64,16,256]{2,1,0:T(8,128)(2,1)} %refs_0_.2) | copy-start | bytes 1572868
  0.0 18.3 %copy-start.11 = (bf16[8,16,256]{2,1,0:T(8,128)(2,1)S(1)}, bf16[8,16,256]{2,1,0:T(8,128)(2,1)}, u32[]{:S(2)}) copy-start(bf16[8,16,256]{2,1,0:T(8,128)(2,1)} %param.19) | copy-start | bytes 196612
  0.0 15.2 %copy-start.4 = (s32[6,64]{1,0:T(8,128)S(1)}, s32[6,64]{1,0:T(8,128)}, u32[]{:S(2)}) copy-start(s32[6,64]{1,0:T(8,128)} %pairs_ref.1) | copy-start | bytes 4612
  0.0 15.2 %copy-start.5 = (s32[6]{0:T(128)S(1)}, s32[6]{0:T(128)}, u32[]{:S(2)}) copy-start(s32[6]{0:T(128)} %first_ref.1) | copy-start | bytes 76
  0.0 15.2 %copy-start.6 = (bf16[256]{0:T(256)(128)(2,1)S(1)}, bf16[256]{0:T(256)(128)(2,1)}, u32[]{:S(2)}) copy-start(bf16[256]{0:T(256)(128)(2,1)} %gap_ref.1) | copy-start | bytes 1540
  0.0 15.2 %collective-permute-start.3 = (bf16[64,16,256]{2,1,0:T(8,128)(2,1)}, bf16[64,16,256]{2,1,0:T(8,128)(2,1)S(1)}, u32[]{:S(2)}, u32[]{:S(2)}) collective-permute-start(bf16[64,16,256]{2,1,0:T(8,128)(2,1)} %refs_0_.2), channel_id=1, source_target_pairs={{0,16},{16,0},{1,17},{17,1},{2,18},{18,2},{3,19},{19,3},{4,20},{20... | collective-permute-start | bytes 1572872 | tf_op jit(solution)/shard_map/ppermute | solution.py:349
  3.0 15.3 %collective-permute-start = (bf16[1,8,16,256]{3,2,1,0:T(8,128)(2,1)}, bf16[1,8,16,256]{3,2,1,0:T(8,128)(2,1)S(1)}, u32[]{:S(2)}, u32[]{:S(2)}) collective-permute-start(bf16[1,8,16,256]{3,2,1,0:T(8,128)(2,1)} %bitcast.35), channel_id=1, source_target_pairs={{0,8},{1,9},{2,10},{3,11},{4,12},{5,13},{6,14},{7,15},{8,0},{9,1},... | collective-permute-start | bytes 196616 | tf_op jit(solution)/shard_map/ppermute | solution.py:284
  5.6 12.7 %collective-permute-start.1 = (bf16[1,8,16,256]{3,2,1,0:T(8,128)(2,1)}, bf16[1,8,16,256]{3,2,1,0:T(8,128)(2,1)S(1)}, u32[]{:S(2)}, u32[]{:S(2)}) collective-permute-start(bf16[1,8,16,256]{3,2,1,0:T(8,128)(2,1)} %bitcast.36), channel_id=1, source_target_pairs={{0,4},{1,5},{2,6},{3,7},{4,0},{5,1},{6,2},{7,3},{8,12},{9,13},{10,... | collective-permute-start | bytes 196616 | tf_op jit(solution)/shard_map/ppermute | solution.py:284
  7.2 11.1 %collective-permute-start.2 = (bf16[1,8,16,256]{3,2,1,0:T(8,128)(2,1)}, bf16[1,8,16,256]{3,2,1,0:T(8,128)(2,1)S(1)}, u32[]{:S(2)}, u32[]{:S(2)}) collective-permute-start(bf16[1,8,16,256]{3,2,1,0:T(8,128)(2,1)} %bitcast.37), channel_id=1, source_target_pairs={{0,12},{1,13},{2,14},{3,15},{4,8},{5,9},{6,10},{7,11},{8,4},{9,5},... | collective-permute-start | bytes 196616 | tf_op jit(solution)/shard_map/ppermute | solution.py:284
  8.8 27.3 %copy-start.3 = (bf16[256,256]{1,0:T(8,128)(2,1)S(1)}, bf16[256,256]{1,0:T(8,128)(2,1)}, u32[]{:S(2)}) copy-start(bf16[256,256]{1,0:T(8,128)(2,1)} %out_weight_ref.1) | copy-start | bytes 393220
  8.8 27.3 %copy-start.7 = (bf16[256]{0:T(256)(128)(2,1)S(1)}, bf16[256]{0:T(256)(128)(2,1)}, u32[]{:S(2)}) copy-start(bf16[256]{0:T(256)(128)(2,1)} %refs_0_.3) | copy-start | bytes 1540
  8.8 27.3 %copy-start.8 = (bf16[256]{0:T(256)(128)(2,1)S(1)}, bf16[256]{0:T(256)(128)(2,1)}, u32[]{:S(2)}) copy-start(bf16[256]{0:T(256)(128)(2,1)} %refs_1_.1) | copy-start | bytes 1540
  8.8 27.3 %copy-start.9 = (bf16[256]{0:T(256)(128)(2,1)S(1)}, bf16[256]{0:T(256)(128)(2,1)}, u32[]{:S(2)}) copy-start(bf16[256]{0:T(256)(128)(2,1)} %refs_2_.1) | copy-start | bytes 1540
  8.9 27.3 %copy-start.10 = (bf16[256]{0:T(256)(128)(2,1)S(1)}, bf16[256]{0:T(256)(128)(2,1)}, u32[]{:S(2)}) copy-start(bf16[256]{0:T(256)(128)(2,1)} %refs_3_.1) | copy-start | bytes 1540
  16.4 2.7 %copy-start = (bf16[2,2,4,16,256]{4,3,2,1,0:T(8,128)(2,1)}, bf16[2,2,4,16,256]{4,3,2,1,0:T(8,128)(2,1)S(1)}, u32[]{:S(2)}) copy-start(bf16[2,2,4,16,256]{4,3,2,1,0:T(8,128)(2,1)S(1)} %get-tuple-element.19.refs_1_.refs_6_) | copy-start | bytes 393220
  16.4 9.6 %collective-permute-start.10 = (bf16[2,2,4,16,256]{4,3,2,1,0:T(8,128)(2,1)S(1)}, bf16[2,2,4,16,256]{4,3,2,1,0:T(8,128)(2,1)S(1)}, u32[]{:S(2)}, u32[]{:S(2)}) collective-permute-start(bf16[2,2,4,16,256]{4,3,2,1,0:T(8,128)(2,1)S(1)} %get-tuple-element.26), channel_id=1, source_target_pairs={{0,4},{1,5},{2,6},{3,7},{4,0},{5,1},{6,2},{7,3},{8,12},{9,13},{10,... | collective-permute-start | bytes 393224 | tf_op jit(solution)/shard_map/ppermute | solution.py:284
  19.1 18.5 %copy-start.1 = (bf16[2,2,4,16,256]{4,3,2,1,0:T(8,128)(2,1)S(1)}, bf16[2,2,4,16,256]{4,3,2,1,0:T(8,128)(2,1)}, u32[]{:S(2)}) copy-start(bf16[2,2,4,16,256]{4,3,2,1,0:T(8,128)(2,1)} %copy-done) | copy-start | bytes 393220
  19.1 14.1 %collective-permute-start.4 = (bf16[4,8,16,256]{3,2,1,0:T(8,128)(2,1)}, bf16[4,8,16,256]{3,2,1,0:T(8,128)(2,1)S(1)}, u32[]{:S(2)}, u32[]{:S(2)}) collective-permute-start(bf16[4,8,16,256]{3,2,1,0:T(8,128)(2,1)} %same_cells.1), channel_id=1, source_target_pairs={{0,2},{1,3},{2,0},{3,1},{4,6},{5,7},{6,4},{7,5},{8,10},{9,11},{10,... | collective-permute-start | bytes 786440 | tf_op jit(solution)/shard_map/ppermute | solution.py:284
  20.7 8.3 %collective-permute-start.6 = (bf16[2,4,16,256]{3,2,1,0:T(8,128)(2,1)S(1)}, bf16[2,4,16,256]{3,2,1,0:T(8,128)(2,1)S(1)}, u32[]{:S(2)}, u32[]{:S(2)}) collective-permute-start(bf16[2,4,16,256]{3,2,1,0:T(8,128)(2,1)S(1)} %get-tuple-element.22), channel_id=1, source_target_pairs={{0,8},{1,9},{2,10},{3,11},{4,12},{5,13},{6,14},{7,15},{8,0},{9,1},... | collective-permute-start | bytes 196616 | tf_op jit(solution)/shard_map/ppermute | solution.py:284
  23.3 8.9 %collective-permute-start.7 = (bf16[2,4,16,256]{3,2,1,0:T(8,128)(2,1)S(1)}, bf16[2,4,16,256]{3,2,1,0:T(8,128)(2,1)S(1)}, u32[]{:S(2)}, u32[]{:S(2)}) collective-permute-start(bf16[2,4,16,256]{3,2,1,0:T(8,128)(2,1)S(1)} %get-tuple-element.23), channel_id=1, source_target_pairs={{0,10},{1,11},{2,8},{3,9},{4,14},{5,15},{6,12},{7,13},{8,2},{9,3},... | collective-permute-start | bytes 196616 | tf_op jit(solution)/shard_map/ppermute | solution.py:284
  23.5 8.6 %collective-permute-start.8 = (bf16[2,4,16,256]{3,2,1,0:T(8,128)(2,1)S(1)}, bf16[2,4,16,256]{3,2,1,0:T(8,128)(2,1)S(1)}, u32[]{:S(2)}, u32[]{:S(2)}) collective-permute-start(bf16[2,4,16,256]{3,2,1,0:T(8,128)(2,1)S(1)} %get-tuple-element.24), channel_id=1, source_target_pairs={{0,12},{1,13},{2,14},{3,15},{4,8},{5,9},{6,10},{7,11},{8,4},{9,5},... | collective-permute-start | bytes 196616 | tf_op jit(solution)/shard_map/ppermute | solution.py:284
  26.0 7.1 %collective-permute-start.9 = (bf16[2,4,16,256]{3,2,1,0:T(8,128)(2,1)S(1)}, bf16[2,4,16,256]{3,2,1,0:T(8,128)(2,1)S(1)}, u32[]{:S(2)}, u32[]{:S(2)}) collective-permute-start(bf16[2,4,16,256]{3,2,1,0:T(8,128)(2,1)S(1)} %get-tuple-element.25), channel_id=1, source_target_pairs={{0,14},{1,15},{2,12},{3,13},{4,10},{5,11},{6,8},{7,9},{8,6},{9,7},... | collective-permute-start | bytes 196616 | tf_op jit(solution)/shard_map/ppermute | solution.py:284
  29.0 5.5 %collective-permute-start.11 = (bf16[2,2,4,16,256]{4,3,2,1,0:T(8,128)(2,1)S(1)}, bf16[2,2,4,16,256]{4,3,2,1,0:T(8,128)(2,1)S(1)}, u32[]{:S(2)}, u32[]{:S(2)}) collective-permute-start(bf16[2,2,4,16,256]{4,3,2,1,0:T(8,128)(2,1)S(1)} %pad_maximum_fusion.2), channel_id=1, source_target_pairs={{0,2},{1,3},{2,0},{3,1},{4,6},{5,7},{6,4},{7,5},{8,10},{9,11},{10,... | collective-permute-start | bytes 393224 | tf_op jit(solution)/shard_map/ppermute | solution.py:284
  34.2 2.0 %collective-permute-start.5 = (bf16[8,8,16,256]{3,2,1,0:T(8,128)(2,1)S(1)}, bf16[8,8,16,256]{3,2,1,0:T(8,128)(2,1)S(1)}, u32[]{:S(2)}, u32[]{:S(2)}) collective-permute-start(bf16[8,8,16,256]{3,2,1,0:T(8,128)(2,1)S(1)} %pad_maximum_fusion.near_ref), channel_id=1, source_target_pairs={{0,1},{1,0},{2,3},{3,2},{4,5},{5,4},{6,7},{7,6},{8,9},{9,8},{10,11... | collective-permute-start | bytes 1572872 | tf_op jit(solution)/shard_map/ppermute | solution.py:284
  35.3 2.3 %collective-permute-start.12 = (bf16[8,4,16,256]{3,2,1,0:T(8,128)(2,1)S(1)}, bf16[8,4,16,256]{3,2,1,0:T(8,128)(2,1)S(1)}, u32[]{:S(2)}, u32[]{:S(2)}) collective-permute-start(bf16[8,4,16,256]{3,2,1,0:T(8,128)(2,1)S(1)} %constant_dynamic-update-slice_fusion), channel_id=1, source_target_pairs={{0,1},{1,0},{2,3},{3,2},{4,5},{5,4},{6,7},{7,6},{8,9},{9,8},{10,11... | collective-permute-start | bytes 786440 | tf_op jit(solution)/shard_map/ppermute | solution.py:284
  42.1 9.8 %collective-permute-start.17 = (bf16[2,2,4,16,256]{4,3,2,1,0:T(8,128)(2,1)S(1)}, bf16[2,2,4,16,256]{4,3,2,1,0:T(8,128)(2,1)S(1)}, u32[]{:S(2)}, u32[]{:S(2)}) collective-permute-start(bf16[2,2,4,16,256]{4,3,2,1,0:T(8,128)(2,1)S(1)} %get-tuple-element.31), channel_id=1, source_target_pairs={{0,4},{1,5},{2,6},{3,7},{4,0},{5,1},{6,2},{7,3},{8,12},{9,13},{10,... | collective-permute-start | bytes 393224 | tf_op jit(solution)/shard_map/ppermute | solution.py:284
  44.3 10.8 %collective-permute-start.13 = (bf16[2,4,16,256]{3,2,1,0:T(8,128)(2,1)S(1)}, bf16[2,4,16,256]{3,2,1,0:T(8,128)(2,1)S(1)}, u32[]{:S(2)}, u32[]{:S(2)}) collective-permute-start(bf16[2,4,16,256]{3,2,1,0:T(8,128)(2,1)S(1)} %get-tuple-element.27), channel_id=1, source_target_pairs={{0,8},{1,9},{2,10},{3,11},{4,12},{5,13},{6,14},{7,15},{8,0},{9,1},... | collective-permute-start | bytes 196616 | tf_op jit(solution)/shard_map/ppermute | solution.py:284
  45.0 12.9 %collective-permute-start.14 = (bf16[2,4,16,256]{3,2,1,0:T(8,128)(2,1)S(1)}, bf16[2,4,16,256]{3,2,1,0:T(8,128)(2,1)S(1)}, u32[]{:S(2)}, u32[]{:S(2)}) collective-permute-start(bf16[2,4,16,256]{3,2,1,0:T(8,128)(2,1)S(1)} %get-tuple-element.28), channel_id=1, source_target_pairs={{0,10},{1,11},{2,8},{3,9},{4,14},{5,15},{6,12},{7,13},{8,2},{9,3},... | collective-permute-start | bytes 196616 | tf_op jit(solution)/shard_map/ppermute | solution.py:284
  48.0 10.0 %collective-permute-start.15 = (bf16[2,4,16,256]{3,2,1,0:T(8,128)(2,1)S(1)}, bf16[2,4,16,256]{3,2,1,0:T(8,128)(2,1)S(1)}, u32[]{:S(2)}, u32[]{:S(2)}) collective-permute-start(bf16[2,4,16,256]{3,2,1,0:T(8,128)(2,1)S(1)} %get-tuple-element.29), channel_id=1, source_target_pairs={{0,12},{1,13},{2,14},{3,15},{4,8},{5,9},{6,10},{7,11},{8,4},{9,5},... | collective-permute-start | bytes 196616 | tf_op jit(solution)/shard_map/ppermute | solution.py:284
  49.8 8.2 %collective-permute-start.16 = (bf16[2,4,16,256]{3,2,1,0:T(8,128)(2,1)S(1)}, bf16[2,4,16,256]{3,2,1,0:T(8,128)(2,1)S(1)}, u32[]{:S(2)}, u32[]{:S(2)}) collective-permute-start(bf16[2,4,16,256]{3,2,1,0:T(8,128)(2,1)S(1)} %get-tuple-element.30), channel_id=1, source_target_pairs={{0,14},{1,15},{2,12},{3,13},{4,10},{5,11},{6,8},{7,9},{8,6},{9,7},... | collective-permute-start | bytes 196616 | tf_op jit(solution)/shard_map/ppermute | solution.py:284
  52.0 6.4 %collective-permute-start.18 = (bf16[2,2,4,16,256]{4,3,2,1,0:T(8,128)(2,1)S(1)}, bf16[2,2,4,16,256]{4,3,2,1,0:T(8,128)(2,1)S(1)}, u32[]{:S(2)}, u32[]{:S(2)}) collective-permute-start(bf16[2,2,4,16,256]{4,3,2,1,0:T(8,128)(2,1)S(1)} %pad_maximum_fusion.3), channel_id=1, source_target_pairs={{0,2},{1,3},{2,0},{3,1},{4,6},{5,7},{6,4},{7,5},{8,10},{9,11},{10,... | collective-permute-start | bytes 393224 | tf_op jit(solution)/shard_map/ppermute | solution.py:284
  58.5 1.6 %collective-permute-start.19 = (bf16[8,4,16,256]{3,2,1,0:T(8,128)(2,1)S(1)}, bf16[8,4,16,256]{3,2,1,0:T(8,128)(2,1)S(1)}, u32[]{:S(2)}, u32[]{:S(2)}) collective-permute-start(bf16[8,4,16,256]{3,2,1,0:T(8,128)(2,1)S(1)} %constant_dynamic-update-slice_fusion.8), channel_id=1, source_target_pairs={{0,1},{1,0},{2,3},{3,2},{4,5},{5,4},{6,7},{7,6},{8,9},{9,8},{10,11... | collective-permute-start | bytes 786440 | tf_op jit(solution)/shard_map/ppermute | solution.py:284
